TPU v7x, 256 devices: a whole 4x4x8 slice. The times are simulated.
256 devices in a mesh: ens: 4 (over x_lo, core), grid: 64 (over z, y, x_hi).
Axes of the slice: x: 4 (x_hi: 2, x_lo: 2; x = x_hi * 2 + x_lo), y: 4, z: 8, core: 2. Of those that a mesh axis runs over, the one named last changes fastest.
Arguments:
- latent: bfloat16 [8, 16384, 1024], P('ens', 'grid'), may hold values from -6 to 6
- edge_src: int32 [16384, 3], P('grid'), may hold values from 0 to 16383, as said below
- counts: int32 [64], replicated, may hold values from 128 to 256, as said below
- targets: float32 [100, 16384], P(None, 'grid'), may hold values from -4 to 4
- area: float32 [16384], P('grid'), may hold values from 0.3 to 3
- var_weight: float32 [100], replicated, may hold values from 0.1 to 1
- w_in: bfloat16 [1024, 1024], replicated, may hold values from -0.1875 to 0.1875
- b_in: float32 [1024], replicated, may hold values from -3 to 3
- w_out: bfloat16 [1024, 100], replicated, may hold values from -0.1875 to 0.1875
- b_out: float32 [100], replicated, may hold values from -3 to 3
Outputs:
- grad_latent: bfloat16 [8, 16384, 1024], P('ens', 'grid')
- grad_w_in: float32 [1024, 1024], replicated
- grad_b_in: float32 [1024], replicated
- grad_w_out: float32 [1024, 100], replicated
- grad_b_out: float32 [100], replicated
- loss: float32 [], replicated
Inputs may be any that keep to these rules, and one draw needn't show every extreme that they name: `edge_src`: every edge of a grid point in tile s (rows s * 256 to (s + 1) * 256 - 1) names a latent node of tile s - 1, s or s + 1 taken cyclically over 64 tiles, latent tile t holding nodes t * 256 to (t + 1) * 256 - 1. The valid points of tile s are its first counts[s].
All inputs are finite; a program needn't handle non-finite values.
Results may differ from a plain program's by a relative error of at most 0.0079.
Values may be sent and summed in bfloat16 or wider, within the bound.
No kernel may reach another device: no remote copies, remote signals or barrier semaphores. Data moves between devices by JAX's collectives and lax.ppermute only.
A program may use at most 128 MiB of HBM per device.

v0:
```python
import jax
import jax.numpy as jnp
from jax import lax
from jax.sharding import PartitionSpec as P

smooth_sq = 0.0025
smooth_width = 0.05


def padded(block, sides, width):
    for axis, dim in sides:
        count = lax.axis_size(axis)
        forward = [(i, i + 1) for i in range(count - 1)]
        forward.append((count - 1, 0))
        backward = [(target, source) for source, target in forward]
        low = lax.ppermute(
            lax.slice_in_dim(block, block.shape[dim] - width, None, axis=dim), axis, forward
        )
        high = lax.ppermute(lax.slice_in_dim(block, 0, width, axis=dim), axis, backward)
        block = jnp.concatenate([low, block, high], axis=dim)
    return block


def passed_along(value, axis, by):
    count = lax.axis_size(axis)
    return lax.ppermute(value, axis, [(i, (i + by) % count) for i in range(count)])


def smooth(d):
    return jnp.sqrt(d * d + smooth_sq) - smooth_width


def smooth_slope(d):
    return d / jnp.sqrt(d * d + smooth_sq)


def gelu_value(v):
    return 0.5 * v * (1.0 + lax.erf(v * 0.7071067811865476))


def gelu_slope(v):
    return (
        0.5 * (1.0 + lax.erf(v * 0.7071067811865476))
        + v * jnp.exp(-0.5 * v * v) * 0.3989422804014327
    )


def body(latent, edge_src, counts, targets, area, var_weight, w_in, b_in, w_out, b_out):
    mem_here, l_tile, width = latent.shape
    g_tile = edge_src.shape[0]
    ens_count = lax.axis_size("ens")
    members = mem_here * ens_count
    latent_all = l_tile * lax.axis_size("grid")
    tile = lax.axis_index("grid")
    extended = padded(latent, (("grid", 1),), l_tile)
    local = jnp.mod(edge_src - (tile - 1) * l_tile, latent_all)
    acc = jnp.zeros((mem_here, g_tile, width), jnp.float32)
    for k in range(edge_src.shape[1]):
        acc = acc + extended[:, local[:, k]].astype(jnp.float32)
    features = (acc / edge_src.shape[1]).astype(jnp.bfloat16)
    pre = jnp.einsum("mgh,hk->mgk", features, w_in, preferred_element_type=jnp.float32) + b_in
    hidden = gelu_value(pre).astype(jnp.bfloat16)
    pred = (
        jnp.einsum("mgh,hv->mvg", hidden, w_out, preferred_element_type=jnp.float32)
        + b_out[None, :, None]
    )
    valid = (jnp.arange(g_tile, dtype=jnp.int32) < counts[tile]).astype(jnp.float32)
    wgt = var_weight[:, None] * (area * valid)[None, :]
    empty = jnp.zeros_like(pred)
    piece = lax.all_gather(pred, "ens", axis=0, tiled=True)
    dsum = empty
    ssum = empty
    for j in range(piece.shape[0]):
        diff = pred - piece[j][None]
        dsum = dsum + smooth_slope(diff)
        ssum = ssum + smooth(diff)
    dsum, ssum = (dsum, ssum)
    err = pred - targets[None]
    mm = float(members)
    total = jnp.sum(wgt[None] * (smooth(err) / mm - ssum / (2.0 * mm * (mm - 1.0))))
    grad_pred = wgt[None] * (smooth_slope(err) / mm - dsum / (mm * (mm - 1.0)))
    gb_out = jnp.sum(grad_pred, axis=(0, 2))
    dpred = grad_pred.astype(jnp.bfloat16)
    gw_out = jnp.einsum("mgh,mvg->hv", hidden, dpred, preferred_element_type=jnp.float32)
    dhid = jnp.einsum("mvg,hv->mgh", dpred, w_out, preferred_element_type=jnp.float32)
    dpre = (dhid * gelu_slope(pre)).astype(jnp.bfloat16)
    gb_in = jnp.sum(dpre.astype(jnp.float32), axis=(0, 1))
    gw_in = jnp.einsum("mgh,mgk->hk", features, dpre, preferred_element_type=jnp.float32)
    gw_in, gb_in, gw_out, gb_out, total = lax.psum(
        (gw_in, gb_in, gw_out, gb_out, total), ("ens", "grid")
    )
    dfeat = (
        jnp.einsum("mgk,hk->mgh", dpre, w_in, preferred_element_type=jnp.float32)
        / edge_src.shape[1]
    )
    grad_ext = jnp.zeros((mem_here, 3 * l_tile, width), jnp.float32)
    for k in range(edge_src.shape[1]):
        grad_ext = grad_ext.at[:, local[:, k]].add(dfeat)
    from_above = passed_along(grad_ext[:, :l_tile], "grid", -1)
    from_below = passed_along(grad_ext[:, 2 * l_tile :], "grid", 1)
    grad_latent = (grad_ext[:, l_tile : 2 * l_tile] + from_above + from_below).astype(jnp.bfloat16)
    return (grad_latent, gw_in, gb_in, gw_out, gb_out, total)


def solution(mesh):
    in_specs = (
        P("ens", "grid", None),
        P("grid", None),
        P(),
        P(None, "grid"),
        P("grid"),
        P(),
        P(),
        P(),
        P(),
        P(),
    )
    out_specs = (P("ens", "grid", None), P(), P(), P(), P(), P())
    return jax.shard_map(body, mesh=mesh, in_specs=in_specs, out_specs=out_specs, check_vma=False)
```

profile of v0, /device:TPU:1, one launch (start us, length us, event | category | flops | bytes accessed | tf_op | source)
XLA Modules:
  0.0 569.7 jit_solution(5030305357771316821)
XLA Ops:
  7.3 3.4 copy.39
  10.7 11.3 %collective-permute-start.1 = (bf16[2,256,1024]{2,0,1:T(2,128)(2,1)}, bf16[2,256,1024]{2,0,1:T(2,128)(2,1)}, u32[]{:S(2)}, u32[]{:S(2)}) collective-permute-start(bf16[2,256,1024]{2,0,1:T(2,128)(2,1)} %copy.39), channel_id=1, source_target_pairs={{1,0},{2,1},{3,2},{4,3},{5,4},{6,5},{7,6},{8,7},{9,8},{10,9},{11,1... | collective-permute-start | bytes 3145736 | tf_op jit(solution)/shard_map/ppermute | solution.py:19
  23.4 39.9 %collective-permute-done = bf16[2,256,1024]{2,0,1:T(2,128)(2,1)} collective-permute-done((bf16[2,256,1024]{2,0,1:T(2,128)(2,1)}, bf16[2,256,1024]{2,0,1:T(2,128)(2,1)}, u32[]{:S(2)}, u32[]{:S(2)}) %collective-permute-start) | collective-permute-done | bytes 1048608 | tf_op jit(solution)/shard_map/ppermute | solution.py:16
  63.3 2.9 constant_dynamic-update-slice_fusion.2
  66.2 2.0 constant_dynamic-update-slice_fusion.1
  68.3 2.9 constant_dynamic-update-slice_fusion
  71.2 4.6 gather_fusion.2
  75.8 5.6 gather_fusion.1
  81.4 5.6 gather_fusion
  87.0 4.0 multiply_convert_fusion.1
  91.5 9.3 %all_gather.3 = f32[8,100,256]{2,1,0:T(8,128)S(1)} all-gather(f32[2,100,256]{2,1,0:T(8,128)S(1)} %fusion.14), channel_id=1, replica_groups=mesh['ens'=4,'grid'=64] {'ens'}, dimensions={0}, use_global_device_ids=true | all-gather | bytes 1024000 | tf_op jit(solution)/shard_map/all_gather | solution.py:70
  100.9 1.9 fusion.23
  107.4 2.9 copy.45
  110.3 4.3 broadcast_in_dim.2
  114.6 35.5 %scatter_fusion = f32[2,768,1024]{2,0,1:T(2,128)} fusion(f32[2,768,1024]{2,0,1:T(2,128)} %broadcast_in_dim.2, s32[256]{0:T(256)S(1)} %bitcast.61, f32[256,2,1024]{2,1,0:T(2,128)} %copy.45), kind=kCustom, calls=%fused_computation.3 | custom fusion | flops 524288 | bytes 6292480 | tf_op jit(solution)/shard_map/scatter-add | solution.py:98
  150.2 35.6 %scatter_fusion.1 = f32[2,768,1024]{2,0,1:T(2,128)} fusion(f32[2,768,1024]{2,0,1:T(2,128)} %scatter_fusion, s32[256]{0:T(256)S(1)} %bitcast.59, f32[256,2,1024]{2,1,0:T(2,128)} %copy.45), kind=kCustom, calls=%fused_computation.4 | custom fusion | flops 524288 | bytes 6292480 | tf_op jit(solution)/shard_map/scatter-add | solution.py:98
  185.7 35.6 %scatter_fusion.2 = f32[2,768,1024]{2,0,1:T(2,128)} fusion(f32[2,768,1024]{2,0,1:T(2,128)} %scatter_fusion.1, s32[256]{0:T(256)S(1)} %bitcast.57, f32[256,2,1024]{2,1,0:T(2,128)} %copy.45), kind=kCustom, calls=%fused_computation.5 | custom fusion | flops 524288 | bytes 6292480 | tf_op jit(solution)/shard_map/scatter-add | solution.py:98
  221.3 5.8 %fusion.24 = (f32[2,256,1024]{2,0,1:T(2,128)}, f32[2,256,1024]{2,0,1:T(2,128)}) fusion(f32[2,768,1024]{2,0,1:T(2,128)} %scatter_fusion.2), kind=kLoop, calls=%fused_computation.69 | loop fusion | bytes 8388608 | tf_op jit(solution)/shard_map/slice | solution.py:99
  227.1 8.3 %collective-permute-start.2 = (f32[2,256,1024]{2,0,1:T(2,128)}, f32[2,256,1024]{2,0,1:T(2,128)}, u32[]{:S(2)}, u32[]{:S(2)}) collective-permute-start(f32[2,256,1024]{2,0,1:T(2,128)} %get-tuple-element.37), channel_id=1, source_target_pairs={{0,63},{1,0},{2,1},{3,2},{4,3},{5,4},{6,5},{7,6},{8,7},{9,8},{10,9... | collective-permute-start | bytes 6291464 | tf_op jit(solution)/shard_map/ppermute | solution.py:26
  235.3 4.6 convolution_bitcast_fusion
  239.9 155.6 %all-reduce = (f32[1024]{0:T(1024)}, f32[100]{0:T(128)}, f32[]{:T(128)}) all-reduce(f32[1024]{0:T(1024)S(1)} %get-tuple-element.53, f32[100]{0:T(128)S(1)} %get-tuple-element.35, f32[]{:T(128)} %get-tuple-element.39), channel_id=1, replica_groups=mesh['ens'=4,'grid'=64] {'ens','grid'}, use_global_device_ids=true, to_apply=%region_5.6 | all-reduce | flops 1125 | bytes 9000 | tf_op jit(solution)/shard_map/psum | solution.py:89
  395.6 3.6 fusion.7
  400.5 156.8 %all-reduce.4.cloned.1.call-done = (f32[1024,1024]{1,0:T(8,128)}, f32[1024,100]{0,1:T(8,128)}) async-done(((f32[1024,1024]{1,0:T(8,128)}, f32[1024,100]{0,1:T(8,128)}), (f32[1024,1024]{1,0:T(8,128)}, f32[1024,100]{0,1:T(8,128)})) %all-reduce.4.cloned.1.call-update) | async-done | bytes 4603920 | tf_op jit(solution)/shard_map/psum | solution.py:89
  557.2 4.8 copy.74
  (51 shorter events, 8.6 us)
Async XLA Ops:
  7.2 79.8 %copy-start = (bf16[1024,1024]{1,0:T(8,128)(2,1)S(1)}, bf16[1024,1024]{1,0:T(8,128)(2,1)}, u32[]{:S(2)}) copy-start(bf16[1024,1024]{1,0:T(8,128)(2,1)} %param.16) | copy-start | bytes 6291460
  7.2 59.0 %copy-start.1 = (bf16[2,256,1024]{2,1,0:T(8,128)(2,1)S(1)}, bf16[2,256,1024]{2,1,0:T(8,128)(2,1)}, u32[]{:S(2)}) copy-start(bf16[2,256,1024]{2,1,0:T(8,128)(2,1)} %param.10) | copy-start | bytes 3145732
  7.2 14.8 %copy-start.7 = (s32[256,3]{0,1:T(4,128)S(1)}, s32[256,3]{0,1:T(4,128)}, u32[]{:S(2)}) copy-start(s32[256,3]{0,1:T(4,128)} %param.11) | copy-start | bytes 9220
  7.2 14.9 %copy-start.12 = (s32[64]{0:T(128)S(1)}, s32[64]{0:T(128)}, u32[]{:S(2)}) copy-start(s32[64]{0:T(128)} %param.12) | copy-start | bytes 772
  7.2 15.5 %copy-start.8 = (f32[256]{0:T(256)S(1)}, f32[256]{0:T(256)}, u32[]{:S(2)}) copy-start(f32[256]{0:T(256)} %param.14) | copy-start | bytes 3076
  7.2 16.1 %copy-start.9 = (f32[100]{0:T(128)S(1)}, f32[100]{0:T(128)}, u32[]{:S(2)}) copy-start(f32[100]{0:T(128)} %param.15) | copy-start | bytes 1204
  7.2 550.0 %all-reduce.4.cloned.1.call-start = ((), (), s32[]{:S(2)}) async-start(), calls=%async_computation | async-start | bytes 9240576 | tf_op jit(solution)/shard_map/psum | solution.py:89
  10.7 57.6 %collective-permute-start.1 = (bf16[2,256,1024]{2,0,1:T(2,128)(2,1)}, bf16[2,256,1024]{2,0,1:T(2,128)(2,1)}, u32[]{:S(2)}, u32[]{:S(2)}) collective-permute-start(bf16[2,256,1024]{2,0,1:T(2,128)(2,1)} %copy.39), channel_id=1, source_target_pairs={{1,0},{2,1},{3,2},{4,3},{5,4},{6,5},{7,6},{8,7},{9,8},{10,9},{11,1... | collective-permute-start | bytes 3145736 | tf_op jit(solution)/shard_map/ppermute | solution.py:19
  22.0 41.3 %collective-permute-start = (bf16[2,256,1024]{2,0,1:T(2,128)(2,1)}, bf16[2,256,1024]{2,0,1:T(2,128)(2,1)}, u32[]{:S(2)}, u32[]{:S(2)}) collective-permute-start(bf16[2,256,1024]{2,0,1:T(2,128)(2,1)} %copy.39), channel_id=1, source_target_pairs={{0,1},{1,2},{2,3},{3,4},{4,5},{5,6},{6,7},{7,8},{8,9},{9,10},{10,1... | collective-permute-start | bytes 3145736 | tf_op jit(solution)/shard_map/ppermute | solution.py:16
  75.8 11.1 %copy-start.11 = (f32[1024]{0:T(1024)S(1)}, f32[1024]{0:T(1024)}, u32[]{:S(2)}) copy-start(f32[1024]{0:T(1024)} %param.17) | copy-start | bytes 12292
  87.0 4.0 copy-start.5
  87.0 4.0 copy-start.10
  91.0 9.8 %copy-start.6 = (f32[100,256]{1,0:T(8,128)S(1)}, f32[100,256]{1,0:T(8,128)}, u32[]{:S(2)}) copy-start(f32[100,256]{1,0:T(8,128)} %param.13) | copy-start | bytes 307204
  105.1 1.0 copy-start.13
  221.3 14.1 %copy-start.2 = (bf16[256,2,1024]{2,1,0:T(2,128)(2,1)S(1)}, bf16[256,2,1024]{2,1,0:T(2,128)(2,1)}, u32[]{:S(2)}) copy-start(bf16[256,2,1024]{2,1,0:T(2,128)(2,1)} %gather_fusion.1) | copy-start | bytes 3145732
  221.3 14.1 %copy-start.3 = (bf16[256,2,1024]{2,1,0:T(2,128)(2,1)S(1)}, bf16[256,2,1024]{2,1,0:T(2,128)(2,1)}, u32[]{:S(2)}) copy-start(bf16[256,2,1024]{2,1,0:T(2,128)(2,1)} %gather_fusion) | copy-start | bytes 3145732
  221.3 14.1 %copy-start.14 = (bf16[2,256,1024]{2,1,0:T(8,128)(2,1)S(1)}, bf16[2,256,1024]{2,1,0:T(8,128)(2,1)}, u32[]{:S(2)}) copy-start(bf16[2,256,1024]{2,1,0:T(8,128)(2,1)} %copy-done.13) | copy-start | bytes 3145732
  227.1 168.5 %collective-permute-start.2 = (f32[2,256,1024]{2,0,1:T(2,128)}, f32[2,256,1024]{2,0,1:T(2,128)}, u32[]{:S(2)}, u32[]{:S(2)}) collective-permute-start(f32[2,256,1024]{2,0,1:T(2,128)} %get-tuple-element.37), channel_id=1, source_target_pairs={{0,63},{1,0},{2,1},{3,2},{4,3},{5,4},{6,5},{7,6},{8,7},{9,8},{10,9... | collective-permute-start | bytes 6291464 | tf_op jit(solution)/shard_map/ppermute | solution.py:26
  235.3 160.2 %collective-permute-start.3 = (f32[2,256,1024]{2,0,1:T(2,128)}, f32[2,256,1024]{2,0,1:T(2,128)}, u32[]{:S(2)}, u32[]{:S(2)}) collective-permute-start(f32[2,256,1024]{2,0,1:T(2,128)} %get-tuple-element.38), channel_id=1, source_target_pairs={{0,1},{1,2},{2,3},{3,4},{4,5},{5,6},{6,7},{7,8},{8,9},{9,10},{10,1... | collective-permute-start | bytes 6291464 | tf_op jit(solution)/shard_map/ppermute | solution.py:26
  557.2 4.8 copy-start.4
Sparse Core Ops, SparseCore 0:
  240.1 317.1 all-reduce.3
where the time goes:
time: 572 us; the launch traced here: 570 us
  waiting for transfers between devices  197 us (34%)
  blocking collectives  165 us (29%)
  other arithmetic  113 us (20%)
  local copies, waits for them, and re-layouts  48.6 us (8%)
  starting transfers between devices  19.6 us (3%)
  between operations  14.3 us (2%)
  matrix products  12.7 us (2%)
    psum x1, waiting for transfers between devices, body(): lax.psum((gw_in, gb_in, gw_out, gb_out, total), ('ens', 'grid'))  157 us
    psum x1, blocking collectives, body(): lax.psum((gw_in, gb_in, gw_out, gb_out, total), ('ens', 'grid'))  156 us
    scatter-add x3, other arithmetic, body(): grad_ext = grad_ext.at[:, local[:, k]].add(dfeat)  107 us
    ppermute x1, waiting for transfers between devices, padded(): lax.ppermute(lax.slice_in_dim(block, block.shape[dim] - width, None, axis...  39.9 us
    unnamed x36, local copies, waits for them, and re-layouts  16.3 us
    gather x3, local copies, waits for them, and re-layouts, body(): acc = acc + extended[:, local[:, k]].astype(jnp.float32)  15.8 us
  transfers between devices with their start and end apart: 5, of which 2 were waited for; matrix products, arithmetic and copies ran while one was open for 3% of the time, Pallas kernels for 0%

commit v1 on v0

v1 whole, which is shorter than its diff:
```python
import jax
import jax.numpy as jnp
from jax import lax
from jax.sharding import Mesh, PartitionSpec as P

smooth_sq = 0.0025
smooth_width = 0.05
bf16 = jnp.bfloat16
f32 = jnp.float32

ENS = ("xl", "c")
GRID = ("z", "y", "xh")
GROUP = ("xh", "xl", "c")
PLANE = ("y", "xh", "xl")
WIDE = 1152


def gelu_parts(v):
    cdf = 0.5 * (1.0 + lax.erf(v * 0.7071067811865476))
    slope = cdf + v * jnp.exp(-0.5 * v * v) * 0.3989422804014327
    return v * cdf, slope


def ring(shift_odd, shift_even):
    n = 64
    return [(i, (i + (shift_odd if i % 2 else shift_even)) % n) for i in range(n)]


SWAP = ring(-1, 1)
SAME = ring(2, -2)
DIAG = ring(1, -1)


def back(perm):
    return [(b, a) for a, b in perm]


def spread(block, axes):
    n = lax.axis_size(axes)
    many = jnp.broadcast_to(block[None], (n,) + block.shape)
    return lax.all_to_all(many, axes, split_axis=0, concat_axis=0, tiled=True)


def resplit(total):
    col = lax.broadcasted_iota(jnp.int32, total.shape, total.ndim - 1)
    both = total[..., WIDE - 2 : WIDE - 1] + total[..., WIDE - 1 : WIDE]
    high = lax.reduce_precision(both, 8, 7)
    low = both - high
    return jnp.where(
        col == WIDE - 2, high, jnp.where(col == WIDE - 1, low, total)
    ).astype(bf16)


def reduced(grads):
    half = grads.shape[0] // 2
    core = lax.axis_index("c")
    mine = lax.dynamic_slice_in_dim(grads, core * half, half, 0)
    other = lax.dynamic_slice_in_dim(grads, (1 - core) * half, half, 0)
    got = lax.ppermute(resplit(other), "c", [(0, 1), (1, 0)])
    part = resplit(mine + got.astype(f32))
    n = lax.axis_size(PLANE)
    part = lax.all_to_all(
        part.reshape(n, half // n, WIDE), PLANE, split_axis=0, concat_axis=0, tiled=True
    )
    part = resplit(jnp.sum(part.astype(f32), axis=0))
    part = spread(part, "z")
    part = resplit(jnp.sum(part.astype(f32), axis=0))
    part = spread(part, PLANE).reshape(half, WIDE)
    got = lax.ppermute(part, "c", [(0, 1), (1, 0)])
    low = jnp.where(core == 0, part, got)
    high = jnp.where(core == 0, got, part)
    return jnp.concatenate([low, high], axis=0)


def body(latent, edge_src, counts, targets, area, var_weight, w_in, b_in, w_out, b_out):
    l_tile, width = latent.shape[1:]
    g_tile, k_edges = edge_src.shape
    n_vars = w_out.shape[1]
    h = lax.axis_index("xh")
    pair = lax.axis_index(("z", "y"))
    tile = 2 * pair + h
    quarter = lax.axis_index(ENS)
    members = 8
    pts = g_tile // 4

    own = lax.dynamic_index_in_dim(latent, h, 0, keepdims=False)
    oth = lax.dynamic_index_in_dim(latent, 1 - h, 0, keepdims=False)
    edges_there = lax.ppermute(edge_src, GRID, SWAP)
    swapped = lax.ppermute(oth, GRID, SWAP)
    diag = lax.ppermute(oth, GRID, DIAG)
    same = lax.ppermute(own, GRID, SAME)

    edges = jnp.where(
        h == 0,
        jnp.concatenate([edge_src, edges_there], axis=0),
        jnp.concatenate([edges_there, edge_src], axis=0),
    )
    step = edges // l_tile - 2 * pair
    block = jnp.mod(jnp.where(h == 0, step, 1 - step), 4)
    local = block * l_tile + jnp.mod(edges, l_tile)
    nodes = lax.broadcasted_iota(jnp.int32, (2 * g_tile, 4 * l_tile), 1)
    pick = jnp.zeros((2 * g_tile, 4 * l_tile), f32)
    for k in range(k_edges):
        pick = pick + (local[:, k : k + 1] == nodes).astype(f32)
    pick = pick.astype(bf16)

    window = jnp.concatenate([own, swapped, same, diag], axis=0)
    features = (jnp.dot(pick, window, preferred_element_type=f32) / k_edges).astype(bf16)
    pre = jnp.dot(features, w_in, preferred_element_type=f32) + b_in
    hidden, slope = gelu_parts(pre)
    hidden = hidden.astype(bf16)
    pred = jnp.dot(hidden, w_out, preferred_element_type=f32) + b_out

    pred = lax.all_to_all(
        pred.reshape(members, pts, n_vars), GROUP, split_axis=0, concat_axis=0, tiled=True
    )
    start = quarter * pts
    point = start + jnp.arange(pts, dtype=jnp.int32)
    valid = (point < counts[tile]).astype(f32)
    wgt = (lax.dynamic_slice_in_dim(area, start, pts, 0) * valid)[:, None] * var_weight[None, :]
    aim = lax.dynamic_slice_in_dim(targets, start, pts, 1).T
    slopes = [None] * members
    gaps = jnp.zeros((pts, n_vars), f32)
    hits = jnp.zeros((pts, n_vars), f32)
    grads = []
    pair_sum = [jnp.zeros((pts, n_vars), f32) for _ in range(members)]
    for i in range(members):
        for j in range(i + 1, members):
            d = pred[i] - pred[j]
            sq = d * d + smooth_sq
            r = lax.rsqrt(sq)
            gaps = gaps + (sq * r - smooth_width)
            pair_sum[i] = pair_sum[i] + d * r
            pair_sum[j] = pair_sum[j] - d * r
    mm = float(members)
    for i in range(members):
        d = pred[i] - aim
        sq = d * d + smooth_sq
        r = lax.rsqrt(sq)
        hits = hits + (sq * r - smooth_width)
        grads.append(wgt * (d * r / mm - pair_sum[i] / (mm * (mm - 1.0))))
    total = jnp.sum(wgt * (hits / mm - gaps / (mm * (mm - 1.0))))
    grad_pred = jnp.stack(grads)
    gb_out = jnp.sum(grad_pred, axis=(0, 1))
    dpred = lax.all_to_all(
        grad_pred.astype(bf16), GROUP, split_axis=0, concat_axis=0, tiled=True
    ).reshape(members * pts, n_vars)

    dhid = lax.dot_general(dpred, w_out, (((1,), (1,)), ((), ())), preferred_element_type=f32)
    dpre = (dhid * slope).astype(bf16)
    gb_in = jnp.sum(dpre.astype(f32), axis=0)
    gw_out = lax.dot_general(hidden, dpred, (((0,), (0,)), ((), ())), preferred_element_type=f32)
    gw_in = lax.dot_general(features, dpre, (((0,), (0,)), ((), ())), preferred_element_type=f32)
    small = jnp.concatenate([gb_out, total[None], jnp.zeros((width - n_vars - 1,), f32)])
    gap = jnp.zeros((width, WIDE - width - n_vars - 3), f32)
    zero = jnp.zeros((width, 1), f32)
    grads = jnp.concatenate([gw_in, gw_out, gap, gb_in[:, None], small[:, None], zero], axis=1)

    dfeat = lax.dot_general(dpre, w_in, (((1,), (1,)), ((), ())), preferred_element_type=f32)
    dfeat = (dfeat / k_edges).astype(bf16)
    dwin = lax.dot_general(pick, dfeat, (((0,), (0,)), ((), ())), preferred_element_type=f32)
    d_own = dwin[:l_tile]
    sent = dwin[l_tile:].astype(bf16)
    to_swap = lax.ppermute(sent[:l_tile], GRID, back(SWAP))
    to_same = lax.ppermute(sent[l_tile : 2 * l_tile], GRID, back(SAME))
    to_diag = lax.ppermute(sent[2 * l_tile :], GRID, back(DIAG))
    d_own = (d_own + to_same.astype(f32)).astype(bf16)
    d_oth = (to_swap.astype(f32) + to_diag.astype(f32)).astype(bf16)
    grad_latent = jnp.stack([jnp.where(h == 0, d_own, d_oth), jnp.where(h == 0, d_oth, d_own)])

    full = reduced(grads).astype(f32)
    small = full[:, WIDE - 2] + full[:, WIDE - 1]
    return (
        grad_latent,
        full[:, :width],
        full[:, WIDE - 3],
        full[:, width : width + n_vars],
        small[:n_vars],
        small[n_vars],
    )


def solution(mesh):
    fine = Mesh(mesh.devices.reshape(2, 2, 8, 4, 2), ENS + GRID)
    in_specs = (
        P(ENS, GRID, None),
        P(GRID, None),
        P(),
        P(None, GRID),
        P(GRID),
        P(),
        P(),
        P(),
        P(),
        P(),
    )
    out_specs = (P(ENS, GRID, None), P(), P(), P(), P(), P())
    return jax.shard_map(body, mesh=fine, in_specs=in_specs, out_specs=out_specs, check_vma=False)
```

time: 572 us -> 224 us (0.39)
  waiting for transfers between devices: 197 us -> 66.8 us
  blocking collectives: 165 us -> 44.1 us
  other arithmetic: 113 us -> 17 us
  local copies, waits for them, and re-layouts: 48.6 us -> 31.1 us
  starting transfers between devices: 19.6 us -> 36.6 us
  between operations: 14.3 us -> 3.35 us
  matrix products: 12.7 us -> 20.9 us
    psum x1 -> x0, waiting for transfers between devices: 157 us -> none  [body(): lax.psum((gw_in, gb_in, gw_out, gb_out, total), ('ens', 'grid'))]
    psum x1 -> x0, blocking collectives: 156 us -> none  [body(): lax.psum((gw_in, gb_in, gw_out, gb_out, total), ('ens', 'grid'))]
    scatter-add x3 -> x0, other arithmetic: 107 us -> none  [body(): grad_ext = grad_ext.at[:, local[:, k]].add(dfeat)]
    all_to_all x0 -> x2, blocking collectives: none -> 44.1 us  [the longest x1 22.1 us: spread(): return lax.all_to_all(many, axes, split_axis=0, concat_axis=0, tiled=True)]
    all_to_all x0 -> x3, waiting for transfers between devices: none -> 18.9 us  [the longest x1 9.28 us: spread(): return lax.all_to_all(many, axes, split_axis=0, concat_axis=0, tiled=True)]
    gather x3 -> x0, local copies, waits for them, and re-layouts: 15.8 us -> none  [body(): acc = acc + extended[:, local[:, k]].astype(jnp.float32)]
    all_to_all x0 -> x3, starting transfers between devices: none -> 13.5 us  [the longest x1 4.91 us: body(): lax.all_to_all(grad_pred.astype(bf16), GROUP, split_axis=0, concat_axis=0...]
    unnamed x36 -> x35, local copies, waits for them, and re-layouts: 16.3 us -> 5.36 us
  transfers between devices with their start and end apart: 5 -> 12, of which waited for: 2 -> 8; matrix products, arithmetic and copies ran while one was open for 3% -> 7% of each run, Pallas kernels for 0% -> 0%
where the time goes in v1:
time: 224 us; the launch traced here: 220 us
  waiting for transfers between devices  66.8 us (30%)
  blocking collectives  44.1 us (20%)
  starting transfers between devices  36.6 us (16%)
  local copies, waits for them, and re-layouts  31.1 us (14%)
  matrix products  20.9 us (9%)
  other arithmetic  17 us (8%)
  between operations  3.35 us (1%)
    ppermute x1, waiting for transfers between devices, body(): to_diag = lax.ppermute(sent[2 * l_tile:], GRID, back(DIAG))  25 us
    all_to_all x1, blocking collectives, spread(): return lax.all_to_all(many, axes, split_axis=0, concat_axis=0, tiled=True)  22.1 us
    all_to_all x1, blocking collectives, reduced(): lax.all_to_all(part.reshape(n, half // n, WIDE), PLANE, split_axis=0, con...  22 us
    ppermute x1, waiting for transfers between devices, body(): edges_there = lax.ppermute(edge_src, GRID, SWAP)  14.4 us
    concatenate x1, local copies, waits for them, and re-layouts, body(): jnp.concatenate([gw_in, gw_out, gap, gb_in[:, None], small[:, None], zero...  13.8 us
    ppermute x1, starting transfers between devices, body(): diag = lax.ppermute(oth, GRID, DIAG)  11.4 us
    all_to_all x1, waiting for transfers between devices, spread(): return lax.all_to_all(many, axes, split_axis=0, concat_axis=0, tiled=True)  9.28 us
    dot_general x1, matrix products, body(): lax.dot_general(pick, dfeat, (((0,), (0,)), ((), ())), preferred_element_...  6.51 us
  transfers between devices with their start and end apart: 12, of which 8 were waited for; matrix products, arithmetic and copies ran while one was open for 7% of the time, Pallas kernels for 0%

profile of v1, /device:TPU:1, one launch (start us, length us, event | category | flops | bytes accessed | tf_op | source)
XLA Modules:
  0.0 219.7 jit_solution(1465945620415587994)
XLA Ops:
  2.1 11.4 %collective-permute-start.3 = (bf16[256,1024]{1,0:T(8,128)(2,1)S(1)}, bf16[256,1024]{1,0:T(8,128)(2,1)}, u32[]{:S(2)}, u32[]{:S(2)}) collective-permute-start(bf16[256,1024]{1,0:T(8,128)(2,1)S(1)} %get-tuple-element.76), channel_id=1, source_target_pairs={{0,63},{1,2},{2,1},{3,4},{4,3},{5,6},{6,5},{7,8},{8,7},{9,10},{10,... | collective-permute-start | bytes 1572872 | tf_op jit(solution)/shard_map/ppermute | solution.py:90
  14.0 3.0 %collective-permute-start = (s32[256,3]{0,1:T(4,128)S(1)}, s32[256,3]{0,1:T(4,128)S(1)}, u32[]{:S(2)}, u32[]{:S(2)}) collective-permute-start(s32[256,3]{0,1:T(4,128)S(1)} %copy-done.8), channel_id=1, source_target_pairs={{0,1},{1,0},{2,3},{3,2},{4,5},{5,4},{6,7},{7,6},{8,9},{9,8},{10,11... | collective-permute-start | bytes 9224 | tf_op jit(solution)/shard_map/ppermute | solution.py:88
  17.7 14.4 %collective-permute-done = s32[256,3]{0,1:T(4,128)S(1)} collective-permute-done((s32[256,3]{0,1:T(4,128)S(1)}, s32[256,3]{0,1:T(4,128)S(1)}, u32[]{:S(2)}, u32[]{:S(2)}) %collective-permute-start) | collective-permute-done | bytes 3104 | tf_op jit(solution)/shard_map/ppermute | solution.py:88
  32.1 3.2 %collective-permute-done.2 = bf16[256,1024]{1,0:T(8,128)(2,1)} collective-permute-done((bf16[256,1024]{1,0:T(8,128)(2,1)S(1)}, bf16[256,1024]{1,0:T(8,128)(2,1)}, u32[]{:S(2)}, u32[]{:S(2)}) %collective-permute-start.2) | collective-permute-done | bytes 524320 | tf_op jit(solution)/shard_map/ppermute | solution.py:91
  35.4 2.9 %multiply_convert_fusion.2 = bf16[512,1024]{1,0:T(8,128)(2,1)S(1)} fusion(bf16[256,1024]{1,0:T(8,128)(2,1)} %collective-permute-done.3, bf16[256,1024]{1,0:T(8,128)(2,1)} %collective-permute-done.2, bf16[256,1024]{1,0:T(8,128)(2,1)} %collective-permute-done.1, bf16[256,1024]{1,0:T(8,128)(2,1)S(1)} %get-tuple-element.75, s32[512]{0:T(512)S(1)} %bitcast.690, ...), kind=kOutput, calls=%fused_computation.24 | convolution fusion | flops 1087897600 | bytes 3151872 | tf_op jit(solution)/shard_map/dot_general | solution.py:108
  38.4 2.7 %multiply_convert_fusion.1 = (bf16[512,1024]{1,0:T(8,128)(2,1)S(1)}, f32[512,1024]{1,0:T(8,128)}) fusion(f32[1024]{0:T(1024)S(1)} %copy-done.11, bf16[512,1024]{1,0:T(8,128)(2,1)S(1)} %multiply_convert_fusion.2, bf16[1024,1024]{1,0:T(8,128)(2,1)S(1)} %copy-done), kind=kOutput, calls=%fused_computation.22 | convolution fusion | flops 1076887552 | bytes 6295552 | tf_op jit(solution)/shard_map/dot_general | solution.py:109
  42.4 4.9 %all-to-all-start = ((f32[8,64,100]{2,1,0:T(8,128)}), f32[8,64,100]{2,1,0:T(8,128)S(1)}, u32[]{:S(2)}, u32[]{:S(2)}) async-start(f32[8,64,100]{2,1,0:T(8,128)} %bitcast.681), calls=%async_computation | async-start | bytes 524288 | tf_op jit(solution)/shard_map/all_to_all | solution.py:114
  48.0 5.8 %all-to-all-done = f32[8,64,100]{2,1,0:T(8,128)S(1)} async-done(((f32[8,64,100]{2,1,0:T(8,128)}), f32[8,64,100]{2,1,0:T(8,128)S(1)}, u32[]{:S(2)}, u32[]{:S(2)}) %all-to-all-start) | async-done | bytes 204832 | tf_op jit(solution)/shard_map/all_to_all | solution.py:114
  59.4 4.9 %all-to-all-start.1 = ((bf16[8,64,100]{2,1,0:T(8,128)(2,1)}), bf16[8,64,100]{2,1,0:T(8,128)(2,1)}, u32[]{:S(2)}, u32[]{:S(2)}) async-start(bf16[8,64,100]{2,1,0:T(8,128)(2,1)} %constant_dynamic-update-slice_fusion), calls=%async_computation.1 | async-start | bytes 262144 | tf_op jit(solution)/shard_map/all_to_all | solution.py:145
  65.9 3.8 %all-to-all-done.1 = bf16[8,64,100]{2,1,0:T(8,128)(2,1)} async-done(((bf16[8,64,100]{2,1,0:T(8,128)(2,1)}), bf16[8,64,100]{2,1,0:T(8,128)(2,1)}, u32[]{:S(2)}, u32[]{:S(2)}) %all-to-all-start.1) | async-done | bytes 102432 | tf_op jit(solution)/shard_map/all_to_all | solution.py:145
  71.7 2.9 %convert_reduce_fusion.1 = (f32[1024]{0:T(1024)S(1)}, bf16[512,1024]{1,0:T(8,128)(2,1)S(1)}) fusion(f32[512,1024]{1,0:T(8,128)} %get-tuple-element.81, f32[1024]{0:T(1024)S(1)} %copy-done.11, bf16[512,100]{1,0:T(8,128)(2,1)} %bitcast.24, bf16[1024,100]{0,1:T(8,128)(2,1)} %param.18), kind=kOutput, calls=%fused_computation.20 | convolution fusion | flops 111672320 | bytes 3461120 | tf_op jit(solution)/shard_map/dot_general | solution.py:149
  74.7 3.3 %fusion.159 = f32[1024,1024]{0,1:T(8,128)} fusion(bf16[512,1024]{1,0:T(8,128)(2,1)S(1)} %copy-done.3, bf16[512,1024]{1,0:T(8,128)(2,1)S(1)} %get-tuple-element.85), kind=kOutput, calls=%fused_computation.356 | convolution fusion | flops 1073741824 | bytes 6291456 | tf_op jit(solution)/shard_map/dot_general | solution.py:153
  78.1 13.8 %concatenate.22 = f32[1024,1152]{0,1:T(8,128)} concatenate(f32[1024,1024]{0,1:T(8,128)} %fusion.159, f32[1024,100]{0,1:T(8,128)S(1)} %copy-done.1, f32[1024,25]{0,1:T(8,128)S(1)} %broadcast_in_dim.96, f32[1024,1]{0,1:T(1,128)S(1)} %bitcast.687, f32[1024,1]{0,1:T(1,128)S(1)} %bitcast.682, f32[1024,1]{0,1:T(1,128)S(1)} %broadcast_in_dim.101), dimensions={1} | concatenate | bytes 9437184 | tf_op jit(solution)/shard_map/concatenate | solution.py:157
  96.1 2.6 %collective-permute-done.7 = bf16[512,1152]{0,1:T(8,128)(2,1)} collective-permute-done((bf16[512,1152]{0,1:T(8,128)(2,1)S(1)}, bf16[512,1152]{0,1:T(8,128)(2,1)}, u32[]{:S(2)}, u32[]{:S(2)}) %collective-permute-start.7) | collective-permute-done | bytes 1179680 | tf_op jit(solution)/shard_map/ppermute | solution.py:59
  103.6 22.0 %all_to_all.25 = bf16[16,32,1152]{2,1,0:T(8,128)(2,1)S(1)} all-to-all(bf16[16,32,1152]{2,1,0:T(8,128)(2,1)} %bitcast.680), channel_id=1, replica_groups=mesh['xl'=2,'c'=2,'z'=8,'y'=4,'xh'=2] {'y','xh','xl'}, dimensions={0} | all-to-all | bytes 2359296 | tf_op jit(solution)/shard_map/all_to_all | solution.py:62
  126.1 22.1 %all_to_all.26 = bf16[8,32,1152]{2,1,0:T(8,128)(2,1)S(1)} all-to-all(bf16[8,32,1152]{2,1,0:T(8,128)(2,1)S(1)} %broadcast_in_dim.114), channel_id=1, replica_groups=mesh['xl'=2,'c'=2,'z'=8,'y'=4,'xh'=2] {'z'}, dimensions={0} | all-to-all | bytes 1179648 | tf_op jit(solution)/shard_map/all_to_all | solution.py:41
  149.7 3.7 %all-to-all-start.4 = ((bf16[16,32,1152]{2,1,0:T(8,128)(2,1)}), bf16[16,32,1152]{2,1,0:T(8,128)(2,1)S(1)}, u32[]{:S(2)}, u32[]{:S(2)}) async-start(bf16[16,32,1152]{2,1,0:T(8,128)(2,1)} %broadcast_in_dim.119), calls=%async_computation.4 | async-start | bytes 2359296 | tf_op jit(solution)/shard_map/all_to_all | solution.py:41
  153.4 6.5 %fusion.158 = (bf16[1024,1024]{1,0:T(8,128)(2,1)}, f32[1024,1024]{1,0:T(8,128)}) fusion(bf16[512,1024]{1,0:T(8,128)(2,1)} %copy-done.4, bf16[1024,1024]{1,0:T(8,128)(2,1)S(1)} %copy-done, s32[512]{0:T(512)S(1)} %bitcast.691, s32[512]{0:T(512)S(1)} %bitcast.693, s32[512]{0:T(512)S(1)} %bitcast.689), kind=kOutput, calls=%fused_computation.355 | convolution fusion | flops 2154299392 | bytes 9443328 | tf_op jit(solution)/shard_map/dot_general | solution.py:161
  159.9 9.3 %all-to-all-done.4 = bf16[16,32,1152]{2,1,0:T(8,128)(2,1)S(1)} async-done(((bf16[16,32,1152]{2,1,0:T(8,128)(2,1)}), bf16[16,32,1152]{2,1,0:T(8,128)(2,1)S(1)}, u32[]{:S(2)}, u32[]{:S(2)}) %all-to-all-start.4) | async-done | bytes 1179680 | tf_op jit(solution)/shard_map/all_to_all | solution.py:41
  169.2 4.2 %collective-permute-start.8 = (bf16[512,1152]{1,0:T(8,128)(2,1)S(1)}, bf16[512,1152]{1,0:T(8,128)(2,1)}, u32[]{:S(2)}, u32[]{:S(2)}) collective-permute-start(bf16[512,1152]{1,0:T(8,128)(2,1)S(1)} %bitcast.679), channel_id=1, source_target_pairs={{0,64},{64,0},{1,65},{65,1},{2,66},{66,2},{3,67},{67,3},{4,68},{68... | collective-permute-start | bytes 3538952 | tf_op jit(solution)/shard_map/ppermute | solution.py:69
  173.4 2.5 %fusion.155 = (bf16[256,1024]{1,0:T(8,128)(2,1)}, bf16[256,1024]{1,0:T(8,128)(2,1)}, bf16[256,1024]{1,0:T(8,128)(2,1)}) fusion(bf16[1024,1024]{1,0:T(8,128)(2,1)} %get-tuple-element.82), kind=kLoop, calls=%fused_computation.352 | loop fusion | bytes 3145728 | tf_op jit(solution)/shard_map/slice | solution.py:165
  178.8 25.0 %collective-permute-done.6 = bf16[256,1024]{1,0:T(8,128)(2,1)} collective-permute-done((bf16[256,1024]{1,0:T(8,128)(2,1)}, bf16[256,1024]{1,0:T(8,128)(2,1)}, u32[]{:S(2)}, u32[]{:S(2)}) %collective-permute-start.6) | collective-permute-done | bytes 524320 | tf_op jit(solution)/shard_map/ppermute | solution.py:166
  203.8 2.7 %collective-permute-done.5 = bf16[256,1024]{1,0:T(8,128)(2,1)} collective-permute-done((bf16[256,1024]{1,0:T(8,128)(2,1)}, bf16[256,1024]{1,0:T(8,128)(2,1)}, u32[]{:S(2)}, u32[]{:S(2)}) %collective-permute-start.5) | collective-permute-done | bytes 524320 | tf_op jit(solution)/shard_map/ppermute | solution.py:164
  213.7 2.6 %slice.207 = f32[1024,1024]{1,0:T(8,128)} slice(f32[1024,1152]{1,0:T(8,128)S(1)} %maximum_convert_fusion), slice={[0:1024], [0:1024]} | slice | bytes 8388608 | tf_op jit(solution)/shard_map/slice | solution.py:175
  (93 shorter events, 36.1 us)
Async XLA Ops:
  0.6 37.7 %copy-start = (bf16[1024,1024]{1,0:T(8,128)(2,1)S(1)}, bf16[1024,1024]{1,0:T(8,128)(2,1)}, u32[]{:S(2)}) copy-start(bf16[1024,1024]{1,0:T(8,128)(2,1)} %param.16) | copy-start | bytes 6291460
  0.6 13.3 %copy-start.8 = (s32[256,3]{0,1:T(4,128)S(1)}, s32[256,3]{0,1:T(4,128)}, u32[]{:S(2)}) copy-start(s32[256,3]{0,1:T(4,128)} %param.11) | copy-start | bytes 9220
  0.7 16.3 %copy-start.7 = (f32[100,256]{1,0:T(8,128)S(1)}, f32[100,256]{1,0:T(8,128)}, u32[]{:S(2)}) copy-start(f32[100,256]{1,0:T(8,128)} %param.13) | copy-start | bytes 307204
  0.7 16.5 %copy-start.12 = (s32[64]{0:T(128)S(1)}, s32[64]{0:T(128)}, u32[]{:S(2)}) copy-start(s32[64]{0:T(128)} %param.12) | copy-start | bytes 772
  2.1 30.0 %collective-permute-start.3 = (bf16[256,1024]{1,0:T(8,128)(2,1)S(1)}, bf16[256,1024]{1,0:T(8,128)(2,1)}, u32[]{:S(2)}, u32[]{:S(2)}) collective-permute-start(bf16[256,1024]{1,0:T(8,128)(2,1)S(1)} %get-tuple-element.76), channel_id=1, source_target_pairs={{0,63},{1,2},{2,1},{3,4},{4,3},{5,6},{6,5},{7,8},{8,7},{9,10},{10,... | collective-permute-start | bytes 1572872 | tf_op jit(solution)/shard_map/ppermute | solution.py:90
  13.5 21.9 %collective-permute-start.2 = (bf16[256,1024]{1,0:T(8,128)(2,1)S(1)}, bf16[256,1024]{1,0:T(8,128)(2,1)}, u32[]{:S(2)}, u32[]{:S(2)}) collective-permute-start(bf16[256,1024]{1,0:T(8,128)(2,1)S(1)} %get-tuple-element.75), channel_id=1, source_target_pairs={{0,62},{1,3},{2,0},{3,5},{4,2},{5,7},{6,4},{7,9},{8,6},{9,11},{10,... | collective-permute-start | bytes 1572872 | tf_op jit(solution)/shard_map/ppermute | solution.py:91
  14.0 21.4 %collective-permute-start.1 = (bf16[256,1024]{1,0:T(8,128)(2,1)S(1)}, bf16[256,1024]{1,0:T(8,128)(2,1)}, u32[]{:S(2)}, u32[]{:S(2)}) collective-permute-start(bf16[256,1024]{1,0:T(8,128)(2,1)S(1)} %get-tuple-element.76), channel_id=1, source_target_pairs={{0,1},{1,0},{2,3},{3,2},{4,5},{5,4},{6,7},{7,6},{8,9},{9,8},{10,11... | collective-permute-start | bytes 1572872 | tf_op jit(solution)/shard_map/ppermute | solution.py:89
  14.0 18.1 %collective-permute-start = (s32[256,3]{0,1:T(4,128)S(1)}, s32[256,3]{0,1:T(4,128)S(1)}, u32[]{:S(2)}, u32[]{:S(2)}) collective-permute-start(s32[256,3]{0,1:T(4,128)S(1)} %copy-done.8), channel_id=1, source_target_pairs={{0,1},{1,0},{2,3},{3,2},{4,5},{5,4},{6,7},{7,6},{8,9},{9,8},{10,11... | collective-permute-start | bytes 9224 | tf_op jit(solution)/shard_map/ppermute | solution.py:88
  35.4 3.0 %copy-start.11 = (f32[1024]{0:T(1024)S(1)}, f32[1024]{0:T(1024)}, u32[]{:S(2)}) copy-start(f32[1024]{0:T(1024)} %param.17) | copy-start | bytes 12292
  38.3 2.7 %copy-start.2 = (bf16[512,1024]{1,0:T(8,128)(2,1)}, bf16[512,1024]{1,0:T(8,128)(2,1)S(1)}, u32[]{:S(2)}) copy-start(bf16[512,1024]{1,0:T(8,128)(2,1)S(1)} %multiply_convert_fusion.2) | copy-start | bytes 3145732
  38.4 2.7 %copy-start.5 = (bf16[1024,100]{0,1:T(8,128)(2,1)S(1)}, bf16[1024,100]{0,1:T(8,128)(2,1)}, u32[]{:S(2)}) copy-start(bf16[1024,100]{0,1:T(8,128)(2,1)} %param.18) | copy-start | bytes 614404
  41.1 6.2 %copy-start.10 = (f32[256]{0:T(256)S(1)}, f32[256]{0:T(256)}, u32[]{:S(2)}) copy-start(f32[256]{0:T(256)} %param.14) | copy-start | bytes 3076
  41.1 12.7 %copy-start.6 = (f32[100]{0:T(128)S(1)}, f32[100]{0:T(128)}, u32[]{:S(2)}) copy-start(f32[100]{0:T(128)} %param.15) | copy-start | bytes 1204
  42.4 11.4 %all-to-all-start = ((f32[8,64,100]{2,1,0:T(8,128)}), f32[8,64,100]{2,1,0:T(8,128)S(1)}, u32[]{:S(2)}, u32[]{:S(2)}) async-start(f32[8,64,100]{2,1,0:T(8,128)} %bitcast.681), calls=%async_computation | async-start | bytes 524288 | tf_op jit(solution)/shard_map/all_to_all | solution.py:114
  59.4 10.3 %all-to-all-start.1 = ((bf16[8,64,100]{2,1,0:T(8,128)(2,1)}), bf16[8,64,100]{2,1,0:T(8,128)(2,1)}, u32[]{:S(2)}, u32[]{:S(2)}) async-start(bf16[8,64,100]{2,1,0:T(8,128)(2,1)} %constant_dynamic-update-slice_fusion), calls=%async_computation.1 | async-start | bytes 262144 | tf_op jit(solution)/shard_map/all_to_all | solution.py:145
  71.7 3.0 %copy-start.3 = (bf16[512,1024]{1,0:T(8,128)(2,1)S(1)}, bf16[512,1024]{1,0:T(8,128)(2,1)}, u32[]{:S(2)}) copy-start(bf16[512,1024]{1,0:T(8,128)(2,1)} %copy-done.2) | copy-start | bytes 3145732
  74.7 3.4 %copy-start.4 = (bf16[512,1024]{1,0:T(8,128)(2,1)}, bf16[512,1024]{1,0:T(8,128)(2,1)S(1)}, u32[]{:S(2)}) copy-start(bf16[512,1024]{1,0:T(8,128)(2,1)S(1)} %get-tuple-element.85) | copy-start | bytes 3145732
  74.7 3.4 %copy-start.1 = (f32[1024,100]{0,1:T(8,128)S(1)}, f32[1024,100]{0,1:T(8,128)}, u32[]{:S(2)}) copy-start(f32[1024,100]{0,1:T(8,128)} %fusion.160) | copy-start | bytes 1228804
  95.0 3.7 %collective-permute-start.7 = (bf16[512,1152]{0,1:T(8,128)(2,1)S(1)}, bf16[512,1152]{0,1:T(8,128)(2,1)}, u32[]{:S(2)}, u32[]{:S(2)}) collective-permute-start(bf16[512,1152]{0,1:T(8,128)(2,1)S(1)} %select_convert_fusion.1), channel_id=1, source_target_pairs={{0,64},{64,0},{1,65},{65,1},{2,66},{66,2},{3,67},{67,3},{4,68},{68... | collective-permute-start | bytes 3538952 | tf_op jit(solution)/shard_map/ppermute | solution.py:59
  149.7 19.5 %all-to-all-start.4 = ((bf16[16,32,1152]{2,1,0:T(8,128)(2,1)}), bf16[16,32,1152]{2,1,0:T(8,128)(2,1)S(1)}, u32[]{:S(2)}, u32[]{:S(2)}) async-start(bf16[16,32,1152]{2,1,0:T(8,128)(2,1)} %broadcast_in_dim.119), calls=%async_computation.4 | async-start | bytes 2359296 | tf_op jit(solution)/shard_map/all_to_all | solution.py:41
  169.2 40.5 %collective-permute-start.8 = (bf16[512,1152]{1,0:T(8,128)(2,1)S(1)}, bf16[512,1152]{1,0:T(8,128)(2,1)}, u32[]{:S(2)}, u32[]{:S(2)}) collective-permute-start(bf16[512,1152]{1,0:T(8,128)(2,1)S(1)} %bitcast.679), channel_id=1, source_target_pairs={{0,64},{64,0},{1,65},{65,1},{2,66},{66,2},{3,67},{67,3},{4,68},{68... | collective-permute-start | bytes 3538952 | tf_op jit(solution)/shard_map/ppermute | solution.py:69
  175.9 27.9 %collective-permute-start.6 = (bf16[256,1024]{1,0:T(8,128)(2,1)}, bf16[256,1024]{1,0:T(8,128)(2,1)}, u32[]{:S(2)}, u32[]{:S(2)}) collective-permute-start(bf16[256,1024]{1,0:T(8,128)(2,1)} %get-tuple-element.71), channel_id=1, source_target_pairs={{63,0},{2,1},{1,2},{4,3},{3,4},{6,5},{5,6},{8,7},{7,8},{10,9},{9,1... | collective-permute-start | bytes 1572872 | tf_op jit(solution)/shard_map/ppermute | solution.py:166
  175.9 30.6 %collective-permute-start.5 = (bf16[256,1024]{1,0:T(8,128)(2,1)}, bf16[256,1024]{1,0:T(8,128)(2,1)}, u32[]{:S(2)}, u32[]{:S(2)}) collective-permute-start(bf16[256,1024]{1,0:T(8,128)(2,1)} %get-tuple-element.72), channel_id=1, source_target_pairs={{1,0},{0,1},{3,2},{2,3},{5,4},{4,5},{7,6},{6,7},{9,8},{8,9},{11,10... | collective-permute-start | bytes 1572872 | tf_op jit(solution)/shard_map/ppermute | solution.py:164
  177.3 29.2 %collective-permute-start.4 = (bf16[256,1024]{1,0:T(8,128)(2,1)}, bf16[256,1024]{1,0:T(8,128)(2,1)}, u32[]{:S(2)}, u32[]{:S(2)}) collective-permute-start(bf16[256,1024]{1,0:T(8,128)(2,1)} %get-tuple-element.70), channel_id=1, source_target_pairs={{62,0},{3,1},{0,2},{5,3},{2,4},{7,5},{4,6},{9,7},{6,8},{11,9},{8,1... | collective-permute-start | bytes 1572872 | tf_op jit(solution)/shard_map/ppermute | solution.py:165
  (1 other events, 2.7 us)

commit v2 on v1

v2 whole, which is shorter than its diff:
```python
import jax
import jax.numpy as jnp
from jax import lax
from jax.experimental import pallas as pl
from jax.experimental.pallas import tpu as pltpu
from jax.sharding import Mesh, PartitionSpec as P

smooth_sq = 0.0025
smooth_width = 0.05
bf16 = jnp.bfloat16
f32 = jnp.float32

ENS = ("xl", "c")
GRID = ("z", "y", "xh")
GROUP = ("xh", "xl", "c")
PLANE = ("y", "xh", "xl")
MEMBERS = 8
H = 1024
LANES = 128
CHUNK = 256
STEPS = H // CHUNK
ROWS = H + LANES
ROW_GROUPS = 4
PART = ROWS // ROW_GROUPS
PARTS = 16
GB_IN, HIGH, LOW = 100, 101, 102
HIGH_IN_PART = H + HIGH - 3 * PART


def dot(a, b, dims=((1,), (0,))):
    return lax.dot_general(a, b, (dims, ((), ())), preferred_element_type=f32)


def call(kernel, name, flops=0, nbytes=0, trans=0, **kw):
    return pl.pallas_call(
        kernel,
        name=name,
        cost_estimate=pl.CostEstimate(flops=flops, bytes_accessed=nbytes, transcendentals=trans),
        compiler_params=pltpu.CompilerParams(vmem_limit_bytes=24 * 1024 * 1024),
        **kw,
    )


def near(*xs):
    return [pltpu.with_memory_space_constraint(x, pltpu.VMEM) for x in xs]


def far(x):
    return pltpu.with_memory_space_constraint(x, pltpu.HBM)


def out(shape, dtype):
    return pltpu.VMEM(shape, dtype)


def ring(shift_odd, shift_even):
    n = 64
    return [(i, (i + (shift_odd if i % 2 else shift_even)) % n) for i in range(n)]


SWAP = ring(-1, 1)
SAME = ring(2, -2)
DIAG = ring(1, -1)


def back(perm):
    return [(b, a) for a, b in perm]


def a2a(x, axes):
    return lax.all_to_all(x, axes, split_axis=0, concat_axis=0, tiled=True)


def forward_kernel(pick, own, swp, same, diag, w_in, b_in, w_out, b_out, feats_t, hid, slope, pred, w_here, sem):
    n = own.shape[0]
    copy = pltpu.make_async_copy(w_in, w_here, sem)
    copy.start()
    total = dot(pick[:, :n], own[...])
    for k, ref in enumerate((swp, same, diag)):
        total = total + dot(pick[:, (k + 1) * n : (k + 2) * n], ref[...])
    feats = (total / 3.0).astype(bf16)
    feats_t[...] = feats.T
    copy.wait()
    v = dot(feats, w_here[...]) + b_in[...]
    cdf = 0.5 * (1.0 + lax.erf(v * 0.7071067811865476))
    slope[...] = (cdf + v * jnp.exp(-0.5 * v * v) * 0.3989422804014327).astype(bf16)
    h = (v * cdf).astype(bf16)
    hid[...] = h
    p = dot(h, w_out[...]) + b_out[...]
    pts = pred.shape[1]
    for i in range(MEMBERS):
        pred[i] = p[i * pts : (i + 1) * pts]


def forward(pick, own, swp, same, diag, w_in, b_in, w_out, b_out):
    m = pick.shape[0]
    return call(
        forward_kernel,
        "forward",
        flops=2 * m * H * (2 * H + LANES),
        nbytes=12 * 2**20,
        trans=2 * m * H,
        in_specs=[pl.BlockSpec(memory_space=pltpu.VMEM)] * 5
        + [pl.BlockSpec(memory_space=pl.ANY)]
        + [pl.BlockSpec(memory_space=pltpu.VMEM)] * 3,
        scratch_shapes=[pltpu.VMEM((H, H), bf16), pltpu.SemaphoreType.DMA],
        out_shape=[
            out((H, m), bf16),
            out((m, H), bf16),
            out((m, H), bf16),
            jax.ShapeDtypeStruct((MEMBERS, m // MEMBERS, LANES), f32),
        ],
    )(*near(pick, own, swp, same, diag), far(w_in), *near(b_in, w_out, b_out))


def crps_kernel(pred, aim, wgt, dpred, small):
    mm = float(MEMBERS)
    pts = pred.shape[1]
    gb = jnp.zeros((1, LANES), f32)
    loss = jnp.zeros((1, LANES), f32)
    for r in range(0, pts, 16):
        p = [pred[i, r : r + 16, :] for i in range(MEMBERS)]
        pair = [jnp.zeros((16, LANES), f32) for _ in range(MEMBERS)]
        gaps = jnp.zeros((16, LANES), f32)
        hits = jnp.zeros((16, LANES), f32)
        for i in range(MEMBERS):
            for j in range(i + 1, MEMBERS):
                d = p[i] - p[j]
                sq = d * d + smooth_sq
                inv = lax.rsqrt(sq)
                gaps = gaps + (sq * inv - smooth_width)
                pair[i] = pair[i] + d * inv
                pair[j] = pair[j] - d * inv
        w = wgt[r : r + 16, :]
        t = aim[r : r + 16, :]
        g_sum = jnp.zeros((16, LANES), f32)
        for i in range(MEMBERS):
            d = p[i] - t
            sq = d * d + smooth_sq
            inv = lax.rsqrt(sq)
            hits = hits + (sq * inv - smooth_width)
            g = w * (d * inv / mm - pair[i] / (mm * (mm - 1.0)))
            g_sum = g_sum + g
            dpred[i, r : r + 16, :] = g.astype(bf16)
        gb = gb + jnp.sum(g_sum, axis=0, keepdims=True)
        loss = loss + jnp.sum(w * (hits / mm - gaps / (mm * (mm - 1.0))), axis=0, keepdims=True)
    small[:, :LANES] = gb
    small[:, LANES:] = loss


def crps(pred, aim, wgt):
    pts = aim.shape[0]
    return call(
        crps_kernel,
        "crps",
        flops=40 * 36 * pts * LANES,
        nbytes=2**19,
        trans=36 * pts * LANES,
        out_shape=[
            jax.ShapeDtypeStruct((MEMBERS, pts, LANES), bf16),
            out((1, 2 * LANES), f32),
        ],
    )(*near(pred, aim, wgt))


def packed(half, feats_t, dpre, dpred, hid, small):
    cols = pl.ds(pl.multiple_of(half * (H // 2), H // 2), H // 2)
    d = dpre[:, cols]
    gb_in = jnp.sum(d.astype(f32), axis=0, keepdims=True)
    foot = dot(dpred[...], hid[:, cols], ((0,), (0,)))
    row = lax.broadcasted_iota(jnp.int32, foot.shape, 0)
    s = jnp.concatenate([small[...], jnp.zeros_like(small[...])], axis=1)
    s = jnp.where(half == 0, s, 0.0)
    high = s.astype(bf16).astype(f32)
    foot = jnp.where(row == GB_IN, gb_in, foot)
    foot = jnp.where(row == HIGH, high, foot)
    foot = jnp.where(row == LOW, s - high, foot)
    main = dot(feats_t[...], d)
    for g in range(ROW_GROUPS):
        lanes = slice(g * LANES, (g + 1) * LANES)
        for r in range(ROW_GROUPS):
            block = main[r * PART : (r + 1) * PART, lanes]
            if r == ROW_GROUPS - 1:
                block = jnp.concatenate([block, foot[:, lanes]], axis=0)
            yield g * ROW_GROUPS + r, block


def backward_kernel(core, dpred, w_out, slope, hid, feats_t, small, dpre, send):
    d = dot(dpred[...], w_out[...], ((1,), (1,))) * slope[...].astype(f32)
    dpre[...] = d.astype(bf16)
    for i, block in packed(1 - core[0], feats_t, dpre, dpred, hid, small):
        send[i] = block.astype(bf16)


def backward(core, dpred, w_out, slope, hid, feats_t, small):
    m = dpred.shape[0]
    return call(
        backward_kernel,
        "backward",
        flops=m * H * (H + 4 * LANES),
        nbytes=6 * 2**20,
        in_specs=[pl.BlockSpec(memory_space=pltpu.SMEM)]
        + [pl.BlockSpec(memory_space=pltpu.VMEM)] * 6,
        out_shape=[out((m, H), bf16), out((PARTS, PART, LANES), bf16)],
    )(core, *near(dpred, w_out, slope, hid, feats_t, small))


def latent_kernel(dpre, w_in, pick_t, own, swp, same, diag):
    d = (dot(dpre[...], w_in[...], ((1,), (1,))) / 3.0).astype(bf16)
    n = own.shape[0]
    for k, ref in enumerate((own, swp, same, diag)):
        ref[...] = dot(pick_t[k * n : (k + 1) * n, :], d).astype(ref.dtype)


def latent_grads(dpre, w_in, pick_t):
    m = dpre.shape[0]
    n = pick_t.shape[0] // 4
    return call(
        latent_kernel,
        "latent_grads",
        flops=4 * m * H * H,
        nbytes=8 * 2**20,
        out_shape=[out((n, H), f32)] + [jax.ShapeDtypeStruct((n, H), bf16)] * 3,
    )(*near(dpre, w_in, pick_t))


def resplit(total):
    row = lax.broadcasted_iota(jnp.int32, total.shape, 0)
    both = total[HIGH_IN_PART : HIGH_IN_PART + 1] + total[HIGH_IN_PART + 1 : HIGH_IN_PART + 2]
    high = both.astype(bf16).astype(f32)
    total_high = jnp.where(row == HIGH_IN_PART, high, total)
    return jnp.where(row == HIGH_IN_PART + 1, both - high, total_high).astype(bf16)


def pair_kernel(core, dpred, dpre, hid, feats_t, small, got, part):
    for i, block in packed(core[0], feats_t, dpre, dpred, hid, small):
        total = block + got[i].astype(f32)
        if i % ROW_GROUPS == ROW_GROUPS - 1:
            total = resplit(total)
        part[i] = total.astype(bf16)


def pair_sum(core, dpred, dpre, hid, feats_t, small, got):
    m = dpred.shape[0]
    return call(
        pair_kernel,
        "pair_sum",
        flops=m * H * (H + 2 * LANES),
        nbytes=6 * 2**20,
        in_specs=[pl.BlockSpec(memory_space=pltpu.SMEM)]
        + [pl.BlockSpec(memory_space=pltpu.VMEM)] * 6,
        out_shape=jax.ShapeDtypeStruct(got.shape, bf16),
    )(core, *near(dpred, dpre, hid, feats_t, small, got))


def total_kernel(group, parts, copies):
    total = parts[0].astype(f32)
    for i in range(1, parts.shape[0]):
        total = total + parts[i].astype(f32)
    last = group[0] == ROW_GROUPS - 1
    done = jnp.where(last, resplit(total).astype(f32), total).astype(bf16)
    for i in range(copies.shape[0]):
        copies[i] = done


def total_and_spread(group, parts, copies):
    n = parts.shape[0]
    return call(
        total_kernel,
        "total",
        flops=n * PART * LANES,
        nbytes=2 * (n + copies) * PART * LANES,
        in_specs=[
            pl.BlockSpec(memory_space=pltpu.SMEM),
            pl.BlockSpec(memory_space=pltpu.VMEM),
        ],
        out_shape=jax.ShapeDtypeStruct((copies, PART, LANES), bf16),
    )(group, *near(parts))


def unpack_kernel(core, mine, got, gw_in, gw_out_t, gb_in, gb_out, loss):
    j = pl.program_id(0)

    def put(ref):
        for g in range(2):
            lanes = slice(g * LANES, (g + 1) * LANES)
            base = g * ROW_GROUPS
            for r in range(ROW_GROUPS - 1):
                gw_in[r * PART : (r + 1) * PART, lanes] = ref[base + r].astype(f32)
            r = ROW_GROUPS - 1
            gw_in[r * PART :, lanes] = ref[base + r, : H - r * PART, :].astype(f32)
            foot = ref[base + r, H - r * PART :, :].astype(f32)
            gw_out_t[:, lanes] = foot[:GB_IN]
            gb_in[:, lanes] = foot[GB_IN : GB_IN + 1]
            small = foot[HIGH : HIGH + 1] + foot[LOW : LOW + 1]

            @pl.when(j == 0)
            def _():
                if g == 0:
                    gb_out[...] = small[:, :GB_IN]
                else:
                    loss[...] = jnp.sum(small, axis=1, keepdims=True)

    here = j // 2 == core[0]

    @pl.when(here)
    def _():
        put(mine)

    @pl.when(jnp.logical_not(here))
    def _():
        put(got)


def unpack(core, mine, got):
    block = (2 * ROW_GROUPS, PART, LANES)
    cols = lambda j, core: (0, j)
    whole = lambda j, core: (0, 0)
    return call(
        unpack_kernel,
        "unpack",
        nbytes=8 * 2**20,
        grid_spec=pltpu.PrefetchScalarGridSpec(
            num_scalar_prefetch=1,
            grid=(STEPS,),
            in_specs=[
                pl.BlockSpec(block, lambda j, core: (jnp.clip(j - 2 * core[0], 0, 1), 0, 0)),
                pl.BlockSpec(block, lambda j, core: (jnp.clip(j - 2 * (1 - core[0]), 0, 1), 0, 0)),
            ],
            out_specs=[
                pl.BlockSpec((H, CHUNK), cols),
                pl.BlockSpec((GB_IN, CHUNK), cols),
                pl.BlockSpec((1, CHUNK), cols),
                pl.BlockSpec((1, GB_IN), whole),
                pl.BlockSpec((1, 1), whole),
            ],
        ),
        out_shape=[
            jax.ShapeDtypeStruct((H, H), f32),
            jax.ShapeDtypeStruct((GB_IN, H), f32),
            jax.ShapeDtypeStruct((1, H), f32),
            jax.ShapeDtypeStruct((1, GB_IN), f32),
            jax.ShapeDtypeStruct((1, 1), f32),
        ],
    )(core, mine, got)


def final_kernel(side, own, same, swp, diag, both):
    j = pl.program_id(0)

    @pl.when(j == 0)
    def _():
        both[0] = (own[...] + same[...].astype(f32)).astype(bf16)

    @pl.when(j == 1)
    def _():
        both[0] = (swp[...].astype(f32) + diag[...].astype(f32)).astype(bf16)


def final_latents(side, own, same, swp, diag):
    n = own.shape[0]
    whole = lambda j, side: (0, 0)
    block = pl.BlockSpec((n, H), whole)
    return call(
        final_kernel,
        "final_latents",
        nbytes=5 * 2**20,
        grid_spec=pltpu.PrefetchScalarGridSpec(
            num_scalar_prefetch=1,
            grid=(2,),
            in_specs=[block] * 4,
            out_specs=pl.BlockSpec(
                (1, n, H), lambda j, side: (jnp.where(j == 0, side[0], 1 - side[0]), 0, 0)
            ),
        ),
        out_shape=jax.ShapeDtypeStruct((2, n, H), bf16),
    )(side, own, same, swp, diag)


def body(latent, edge_src, counts, targets, area, var_weight, w_in, b_in, w_out, b_out):
    l_tile = latent.shape[1]
    g_tile, k_edges = edge_src.shape
    n_vars = w_out.shape[1]
    h = lax.axis_index("xh")
    core = lax.axis_index("c")
    pair = lax.axis_index(("z", "y"))
    tile = 2 * pair + h
    quarter = lax.axis_index(ENS)
    pts = g_tile // 4
    side = jnp.reshape(h, (1,)).astype(jnp.int32)
    core = jnp.reshape(core, (1,)).astype(jnp.int32)
    group = lax.rem(lax.axis_index(PLANE), ROW_GROUPS)
    group = jnp.reshape(group, (1,)).astype(jnp.int32)

    own = lax.dynamic_index_in_dim(latent, h, 0, keepdims=False)
    oth = lax.dynamic_index_in_dim(latent, 1 - h, 0, keepdims=False)
    edges_there = lax.ppermute(edge_src, GRID, SWAP)
    swapped = lax.ppermute(oth, GRID, SWAP)
    diag = lax.ppermute(oth, GRID, DIAG)
    same = lax.ppermute(own, GRID, SAME)

    edges = jnp.where(
        h == 0,
        jnp.concatenate([edge_src, edges_there], axis=0),
        jnp.concatenate([edges_there, edge_src], axis=0),
    )
    step = edges // l_tile - 2 * pair
    block = jnp.mod(jnp.where(h == 0, step, 1 - step), 4)
    local = block * l_tile + jnp.mod(edges, l_tile)
    nodes = lax.broadcasted_iota(jnp.int32, (2 * g_tile, 4 * l_tile), 1)
    nodes_t = lax.broadcasted_iota(jnp.int32, (4 * l_tile, 2 * g_tile), 0)
    pick = jnp.zeros((2 * g_tile, 4 * l_tile), f32)
    pick_t = jnp.zeros((4 * l_tile, 2 * g_tile), f32)
    for k in range(k_edges):
        pick = pick + (local[:, k : k + 1] == nodes).astype(f32)
        pick_t = pick_t + (local[:, k][None, :] == nodes_t).astype(f32)
    pick = pick.astype(bf16)
    pick_t = pick_t.astype(bf16)

    start = quarter * pts
    point = start + jnp.arange(pts, dtype=jnp.int32)
    valid = (point < counts[tile]).astype(f32)
    pad = LANES - n_vars
    var_weight = jnp.pad(var_weight, (0, pad))
    wgt = (lax.dynamic_slice_in_dim(area, start, pts, 0) * valid)[:, None] * var_weight[None, :]
    aim = jnp.pad(lax.dynamic_slice_in_dim(targets, start, pts, 1).T, ((0, 0), (0, pad)))
    w_out_p = jnp.pad(w_out, ((0, 0), (0, pad)))
    b_out_p = jnp.pad(b_out, (0, pad))[None]

    pick, pick_t, aim, wgt = lax.optimization_barrier((pick, pick_t, aim, wgt))
    feats_t, hidden, slope, pred = forward(
        pick, own, swapped, same, diag, w_in, b_in[None], w_out_p, b_out_p
    )
    pred = a2a(pred, GROUP)
    dpred, small = crps(pred, aim, wgt)
    dpred = a2a(dpred, GROUP).reshape(MEMBERS * pts, LANES)
    dpre, send = backward(core, dpred, w_out_p, slope, hidden, feats_t, small)
    got = lax.ppermute(send, "c", [(0, 1), (1, 0)])
    d_own, d_swap, d_same, d_diag = latent_grads(dpre, w_in, pick_t)
    got, d_own = lax.optimization_barrier((got, d_own))
    part = pair_sum(core, dpred, dpre, hidden, feats_t, small, got)
    part = a2a(part, PLANE)
    part, d_swap, d_same, d_diag = lax.optimization_barrier((part, d_swap, d_same, d_diag))
    r_swap = lax.ppermute(d_swap, GRID, back(SWAP))
    r_same = lax.ppermute(d_same, GRID, back(SAME))
    r_diag = lax.ppermute(d_diag, GRID, back(DIAG))
    part = total_and_spread(group, part, 8)
    part = lax.cond(counts[0] >= 0, lambda x: a2a(x, "z"), lambda x: x, part)
    part, r_swap, r_same, r_diag = lax.optimization_barrier((part, r_swap, r_same, r_diag))
    part = total_and_spread(group, part, PARTS)
    part = a2a(part, PLANE)
    got = lax.ppermute(part, "c", [(0, 1), (1, 0)])
    grad_latent = final_latents(side, d_own, r_same, r_swap, r_diag)
    gw_in, gw_out_t, gb_in, gb_out, loss = unpack(core, part, got)
    return (
        grad_latent,
        gw_in,
        gb_in[0],
        gw_out_t.T,
        gb_out[0],
        loss[0, 0],
    )


def solution(mesh):
    fine = Mesh(mesh.devices.reshape(2, 2, 8, 4, 2), ENS + GRID)
    in_specs = (
        P(ENS, GRID, None),
        P(GRID, None),
        P(),
        P(None, GRID),
        P(GRID),
        P(),
        P(),
        P(),
        P(),
        P(),
    )
    out_specs = (P(ENS, GRID, None), P(), P(), P(), P(), P())
    return jax.shard_map(body, mesh=fine, in_specs=in_specs, out_specs=out_specs, check_vma=False)
```

time: 224 us -> 154 us (0.69); the launches traced: 220 us -> 154 us
  waiting for transfers between devices: 66.8 us -> 15.2 us
  blocking collectives: 44.1 us -> 88.7 us
  local copies, waits for them, and re-layouts: 31.1 us -> 2.46 us
  matrix products: 20.9 us -> 0 us
  other arithmetic: 17 us -> 2.33 us
  Pallas kernels: 0 us -> 14.3 us
  starting transfers between devices: 36.6 us -> 29.3 us
    all_to_all x2 -> x5, blocking collectives: 44.1 us -> 88.7 us  [a2a(): return lax.all_to_all(x, axes, split_axis=0, concat_axis=0, tiled=True)]
    ppermute x5, waiting for transfers between devices: 30.3 us -> 0.2 us  [the longest x1 0.19 us: body(): got = lax.ppermute(part, 'c', [(0, 1), (1, 0)])]
    dot_general x7 -> x0, matrix products: 20.9 us -> none  [the longest x1 6.51 us: body(): lax.dot_general(pick, dfeat, (((0,), (0,)), ((), ())), preferred_element_...]
    all_to_all x3 -> x0, waiting for transfers between devices: 18.9 us -> none  [the longest x1 9.28 us: spread(): return lax.all_to_all(many, axes, split_axis=0, concat_axis=0, tiled=True)]
    pallas_call x0 -> x9, Pallas kernels: none -> 14.3 us  [the longest x1 3.55 us: forward(): call(forward_kernel, 'forward', flops=2 * m * H * (2 * H + LANES), nbytes...]
    concatenate x1 -> x0, local copies, waits for them, and re-layouts: 13.8 us -> none  [body(): jnp.concatenate([gw_in, gw_out, gap, gb_in[:, None], small[:, None], zero...]
    all_to_all x3 -> x0, starting transfers between devices: 13.5 us -> none  [the longest x1 4.91 us: body(): lax.all_to_all(grad_pred.astype(bf16), GROUP, split_axis=0, concat_axis=0...]
    ppermute x5, starting transfers between devices: 8.29 us -> 14.4 us  [the longest x1 6.85 us: body(): r_diag = lax.ppermute(d_diag, GRID, back(DIAG))]
  transfers between devices with their start and end apart: 12 -> 9, of which waited for: 8 -> 3; matrix products, arithmetic and copies ran while one was open for 7% -> 2% of each run, Pallas kernels for 0% -> 4%
where the time goes in v2:
time: 154 us
  blocking collectives  88.7 us (58%)
  starting transfers between devices  29.3 us (19%)
  waiting for transfers between devices  15.2 us (10%)
  Pallas kernels  14.3 us (9%)
  local copies, waits for them, and re-layouts  2.46 us (2%)
  other arithmetic  2.33 us (2%)
  between operations  1.58 us (1%)
    all_to_all x5, blocking collectives, a2a(): return lax.all_to_all(x, axes, split_axis=0, concat_axis=0, tiled=True)  88.7 us
    ppermute x1, waiting for transfers between devices, body(): edges_there = lax.ppermute(edge_src, GRID, SWAP)  13.3 us
    ppermute x1, starting transfers between devices, body(): diag = lax.ppermute(oth, GRID, DIAG)  11.4 us
    ppermute x1, starting transfers between devices, body(): r_diag = lax.ppermute(d_diag, GRID, back(DIAG))  6.85 us
    ppermute x1, starting transfers between devices, body(): got = lax.ppermute(part, 'c', [(0, 1), (1, 0)])  5.22 us
    pallas_call x1, Pallas kernels, forward(): call(forward_kernel, 'forward', flops=2 * m * H * (2 * H + LANES), nbytes...  3.55 us
    pallas_call x1, Pallas kernels, latent_grads(): call(latent_kernel, 'latent_grads', flops=4 * m * H * H, nbytes=8 * 2 **...  3.18 us
  transfers between devices with their start and end apart: 9, of which 3 were waited for; matrix products, arithmetic and copies ran while one was open for 2% of the time, Pallas kernels for 4%

profile of v2, /device:TPU:1, one launch (start us, length us, event | category | flops | bytes accessed | tf_op | source)
XLA Modules:
  0.0 153.9 jit_solution(4072914082741644847)
XLA Ops:
  0.7 1.4 dynamic-slice_bitcast_fusion
  2.1 11.4 %collective-permute-start.3 = (bf16[256,1024]{1,0:T(8,128)(2,1)S(1)}, bf16[256,1024]{1,0:T(8,128)(2,1)S(1)}, u32[]{:S(2)}, u32[]{:S(2)}) collective-permute-start(bf16[256,1024]{1,0:T(8,128)(2,1)S(1)} %get-tuple-element.73), channel_id=1, source_target_pairs={{0,63},{1,2},{2,1},{3,4},{4,3},{5,6},{6,5},{7,8},{8,7},{9,10},{10,... | collective-permute-start | bytes 1572872 | tf_op jit(solution)/shard_map/ppermute | solution.py:399
  13.5 3.0 %collective-permute-start = (s32[256,3]{0,1:T(4,128)S(1)}, s32[256,3]{0,1:T(4,128)S(1)}, u32[]{:S(2)}, u32[]{:S(2)}) collective-permute-start(s32[256,3]{0,1:T(4,128)S(1)} %copy-done.4), channel_id=1, source_target_pairs={{0,1},{1,0},{2,3},{3,2},{4,5},{5,4},{6,7},{7,6},{8,9},{9,8},{10,11... | collective-permute-start | bytes 9224 | tf_op jit(solution)/shard_map/ppermute | solution.py:397
  17.6 0.7 compare_select_fusion
  18.8 13.3 %collective-permute-done = s32[256,3]{0,1:T(4,128)S(1)} collective-permute-done((s32[256,3]{0,1:T(4,128)S(1)}, s32[256,3]{0,1:T(4,128)S(1)}, u32[]{:S(2)}, u32[]{:S(2)}) %collective-permute-start) | collective-permute-done | bytes 3104 | tf_op jit(solution)/shard_map/ppermute | solution.py:397
  32.1 0.8 add_convert_fusion.pick_t
  33.0 0.7 add_convert_fusion.1.pick
  33.7 1.7 %collective-permute-done.2.same = bf16[256,1024]{1,0:T(8,128)(2,1)S(1)} collective-permute-done((bf16[256,1024]{1,0:T(8,128)(2,1)S(1)}, bf16[256,1024]{1,0:T(8,128)(2,1)S(1)}, u32[]{:S(2)}, u32[]{:S(2)}) %collective-permute-start.2) | collective-permute-done | bytes 524320 | tf_op jit(solution)/shard_map/ppermute | solution.py:400
  35.4 3.6 %forward.1 = (bf16[1024,512]{1,0:T(8,128)(2,1)S(1)}, bf16[512,1024]{1,0:T(8,128)(2,1)S(1)}, bf16[512,1024]{1,0:T(8,128)(2,1)S(1)}, f32[8,64,128]{2,1,0:T(8,128)S(1)}) custom-call(bf16[512,1024]{1,0:T(8,128)(2,1)S(1)} %add_convert_fusion.1.pick, bf16[256,1024]{1,0:T(8,128)(2,1)S(1)} %get-tuple-element.74.own, ...), custom_call_target="tpu_custom_call" | custom-call | flops 2281701376 | bytes 12582912 | tf_op jit(solution)/shard_map/forward/pallas_call | solution.py:97
  38.9 10.4 %all_to_all.25.pred = f32[8,64,128]{2,1,0:T(8,128)S(1)} all-to-all(f32[8,64,128]{2,1,0:T(8,128)S(1)} %get-tuple-element.43), channel_id=1, replica_groups=mesh['xl'=2,'c'=2,'z'=8,'y'=4,'xh'=2] {'xh','xl','c'}, dimensions={0} | all-to-all | bytes 524288 | tf_op jit(solution)/shard_map/all_to_all | solution.py:71
  49.8 8.8 %all_to_all.26 = bf16[8,64,128]{2,1,0:T(8,128)(2,1)S(1)} all-to-all(bf16[8,64,128]{2,1,0:T(8,128)(2,1)S(1)} %get-tuple-element.46), channel_id=1, replica_groups=mesh['xl'=2,'c'=2,'z'=8,'y'=4,'xh'=2] {'xh','xl','c'}, dimensions={0} | all-to-all | bytes 262144 | tf_op jit(solution)/shard_map/all_to_all | solution.py:71
  58.7 1.2 backward.1
  59.8 1.1 collective-permute-start.4
  61.0 3.2 %latent_grads.1 = (f32[256,1024]{1,0:T(8,128)S(1)}, bf16[256,1024]{1,0:T(8,128)(2,1)}, bf16[256,1024]{1,0:T(8,128)(2,1)}, bf16[256,1024]{1,0:T(8,128)(2,1)}) custom-call(bf16[512,1024]{1,0:T(8,128)(2,1)S(1)} %get-tuple-element.52.dpre, bf16[1024,1024]{1,0:T(8,128)(2,1)S(1)} %copy-done.1, bf16[1024,512]{1,0:T(8,128)(2,1)S(1)} %add_convert_fusion.pick_t), custom_call_target="tpu_custom_call" | custom-call | flops 2147483648 | bytes 8388608 | tf_op jit(solution)/shard_map/latent_grads/pallas_call | solution.py:218
  64.2 0.8 pair_sum.1
  65.0 21.2 %all_to_all.27.parts = bf16[16,288,128]{2,1,0:T(8,128)(2,1)S(1)} all-to-all(bf16[16,288,128]{2,1,0:T(8,128)(2,1)S(1)} %pair_sum.1), channel_id=1, replica_groups=mesh['xl'=2,'c'=2,'z'=8,'y'=4,'xh'=2] {'y','xh','xl'}, dimensions={0} | all-to-all | bytes 2359296 | tf_op jit(solution)/shard_map/all_to_all | solution.py:71
  86.2 1.2 collective-permute-start.5
  87.4 6.8 %collective-permute-start.7 = (bf16[256,1024]{1,0:T(8,128)(2,1)}, bf16[256,1024]{1,0:T(8,128)(2,1)}, u32[]{:S(2)}, u32[]{:S(2)}) collective-permute-start(bf16[256,1024]{1,0:T(8,128)(2,1)} %get-tuple-element.63), channel_id=1, source_target_pairs={{63,0},{2,1},{1,2},{4,3},{3,4},{6,5},{5,6},{8,7},{7,8},{10,9},{9,1... | collective-permute-start | bytes 1572872 | tf_op jit(solution)/shard_map/ppermute | solution.py:446
  95.1 24.8 %conditional.1 = (bf16[8,288,128]{2,1,0:T(8,128)(2,1)S(1)}) conditional(s32[]{:T(128)} %bitcast.12, bf16[8,288,128]{2,1,0:T(8,128)(2,1)S(1)} %total.2, bf16[8,288,128]{2,1,0:T(8,128)(2,1)S(1)} %total.2), branch_computations={%region_0.1_spmd, %region_1.2_spmd} | conditional | bytes 2359304 | solution.py:448
  95.2 24.8 %all_to_all.24 = bf16[8,288,128]{2,1,0:T(8,128)(2,1)S(1)} all-to-all(bf16[8,288,128]{2,1,0:T(8,128)(2,1)S(1)} %copy.21), channel_id=1, replica_groups=mesh['xl'=2,'c'=2,'z'=8,'y'=4,'xh'=2] {'z'}, dimensions={0} | all-to-all | bytes 1179648 | tf_op jit(solution)/shard_map/cond/branch_1_fun/all_to_all | solution.py:71
  120.0 23.5 %all_to_all.28.mine = bf16[16,288,128]{2,1,0:T(8,128)(2,1)S(1)} all-to-all(bf16[16,288,128]{2,1,0:T(8,128)(2,1)S(1)} %total.3), channel_id=1, replica_groups=mesh['xl'=2,'c'=2,'z'=8,'y'=4,'xh'=2] {'y','xh','xl'}, dimensions={0} | all-to-all | bytes 2359296 | tf_op jit(solution)/shard_map/all_to_all | solution.py:71
  143.5 5.2 %collective-permute-start.8 = (bf16[16,288,128]{2,1,0:T(8,128)(2,1)S(1)}, bf16[16,288,128]{2,1,0:T(8,128)(2,1)S(1)}, u32[]{:S(2)}, u32[]{:S(2)}) collective-permute-start(bf16[16,288,128]{2,1,0:T(8,128)(2,1)S(1)} %all_to_all.28.mine), channel_id=1, source_target_pairs={{0,64},{64,0},{1,65},{65,1},{2,66},{66,2},{3,67},{67,3},{4,68},{68... | collective-permute-start | bytes 3538952 | tf_op jit(solution)/shard_map/ppermute | solution.py:452
  148.7 2.3 %final_latents.1 = bf16[2,256,1024]{2,1,0:T(8,128)(2,1)} custom-call(s32[1]{0:T(128)} %bitcast.side, f32[256,1024]{1,0:T(8,128)S(1)} %get-tuple-element.55.own, bf16[256,1024]{1,0:T(8,128)(2,1)} %collective-permute-done.6.same, bf16[256,1024]{1,0:T(8,128)(2,1)S(1)} %collective-permute-done.5.swp, bf16[256,1024]{1,0:T(8,128)(2,1)} %collective-permute-done.7.diag), custom_call_target="tpu_custom_call" | custom-call | bytes 5242880 | tf_op jit(solution)/shard_map/final_latents/pallas_call | solution.py:364
  151.2 2.6 %unpack.1 = (f32[1024,1024]{1,0:T(8,128)}, f32[100,1024]{1,0:T(8,128)}, f32[1,1024]{1,0:T(1,128)}, f32[1,100]{1,0:T(1,128)}, f32[1,1]{1,0:T(1,128)}) custom-call(s32[1]{0:T(128)} %bitcast.1.core, bf16[16,288,128]{2,1,0:T(8,128)(2,1)S(1)} %all_to_all.28.mine, bf16[16,288,128]{2,1,0:T(8,128)(2,1)S(1)} %collective-permute-done.8.got), custom_call_target="tpu_custom_call" | custom-call | bytes 8388608 | tf_op jit(solution)/shard_map/unpack/pallas_call | solution.py:319
  (43 shorter events, 2.6 us)
Async XLA Ops:
  0.6 16.9 %copy-start = (f32[100,256]{1,0:T(8,128)S(1)}, f32[100,256]{1,0:T(8,128)}, u32[]{:S(2)}) copy-start(f32[100,256]{1,0:T(8,128)} %param.15) | copy-start | bytes 307204
  0.6 12.9 %copy-start.4 = (s32[256,3]{0,1:T(4,128)S(1)}, s32[256,3]{0,1:T(4,128)}, u32[]{:S(2)}) copy-start(s32[256,3]{0,1:T(4,128)} %param.13) | copy-start | bytes 9220
  0.7 16.3 %copy-start.7 = (f32[100]{0:T(128)S(1)}, f32[100]{0:T(128)}, u32[]{:S(2)}) copy-start(f32[100]{0:T(128)} %param.17) | copy-start | bytes 1204
  0.7 16.3 %copy-start.5 = (s32[64]{0:T(128)S(1)}, s32[64]{0:T(128)}, u32[]{:S(2)}) copy-start(s32[64]{0:T(128)} %param.14) | copy-start | bytes 772
  0.7 17.0 %copy-start.6 = (f32[256]{0:T(256)S(1)}, f32[256]{0:T(256)}, u32[]{:S(2)}) copy-start(f32[256]{0:T(256)} %param.16) | copy-start | bytes 3076
  0.7 17.8 %copy-start.8 = (f32[100]{0:T(128)S(1)}, f32[100]{0:T(128)}, u32[]{:S(2)}) copy-start(f32[100]{0:T(128)} %param.21) | copy-start | bytes 1204
  0.7 17.9 %copy-start.3 = (bf16[1024,100]{0,1:T(8,128)(2,1)S(1)}, bf16[1024,100]{0,1:T(8,128)(2,1)}, u32[]{:S(2)}) copy-start(bf16[1024,100]{0,1:T(8,128)(2,1)} %param.20) | copy-start | bytes 614404
  2.1 33.3 %copy-start.2 = (f32[1024]{0:T(1024)S(1)}, f32[1024]{0:T(1024)}, u32[]{:S(2)}) copy-start(f32[1024]{0:T(1024)} %param.19) | copy-start | bytes 12292
  2.1 31.5 %collective-permute-start.3 = (bf16[256,1024]{1,0:T(8,128)(2,1)S(1)}, bf16[256,1024]{1,0:T(8,128)(2,1)S(1)}, u32[]{:S(2)}, u32[]{:S(2)}) collective-permute-start(bf16[256,1024]{1,0:T(8,128)(2,1)S(1)} %get-tuple-element.73), channel_id=1, source_target_pairs={{0,63},{1,2},{2,1},{3,4},{4,3},{5,6},{6,5},{7,8},{8,7},{9,10},{10,... | collective-permute-start | bytes 1572872 | tf_op jit(solution)/shard_map/ppermute | solution.py:399
  13.5 20.1 %collective-permute-start.1 = (bf16[256,1024]{1,0:T(8,128)(2,1)S(1)}, bf16[256,1024]{1,0:T(8,128)(2,1)S(1)}, u32[]{:S(2)}, u32[]{:S(2)}) collective-permute-start(bf16[256,1024]{1,0:T(8,128)(2,1)S(1)} %get-tuple-element.73), channel_id=1, source_target_pairs={{0,1},{1,0},{2,3},{3,2},{4,5},{5,4},{6,7},{7,6},{8,9},{9,8},{10,11... | collective-permute-start | bytes 1572872 | tf_op jit(solution)/shard_map/ppermute | solution.py:398
  13.5 18.6 %collective-permute-start = (s32[256,3]{0,1:T(4,128)S(1)}, s32[256,3]{0,1:T(4,128)S(1)}, u32[]{:S(2)}, u32[]{:S(2)}) collective-permute-start(s32[256,3]{0,1:T(4,128)S(1)} %copy-done.4), channel_id=1, source_target_pairs={{0,1},{1,0},{2,3},{3,2},{4,5},{5,4},{6,7},{7,6},{8,9},{9,8},{10,11... | collective-permute-start | bytes 9224 | tf_op jit(solution)/shard_map/ppermute | solution.py:397
  16.5 18.9 %collective-permute-start.2 = (bf16[256,1024]{1,0:T(8,128)(2,1)S(1)}, bf16[256,1024]{1,0:T(8,128)(2,1)S(1)}, u32[]{:S(2)}, u32[]{:S(2)}) collective-permute-start(bf16[256,1024]{1,0:T(8,128)(2,1)S(1)} %get-tuple-element.74.own), channel_id=1, source_target_pairs={{0,62},{1,3},{2,0},{3,5},{4,2},{5,7},{6,4},{7,9},{8,6},{9,11},{10,... | collective-permute-start | bytes 1572872 | tf_op jit(solution)/shard_map/ppermute | solution.py:400
  49.4 11.6 %copy-start.1 = (bf16[1024,1024]{1,0:T(8,128)(2,1)S(1)}, bf16[1024,1024]{1,0:T(8,128)(2,1)}, u32[]{:S(2)}) copy-start(bf16[1024,1024]{1,0:T(8,128)(2,1)} %w_in.3) | copy-start | bytes 6291460
  59.8 4.3 %collective-permute-start.4 = (bf16[16,288,128]{2,1,0:T(8,128)(2,1)S(1)}, bf16[16,288,128]{2,1,0:T(8,128)(2,1)S(1)}, u32[]{:S(2)}, u32[]{:S(2)}) collective-permute-start(bf16[16,288,128]{2,1,0:T(8,128)(2,1)S(1)} %get-tuple-element.51), channel_id=1, source_target_pairs={{0,64},{64,0},{1,65},{65,1},{2,66},{66,2},{3,67},{67,3},{4,68},{68... | collective-permute-start | bytes 3538952 | tf_op jit(solution)/shard_map/ppermute | solution.py:438
  86.2 33.7 %collective-permute-start.5 = (bf16[256,1024]{1,0:T(8,128)(2,1)}, bf16[256,1024]{1,0:T(8,128)(2,1)S(1)}, u32[]{:S(2)}, u32[]{:S(2)}) collective-permute-start(bf16[256,1024]{1,0:T(8,128)(2,1)} %get-tuple-element.61), channel_id=1, source_target_pairs={{1,0},{0,1},{3,2},{2,3},{5,4},{4,5},{7,6},{6,7},{9,8},{8,9},{11,10... | collective-permute-start | bytes 1572872 | tf_op jit(solution)/shard_map/ppermute | solution.py:444
  87.4 32.5 %collective-permute-start.6 = (bf16[256,1024]{1,0:T(8,128)(2,1)}, bf16[256,1024]{1,0:T(8,128)(2,1)}, u32[]{:S(2)}, u32[]{:S(2)}) collective-permute-start(bf16[256,1024]{1,0:T(8,128)(2,1)} %get-tuple-element.62), channel_id=1, source_target_pairs={{62,0},{3,1},{0,2},{5,3},{2,4},{7,5},{4,6},{9,7},{6,8},{11,9},{8,1... | collective-permute-start | bytes 1572872 | tf_op jit(solution)/shard_map/ppermute | solution.py:445
  87.4 32.5 %collective-permute-start.7 = (bf16[256,1024]{1,0:T(8,128)(2,1)}, bf16[256,1024]{1,0:T(8,128)(2,1)}, u32[]{:S(2)}, u32[]{:S(2)}) collective-permute-start(bf16[256,1024]{1,0:T(8,128)(2,1)} %get-tuple-element.63), channel_id=1, source_target_pairs={{63,0},{2,1},{1,2},{4,3},{3,4},{6,5},{5,6},{8,7},{7,8},{10,9},{9,1... | collective-permute-start | bytes 1572872 | tf_op jit(solution)/shard_map/ppermute | solution.py:446
  143.5 7.7 %collective-permute-start.8 = (bf16[16,288,128]{2,1,0:T(8,128)(2,1)S(1)}, bf16[16,288,128]{2,1,0:T(8,128)(2,1)S(1)}, u32[]{:S(2)}, u32[]{:S(2)}) collective-permute-start(bf16[16,288,128]{2,1,0:T(8,128)(2,1)S(1)} %all_to_all.28.mine), channel_id=1, source_target_pairs={{0,64},{64,0},{1,65},{65,1},{2,66},{66,2},{3,67},{67,3},{4,68},{68... | collective-permute-start | bytes 3538952 | tf_op jit(solution)/shard_map/ppermute | solution.py:452

commit v3 on v2

--- a/solution.py
+++ b/solution.py
@@ -42,7 +42,11 @@
 
 
 def near(*xs):
-    return [pltpu.with_memory_space_constraint(x, pltpu.VMEM) for x in xs]
+    return list(xs)
+
+
+def pinned(x):
+    return pltpu.with_memory_space_constraint(x, pltpu.VMEM)
 
 
 def far(x):
@@ -50,7 +54,7 @@
 
 
 def out(shape, dtype):
-    return pltpu.VMEM(shape, dtype)
+    return jax.ShapeDtypeStruct(shape, dtype)
 
 
 def ring(shift_odd, shift_even):
@@ -65,6 +69,18 @@
 
 def back(perm):
     return [(b, a) for a, b in perm]
+
+
+def at(z, y, h):
+    return (z % 8 * 4 + y % 4) * 2 + h
+
+
+PLACES = [(z, y, h) for z in range(8) for y in range(4) for h in range(2)]
+BACK_SAME = [(at(z, y, h), at(z, y - 1 if h else y + 1, h)) for z, y, h in PLACES]
+BACK_DIAG = [(at(z, y, h), at(z, y + 1 if h else y - 1, 1 - h)) for z, y, h in PLACES]
+CARRY = [
+    (at(z, y, h), at(z + 1 if y else z - 1, y, h)) for z, y, h in PLACES if y in (0, 3)
+]
 
 
 def a2a(x, axes):
@@ -275,7 +291,7 @@
             pl.BlockSpec(memory_space=pltpu.VMEM),
         ],
         out_shape=jax.ShapeDtypeStruct((copies, PART, LANES), bf16),
-    )(group, *near(parts))
+    )(group, pinned(parts))
 
 
 def unpack_kernel(core, mine, got, gw_in, gw_out_t, gb_in, gb_out, loss):
@@ -342,7 +358,7 @@
             jax.ShapeDtypeStruct((1, GB_IN), f32),
             jax.ShapeDtypeStruct((1, 1), f32),
         ],
-    )(core, mine, got)
+    )(core, pinned(mine), pinned(got))
 
 
 def final_kernel(side, own, same, swp, diag, both):
@@ -439,16 +455,25 @@
     d_own, d_swap, d_same, d_diag = latent_grads(dpre, w_in, pick_t)
     got, d_own = lax.optimization_barrier((got, d_own))
     part = pair_sum(core, dpred, dpre, hidden, feats_t, small, got)
+    y = lax.axis_index("y")
+    up, down = jnp.logical_and(y == 3, h == 0), jnp.logical_and(y == 0, h == 1)
+    same_crosses = jnp.logical_or(up, down)
+    up, down = jnp.logical_and(y == 3, h == 1), jnp.logical_and(y == 0, h == 0)
+    diag_crosses = jnp.logical_or(up, down)
+    crossed = lax.ppermute(jnp.where(same_crosses, d_same, d_diag), GRID, CARRY)
+    d_same = jnp.where(same_crosses, crossed, d_same)
+    d_diag = jnp.where(diag_crosses, crossed, d_diag)
     part = a2a(part, PLANE)
     part, d_swap, d_same, d_diag = lax.optimization_barrier((part, d_swap, d_same, d_diag))
     r_swap = lax.ppermute(d_swap, GRID, back(SWAP))
-    r_same = lax.ppermute(d_same, GRID, back(SAME))
-    r_diag = lax.ppermute(d_diag, GRID, back(DIAG))
-    part = total_and_spread(group, part, 8)
-    part = lax.cond(counts[0] >= 0, lambda x: a2a(x, "z"), lambda x: x, part)
+    r_same = lax.ppermute(d_same, GRID, BACK_SAME)
+    r_diag = lax.ppermute(d_diag, GRID, BACK_DIAG)
+    def planes(x):
+        x = a2a(total_and_spread(group, x, 8), "z")
+        return a2a(total_and_spread(group, x, PARTS), PLANE)
+
+    part = lax.cond(counts[0] >= 0, planes, lambda x: x, part)
     part, r_swap, r_same, r_diag = lax.optimization_barrier((part, r_swap, r_same, r_diag))
-    part = total_and_spread(group, part, PARTS)
-    part = a2a(part, PLANE)
     got = lax.ppermute(part, "c", [(0, 1), (1, 0)])
     grad_latent = final_latents(side, d_own, r_same, r_swap, r_diag)
     gw_in, gw_out_t, gb_in, gb_out, loss = unpack(core, part, got)

time: 154 us -> 151 us (0.981)
  blocking collectives: 88.7 us -> 60.6 us
  waiting for transfers between devices: 15.2 us -> 30.7 us
  starting transfers between devices: 29.3 us -> 32.4 us
  other arithmetic: 2.33 us -> 5.31 us
  local copies, waits for them, and re-layouts: 2.46 us -> 5.07 us
    all_to_all x5 -> x4, blocking collectives: 88.7 us -> 60.6 us  [a2a(): return lax.all_to_all(x, axes, split_axis=0, concat_axis=0, tiled=True)]
    ppermute x2 -> x3, waiting for transfers between devices: 0.01 us -> 11.3 us  [the longest x1 11.3 us: body(): crossed = lax.ppermute(jnp.where(same_crosses, d_same, d_diag), GRID, CARRY)]
    ppermute x1, waiting for transfers between devices: 1.71 us -> 6.04 us  [body(): same = lax.ppermute(own, GRID, SAME)]
    all_to_all x0 -> x1, starting transfers between devices: none -> 3.7 us  [a2a(): return lax.all_to_all(x, axes, split_axis=0, concat_axis=0, tiled=True)]
    ppermute x1, starting transfers between devices: 0.01 us -> 3.66 us  [body(): swapped = lax.ppermute(oth, GRID, SWAP)]
    ppermute x1, starting transfers between devices: 11.4 us -> 7.97 us  [body(): diag = lax.ppermute(oth, GRID, DIAG)]
    select_n x0 -> x2, other arithmetic: none -> 2.98 us  [the longest x1 2.13 us: body(): d_diag = jnp.where(diag_crosses, crossed, d_diag)]
    ppermute x1, starting transfers between devices: 2.97 us -> 0.01 us  [body(): edges_there = lax.ppermute(edge_src, GRID, SWAP)]
  transfers between devices with their start and end apart: 9 -> 11, of which waited for: 3 -> 5; matrix products, arithmetic and copies ran while one was open for 2% -> 4% of each run, Pallas kernels for 4% -> 3%
where the time goes in v3:
time: 151 us; the launch traced here: 150 us
  blocking collectives  60.6 us (40%)
  starting transfers between devices  32.4 us (21%)
  waiting for transfers between devices  30.7 us (20%)
  Pallas kernels  14.4 us (10%)
  other arithmetic  5.31 us (4%)
  local copies, waits for them, and re-layouts  5.07 us (3%)
  between operations  1.63 us (1%)
    all_to_all x4, blocking collectives, a2a(): return lax.all_to_all(x, axes, split_axis=0, concat_axis=0, tiled=True)  60.6 us
    ppermute x1, waiting for transfers between devices, body(): edges_there = lax.ppermute(edge_src, GRID, SWAP)  11.6 us
    ppermute x1, waiting for transfers between devices, body(): crossed = lax.ppermute(jnp.where(same_crosses, d_same, d_diag), GRID, CARRY)  11.3 us
    ppermute x1, starting transfers between devices, body(): diag = lax.ppermute(oth, GRID, DIAG)  7.97 us
    ppermute x1, waiting for transfers between devices, body(): same = lax.ppermute(own, GRID, SAME)  6.04 us
    ppermute x1, starting transfers between devices, body(): crossed = lax.ppermute(jnp.where(same_crosses, d_same, d_diag), GRID, CARRY)  5.53 us
    ppermute x1, starting transfers between devices, body(): got = lax.ppermute(part, 'c', [(0, 1), (1, 0)])  5.34 us
    all_to_all x1, starting transfers between devices, a2a(): return lax.all_to_all(x, axes, split_axis=0, concat_axis=0, tiled=True)  3.7 us
  transfers between devices with their start and end apart: 11, of which 5 were waited for; matrix products, arithmetic and copies ran while one was open for 4% of the time, Pallas kernels for 3%

profile of v3, /device:TPU:1, one launch (start us, length us, event | category | flops | bytes accessed | tf_op | source)
XLA Modules:
  0.0 150.0 jit_solution(17411788883538133336)
XLA Ops:
  0.7 1.4 dynamic-slice_bitcast_fusion
  2.1 3.7 %collective-permute-start.1 = (bf16[256,1024]{1,0:T(8,128)(2,1)S(1)}, bf16[256,1024]{1,0:T(8,128)(2,1)S(1)}, u32[]{:S(2)}, u32[]{:S(2)}) collective-permute-start(bf16[256,1024]{1,0:T(8,128)(2,1)S(1)} %get-tuple-element.103), channel_id=1, source_target_pairs={{0,1},{1,0},{2,3},{3,2},{4,5},{5,4},{6,7},{7,6},{8,9},{9,8},{10,11... | collective-permute-start | bytes 1572872 | tf_op jit(solution)/shard_map/ppermute | solution.py:414
  5.8 8.0 %collective-permute-start.3 = (bf16[256,1024]{1,0:T(8,128)(2,1)S(1)}, bf16[256,1024]{1,0:T(8,128)(2,1)S(1)}, u32[]{:S(2)}, u32[]{:S(2)}) collective-permute-start(bf16[256,1024]{1,0:T(8,128)(2,1)S(1)} %get-tuple-element.103), channel_id=1, source_target_pairs={{0,63},{1,2},{2,1},{3,4},{4,3},{5,6},{6,5},{7,8},{8,7},{9,10},{10,... | collective-permute-start | bytes 1572872 | tf_op jit(solution)/shard_map/ppermute | solution.py:415
  16.1 11.6 %collective-permute-done = s32[256,3]{0,1:T(4,128)S(1)} collective-permute-done((s32[256,3]{0,1:T(4,128)S(1)}, s32[256,3]{0,1:T(4,128)S(1)}, u32[]{:S(2)}, u32[]{:S(2)}) %collective-permute-start) | collective-permute-done | bytes 3104 | tf_op jit(solution)/shard_map/ppermute | solution.py:413
  29.3 6.0 %collective-permute-done.2.same = bf16[256,1024]{1,0:T(8,128)(2,1)S(1)} collective-permute-done((bf16[256,1024]{1,0:T(8,128)(2,1)S(1)}, bf16[256,1024]{1,0:T(8,128)(2,1)S(1)}, u32[]{:S(2)}, u32[]{:S(2)}) %collective-permute-start.2) | collective-permute-done | bytes 524320 | tf_op jit(solution)/shard_map/ppermute | solution.py:416
  37.2 3.6 %forward.1 = (bf16[1024,512]{1,0:T(8,128)(2,1)S(1)}, bf16[512,1024]{1,0:T(8,128)(2,1)S(1)}, bf16[512,1024]{1,0:T(8,128)(2,1)S(1)}, f32[8,64,128]{2,1,0:T(8,128)S(1)}) custom-call(bf16[512,1024]{1,0:T(8,128)(2,1)S(1)} %add_convert_fusion.1.pick, bf16[256,1024]{1,0:T(8,128)(2,1)S(1)} %get-tuple-element.104.own, ...), custom_call_target="tpu_custom_call" | custom-call | flops 2281701376 | bytes 12582912 | tf_op jit(solution)/shard_map/forward/pallas_call | solution.py:113
  40.7 11.4 %all_to_all.25.pred = f32[8,64,128]{2,1,0:T(8,128)S(1)} all-to-all(f32[8,64,128]{2,1,0:T(8,128)S(1)} %get-tuple-element.73), channel_id=1, replica_groups=mesh['xl'=2,'c'=2,'z'=8,'y'=4,'xh'=2] {'xh','xl','c'}, dimensions={0} | all-to-all | bytes 524288 | tf_op jit(solution)/shard_map/all_to_all | solution.py:87
  52.6 8.8 %all_to_all.26 = bf16[8,64,128]{2,1,0:T(8,128)(2,1)S(1)} all-to-all(bf16[8,64,128]{2,1,0:T(8,128)(2,1)S(1)} %get-tuple-element.76), channel_id=1, replica_groups=mesh['xl'=2,'c'=2,'z'=8,'y'=4,'xh'=2] {'xh','xl','c'}, dimensions={0} | all-to-all | bytes 262144 | tf_op jit(solution)/shard_map/all_to_all | solution.py:87
  61.4 1.2 backward.1
  63.7 2.4 %latent_grads.1 = (f32[256,1024]{1,0:T(8,128)S(1)}, bf16[256,1024]{1,0:T(8,128)(2,1)S(1)}, bf16[256,1024]{1,0:T(8,128)(2,1)S(1)}, bf16[256,1024]{1,0:T(8,128)(2,1)S(1)}) custom-call(bf16[512,1024]{1,0:T(8,128)(2,1)S(1)} %get-tuple-element.82.dpre, bf16[1024,1024]{1,0:T(8,128)(2,1)S(1)} %copy-done.1, bf16[1024,512]{1,0:T(8,128)(2,1)S(1)} %add_convert_fusion.pick_t), custom_call_target="tpu_custom_call" | custom-call | flops 2147483648 | bytes 8388608 | tf_op jit(solution)/shard_map/latent_grads/pallas_call | solution.py:234
  66.9 1.8 %pair_sum.1 = bf16[16,288,128]{2,1,0:T(8,128)(2,1)} custom-call(s32[1]{0:T(128)} %bitcast.2.core, bf16[512,128]{1,0:T(8,128)(2,1)S(1)} %bitcast.22, bf16[512,1024]{1,0:T(8,128)(2,1)S(1)} %get-tuple-element.82.dpre, bf16[512,1024]{1,0:T(8,128)(2,1)S(1)} %get-tuple-element.78.hid, bf16[1024,512]{1,0:T(8,128)(2,1)S(1)} %get-tuple-element.79.feats_t, ...), custom_call_target="tpu_custom_call" | custom-call | flops 671088640 | bytes 6291456 | tf_op jit(solution)/shard_map/pair_sum/pallas_call | solution.py:261
  68.7 3.7 %all-to-all-start.4 = ((bf16[16,288,128]{2,1,0:T(8,128)(2,1)}), bf16[16,288,128]{2,1,0:T(8,128)(2,1)S(1)}, u32[]{:S(2)}, u32[]{:S(2)}) async-start(bf16[16,288,128]{2,1,0:T(8,128)(2,1)} %pair_sum.1), calls=%async_computation.4 | async-start | bytes 2359296 | tf_op jit(solution)/shard_map/all_to_all | solution.py:87
  73.3 5.5 %collective-permute-start.5 = (bf16[256,1024]{1,0:T(8,128)(2,1)}, bf16[256,1024]{1,0:T(8,128)(2,1)}, u32[]{:S(2)}, u32[]{:S(2)}) collective-permute-start(bf16[256,1024]{1,0:T(8,128)(2,1)} %broadcast_select_fusion.2), channel_id=1, source_target_pairs={{0,56},{1,57},{6,14},{7,15},{8,0},{9,1},{14,22},{15,23},{16,8},{17... | collective-permute-start | bytes 1572872 | tf_op jit(solution)/shard_map/ppermute | solution.py:463
  78.8 11.3 %collective-permute-done.5 = bf16[256,1024]{1,0:T(8,128)(2,1)} collective-permute-done((bf16[256,1024]{1,0:T(8,128)(2,1)}, bf16[256,1024]{1,0:T(8,128)(2,1)}, u32[]{:S(2)}, u32[]{:S(2)}) %collective-permute-start.5) | collective-permute-done | bytes 524320 | tf_op jit(solution)/shard_map/ppermute | solution.py:463
  90.1 2.1 %broadcast_select_fusion = (bf16[256,1024]{1,0:T(8,128)(2,1)}, bf16[256,1024]{1,0:T(8,128)(2,1)}) fusion(bf16[256,1024]{1,0:T(8,128)(2,1)} %collective-permute-done.5, bf16[256,1024]{1,0:T(8,128)(2,1)S(1)} %get-tuple-element.89, pred[]{:T(512)S(6)} %or.7, bf16[256,1024]{1,0:T(8,128)(2,1)S(1)} %get-tuple-element.88, pred[]{:T(512)S(6)} %or.6), kind=kLoop, calls=%fused_computation.10 | loop fusion | flops 524288 | bytes 2621442 | tf_op jit(solution)/shard_map/jit(_where)/select_n | solution.py:465
  92.3 1.4 all-to-all-done.4
  93.6 1.2 collective-permute-start.6
  94.8 3.5 %collective-permute-start.8 = (bf16[256,1024]{1,0:T(8,128)(2,1)}, bf16[256,1024]{1,0:T(8,128)(2,1)}, u32[]{:S(2)}, u32[]{:S(2)}) collective-permute-start(bf16[256,1024]{1,0:T(8,128)(2,1)} %get-tuple-element.93), channel_id=1, source_target_pairs={{0,7},{1,2},{2,1},{3,4},{4,3},{5,6},{6,5},{7,0},{8,15},{9,10},{10,... | collective-permute-start | bytes 1572872 | tf_op jit(solution)/shard_map/ppermute | solution.py:470
  98.9 40.6 %conditional.1 = (bf16[16,288,128]{2,1,0:T(8,128)(2,1)S(1)}) conditional(s32[]{:T(128)} %bitcast.13, bf16[16,288,128]{2,1,0:T(8,128)(2,1)S(1)} %all-to-all-done.4, (s32[]{:T(128)}, s32[]{:T(128)}, s32[]{:T(128)}, bf16[16,288,128]{2,1,0:T(8,128)(2,1)S(1)}) %tuple.22), branch_computations={%region_0.1_spmd, %region_1.2_spmd} | conditional | flops 884746 | bytes 7078007 | solution.py:475
  99.1 22.4 %all_to_all.23.parts = bf16[8,288,128]{2,1,0:T(8,128)(2,1)S(1)} all-to-all(bf16[8,288,128]{2,1,0:T(8,128)(2,1)S(1)} %total.2), channel_id=1, replica_groups=mesh['xl'=2,'c'=2,'z'=8,'y'=4,'xh'=2] {'z'}, dimensions={0} | all-to-all | bytes 1179648 | tf_op jit(solution)/shard_map/cond/branch_1_fun/all_to_all | solution.py:87
  121.6 17.9 %all_to_all.24 = bf16[16,288,128]{2,1,0:T(8,128)(2,1)S(1)} all-to-all(bf16[16,288,128]{2,1,0:T(8,128)(2,1)S(1)} %total.3), channel_id=1, replica_groups=mesh['xl'=2,'c'=2,'z'=8,'y'=4,'xh'=2] {'y','xh','xl'}, dimensions={0} | all-to-all | bytes 2359296 | tf_op jit(solution)/shard_map/cond/branch_1_fun/all_to_all | solution.py:87
  139.6 5.3 %collective-permute-start.9 = (bf16[16,288,128]{2,1,0:T(8,128)(2,1)S(1)}, bf16[16,288,128]{2,1,0:T(8,128)(2,1)S(1)}, u32[]{:S(2)}, u32[]{:S(2)}) collective-permute-start(bf16[16,288,128]{2,1,0:T(8,128)(2,1)S(1)} %get-tuple-element.112.mine), channel_id=1, source_target_pairs={{0,64},{64,0},{1,65},{65,1},{2,66},{66,2},{3,67},{67,3},{4,68},{68... | collective-permute-start | bytes 3538952 | tf_op jit(solution)/shard_map/ppermute | solution.py:477
  144.9 2.1 %final_latents.1 = bf16[2,256,1024]{2,1,0:T(8,128)(2,1)} custom-call(s32[1]{0:T(128)} %bitcast.1.side, f32[256,1024]{1,0:T(8,128)S(1)} %get-tuple-element.85.own, bf16[256,1024]{1,0:T(8,128)(2,1)S(1)} %collective-permute-done.7.same, bf16[256,1024]{1,0:T(8,128)(2,1)S(1)} %collective-permute-done.6.swp, bf16[256,1024]{1,0:T(8,128)(2,1)} %collective-permute-done.8.diag), custom_call_target="tpu_custom_call" | custom-call | bytes 5242880 | tf_op jit(solution)/shard_map/final_latents/pallas_call | solution.py:380
  147.4 2.6 %unpack.1 = (f32[1024,1024]{1,0:T(8,128)}, f32[100,1024]{1,0:T(8,128)}, f32[1,1024]{1,0:T(1,128)}, f32[1,100]{1,0:T(1,128)}, f32[1,1]{1,0:T(1,128)}) custom-call(s32[1]{0:T(128)} %bitcast.2.core, bf16[16,288,128]{2,1,0:T(8,128)(2,1)S(1)} %get-tuple-element.112.mine, bf16[16,288,128]{2,1,0:T(8,128)(2,1)S(1)} %collective-permute-done.9.got), custom_call_target="tpu_custom_call" | custom-call | bytes 8388608 | tf_op jit(solution)/shard_map/unpack/pallas_call | solution.py:335
  (53 shorter events, 9.5 us)
Async XLA Ops:
  0.6 13.6 %copy-start = (f32[100,256]{1,0:T(8,128)S(1)}, f32[100,256]{1,0:T(8,128)}, u32[]{:S(2)}) copy-start(f32[100,256]{1,0:T(8,128)} %param.15) | copy-start | bytes 307204
  0.6 13.1 %copy-start.7 = (s32[256,3]{0,1:T(4,128)S(1)}, s32[256,3]{0,1:T(4,128)}, u32[]{:S(2)}) copy-start(s32[256,3]{0,1:T(4,128)} %param.13) | copy-start | bytes 9220
  0.7 13.7 %copy-start.10 = (f32[100]{0:T(128)S(1)}, f32[100]{0:T(128)}, u32[]{:S(2)}) copy-start(f32[100]{0:T(128)} %param.17) | copy-start | bytes 1204
  0.7 13.7 %copy-start.8 = (s32[64]{0:T(128)S(1)}, s32[64]{0:T(128)}, u32[]{:S(2)}) copy-start(s32[64]{0:T(128)} %param.14) | copy-start | bytes 772
  0.7 14.3 %copy-start.9 = (f32[256]{0:T(256)S(1)}, f32[256]{0:T(256)}, u32[]{:S(2)}) copy-start(f32[256]{0:T(256)} %param.16) | copy-start | bytes 3076
  0.7 15.0 %copy-start.11 = (f32[100]{0:T(128)S(1)}, f32[100]{0:T(128)}, u32[]{:S(2)}) copy-start(f32[100]{0:T(128)} %param.21) | copy-start | bytes 1204
  0.7 15.2 %copy-start.6 = (bf16[1024,100]{0,1:T(8,128)(2,1)S(1)}, bf16[1024,100]{0,1:T(8,128)(2,1)}, u32[]{:S(2)}) copy-start(bf16[1024,100]{0,1:T(8,128)(2,1)} %param.20) | copy-start | bytes 614404
  2.1 34.0 %copy-start.5 = (f32[1024]{0:T(1024)S(1)}, f32[1024]{0:T(1024)}, u32[]{:S(2)}) copy-start(f32[1024]{0:T(1024)} %param.19) | copy-start | bytes 12292
  2.1 27.1 %collective-permute-start.1 = (bf16[256,1024]{1,0:T(8,128)(2,1)S(1)}, bf16[256,1024]{1,0:T(8,128)(2,1)S(1)}, u32[]{:S(2)}, u32[]{:S(2)}) collective-permute-start(bf16[256,1024]{1,0:T(8,128)(2,1)S(1)} %get-tuple-element.103), channel_id=1, source_target_pairs={{0,1},{1,0},{2,3},{3,2},{4,5},{5,4},{6,7},{7,6},{8,9},{9,8},{10,11... | collective-permute-start | bytes 1572872 | tf_op jit(solution)/shard_map/ppermute | solution.py:414
  5.8 30.3 %collective-permute-start.3 = (bf16[256,1024]{1,0:T(8,128)(2,1)S(1)}, bf16[256,1024]{1,0:T(8,128)(2,1)S(1)}, u32[]{:S(2)}, u32[]{:S(2)}) collective-permute-start(bf16[256,1024]{1,0:T(8,128)(2,1)S(1)} %get-tuple-element.103), channel_id=1, source_target_pairs={{0,63},{1,2},{2,1},{3,4},{4,3},{5,6},{6,5},{7,8},{8,7},{9,10},{10,... | collective-permute-start | bytes 1572872 | tf_op jit(solution)/shard_map/ppermute | solution.py:415
  13.8 13.9 %collective-permute-start = (s32[256,3]{0,1:T(4,128)S(1)}, s32[256,3]{0,1:T(4,128)S(1)}, u32[]{:S(2)}, u32[]{:S(2)}) collective-permute-start(s32[256,3]{0,1:T(4,128)S(1)} %copy-done.7), channel_id=1, source_target_pairs={{0,1},{1,0},{2,3},{3,2},{4,5},{5,4},{6,7},{7,6},{8,9},{9,8},{10,11... | collective-permute-start | bytes 9224 | tf_op jit(solution)/shard_map/ppermute | solution.py:413
  13.8 21.5 %collective-permute-start.2 = (bf16[256,1024]{1,0:T(8,128)(2,1)S(1)}, bf16[256,1024]{1,0:T(8,128)(2,1)S(1)}, u32[]{:S(2)}, u32[]{:S(2)}) collective-permute-start(bf16[256,1024]{1,0:T(8,128)(2,1)S(1)} %get-tuple-element.104.own), channel_id=1, source_target_pairs={{0,62},{1,3},{2,0},{3,5},{4,2},{5,7},{6,4},{7,9},{8,6},{9,11},{10,... | collective-permute-start | bytes 1572872 | tf_op jit(solution)/shard_map/ppermute | solution.py:416
  35.3 0.8 copy-start.3
  36.1 1.0 copy-start.4
  52.1 11.6 %copy-start.1 = (bf16[1024,1024]{1,0:T(8,128)(2,1)S(1)}, bf16[1024,1024]{1,0:T(8,128)(2,1)}, u32[]{:S(2)}) copy-start(bf16[1024,1024]{1,0:T(8,128)(2,1)} %w_in.3) | copy-start | bytes 6291460
  62.6 4.3 %collective-permute-start.4 = (bf16[16,288,128]{2,1,0:T(8,128)(2,1)S(1)}, bf16[16,288,128]{2,1,0:T(8,128)(2,1)S(1)}, u32[]{:S(2)}, u32[]{:S(2)}) collective-permute-start(bf16[16,288,128]{2,1,0:T(8,128)(2,1)S(1)} %get-tuple-element.81), channel_id=1, source_target_pairs={{0,64},{64,0},{1,65},{65,1},{2,66},{66,2},{3,67},{67,3},{4,68},{68... | collective-permute-start | bytes 3538952 | tf_op jit(solution)/shard_map/ppermute | solution.py:454
  66.1 0.8 copy-start.2
  68.7 24.9 %all-to-all-start.4 = ((bf16[16,288,128]{2,1,0:T(8,128)(2,1)}), bf16[16,288,128]{2,1,0:T(8,128)(2,1)S(1)}, u32[]{:S(2)}, u32[]{:S(2)}) async-start(bf16[16,288,128]{2,1,0:T(8,128)(2,1)} %pair_sum.1), calls=%async_computation.4 | async-start | bytes 2359296 | tf_op jit(solution)/shard_map/all_to_all | solution.py:87
  73.3 16.8 %collective-permute-start.5 = (bf16[256,1024]{1,0:T(8,128)(2,1)}, bf16[256,1024]{1,0:T(8,128)(2,1)}, u32[]{:S(2)}, u32[]{:S(2)}) collective-permute-start(bf16[256,1024]{1,0:T(8,128)(2,1)} %broadcast_select_fusion.2), channel_id=1, source_target_pairs={{0,56},{1,57},{6,14},{7,15},{8,0},{9,1},{14,22},{15,23},{16,8},{17... | collective-permute-start | bytes 1572872 | tf_op jit(solution)/shard_map/ppermute | solution.py:463
  93.6 45.9 %collective-permute-start.6 = (bf16[256,1024]{1,0:T(8,128)(2,1)}, bf16[256,1024]{1,0:T(8,128)(2,1)S(1)}, u32[]{:S(2)}, u32[]{:S(2)}) collective-permute-start(bf16[256,1024]{1,0:T(8,128)(2,1)} %copy-done.2), channel_id=1, source_target_pairs={{1,0},{0,1},{3,2},{2,3},{5,4},{4,5},{7,6},{6,7},{9,8},{8,9},{11,10... | collective-permute-start | bytes 1572872 | tf_op jit(solution)/shard_map/ppermute | solution.py:468
  94.8 44.8 %collective-permute-start.7 = (bf16[256,1024]{1,0:T(8,128)(2,1)}, bf16[256,1024]{1,0:T(8,128)(2,1)S(1)}, u32[]{:S(2)}, u32[]{:S(2)}) collective-permute-start(bf16[256,1024]{1,0:T(8,128)(2,1)} %get-tuple-element.92), channel_id=1, source_target_pairs={{0,2},{1,7},{2,4},{3,1},{4,6},{5,3},{6,0},{7,5},{8,10},{9,15},{10,... | collective-permute-start | bytes 1572872 | tf_op jit(solution)/shard_map/ppermute | solution.py:469
  94.8 44.8 %collective-permute-start.8 = (bf16[256,1024]{1,0:T(8,128)(2,1)}, bf16[256,1024]{1,0:T(8,128)(2,1)}, u32[]{:S(2)}, u32[]{:S(2)}) collective-permute-start(bf16[256,1024]{1,0:T(8,128)(2,1)} %get-tuple-element.93), channel_id=1, source_target_pairs={{0,7},{1,2},{2,1},{3,4},{4,3},{5,6},{6,5},{7,0},{8,15},{9,10},{10,... | collective-permute-start | bytes 1572872 | tf_op jit(solution)/shard_map/ppermute | solution.py:470
  139.6 7.8 %collective-permute-start.9 = (bf16[16,288,128]{2,1,0:T(8,128)(2,1)S(1)}, bf16[16,288,128]{2,1,0:T(8,128)(2,1)S(1)}, u32[]{:S(2)}, u32[]{:S(2)}) collective-permute-start(bf16[16,288,128]{2,1,0:T(8,128)(2,1)S(1)} %get-tuple-element.112.mine), channel_id=1, source_target_pairs={{0,64},{64,0},{1,65},{65,1},{2,66},{66,2},{3,67},{67,3},{4,68},{68... | collective-permute-start | bytes 3538952 | tf_op jit(solution)/shard_map/ppermute | solution.py:477

commit v4 on v3

--- a/solution.py
+++ b/solution.py
@@ -236,7 +236,7 @@
         "latent_grads",
         flops=4 * m * H * H,
         nbytes=8 * 2**20,
-        out_shape=[out((n, H), f32)] + [jax.ShapeDtypeStruct((n, H), bf16)] * 3,
+        out_shape=[pltpu.HBM((n, H), f32)] + [pltpu.HBM((n, H), bf16)] * 3,
     )(*near(dpre, w_in, pick_t))
 
 
@@ -294,62 +294,80 @@
     )(group, pinned(parts))
 
 
-def unpack_kernel(core, mine, got, gw_in, gw_out_t, gb_in, gb_out, loss):
+def unpack_half(half, parts, gw_in, gw_out_t, gb_in, keep):
     j = pl.program_id(0)
-
-    def put(ref):
-        for g in range(2):
-            lanes = slice(g * LANES, (g + 1) * LANES)
-            base = g * ROW_GROUPS
-            for r in range(ROW_GROUPS - 1):
-                gw_in[r * PART : (r + 1) * PART, lanes] = ref[base + r].astype(f32)
-            r = ROW_GROUPS - 1
-            gw_in[r * PART :, lanes] = ref[base + r, : H - r * PART, :].astype(f32)
-            foot = ref[base + r, H - r * PART :, :].astype(f32)
-            gw_out_t[:, lanes] = foot[:GB_IN]
-            gb_in[:, lanes] = foot[GB_IN : GB_IN + 1]
-            small = foot[HIGH : HIGH + 1] + foot[LOW : LOW + 1]
-
-            @pl.when(j == 0)
-            def _():
-                if g == 0:
-                    gb_out[...] = small[:, :GB_IN]
-                else:
-                    loss[...] = jnp.sum(small, axis=1, keepdims=True)
-
-    here = j // 2 == core[0]
-
-    @pl.when(here)
+    for g in range(2):
+        lanes = slice(g * LANES, (g + 1) * LANES)
+        base = g * ROW_GROUPS
+        for r in range(ROW_GROUPS - 1):
+            gw_in[r * PART : (r + 1) * PART, lanes] = parts[base + r].astype(f32)
+        r = ROW_GROUPS - 1
+        gw_in[r * PART :, lanes] = parts[base + r, : H - r * PART, :].astype(f32)
+        foot = parts[base + r, H - r * PART :, :].astype(f32)
+        gw_out_t[:, lanes] = foot[:GB_IN]
+        gb_in[:, lanes] = foot[GB_IN : GB_IN + 1]
+        small = foot[HIGH : HIGH + 1] + foot[LOW : LOW + 1]
+
+        @pl.when(jnp.logical_and(j == 0, half[0] == 0))
+        def _():
+            keep(g, small)
+
+
+def first_kernel(half, parts, gw_in, gw_out_t, gb_in, gb_out, loss):
+    @pl.when(pl.program_id(0) == 0)
     def _():
-        put(mine)
-
-    @pl.when(jnp.logical_not(here))
+        gb_out[...] = jnp.zeros_like(gb_out)
+        loss[...] = jnp.zeros_like(loss)
+
+    def keep(g, small):
+        if g == 0:
+            gb_out[...] = small[:, :GB_IN]
+        else:
+            loss[...] = jnp.sum(small, axis=1, keepdims=True)
+
+    unpack_half(half, parts, gw_in, gw_out_t, gb_in, keep)
+
+
+def second_kernel(half, parts, a, b, c, gb_one, loss_one, gw_in, gw_out_t, gb_in, gb_out, loss):
+    del a, b, c
+
+    @pl.when(pl.program_id(0) == 0)
     def _():
-        put(got)
-
-
-def unpack(core, mine, got):
-    block = (2 * ROW_GROUPS, PART, LANES)
-    cols = lambda j, core: (0, j)
-    whole = lambda j, core: (0, 0)
-    return call(
-        unpack_kernel,
-        "unpack",
-        nbytes=8 * 2**20,
+        gb_out[...] = gb_one[...]
+        loss[...] = loss_one[...]
+
+    def keep(g, small):
+        if g == 0:
+            gb_out[...] = small[:, :GB_IN]
+        else:
+            loss[...] = jnp.sum(small, axis=1, keepdims=True)
+
+    unpack_half(half, parts, gw_in, gw_out_t, gb_in, keep)
+
+
+def unpack(half, parts, first=None):
+    cols = lambda j, half: (0, 2 * half[0] + j)
+    whole = lambda j, half: (0, 0)
+    anywhere = pl.BlockSpec(memory_space=pl.ANY)
+    smalls = [pl.BlockSpec((1, GB_IN), whole), pl.BlockSpec((1, 1), whole)]
+    more = [] if first is None else [anywhere] * 3 + smalls
+    return call(
+        first_kernel if first is None else second_kernel,
+        "unpack_first" if first is None else "unpack_second",
+        nbytes=4 * 2**20,
         grid_spec=pltpu.PrefetchScalarGridSpec(
             num_scalar_prefetch=1,
-            grid=(STEPS,),
+            grid=(2,),
             in_specs=[
-                pl.BlockSpec(block, lambda j, core: (jnp.clip(j - 2 * core[0], 0, 1), 0, 0)),
-                pl.BlockSpec(block, lambda j, core: (jnp.clip(j - 2 * (1 - core[0]), 0, 1), 0, 0)),
-            ],
+                pl.BlockSpec((2 * ROW_GROUPS, PART, LANES), lambda j, half: (j, 0, 0)),
+            ]
+            + more,
             out_specs=[
                 pl.BlockSpec((H, CHUNK), cols),
                 pl.BlockSpec((GB_IN, CHUNK), cols),
                 pl.BlockSpec((1, CHUNK), cols),
-                pl.BlockSpec((1, GB_IN), whole),
-                pl.BlockSpec((1, 1), whole),
-            ],
+            ]
+            + smalls,
         ),
         out_shape=[
             jax.ShapeDtypeStruct((H, H), f32),
@@ -358,7 +376,8 @@
             jax.ShapeDtypeStruct((1, GB_IN), f32),
             jax.ShapeDtypeStruct((1, 1), f32),
         ],
-    )(core, pinned(mine), pinned(got))
+        input_output_aliases={} if first is None else {2: 0, 3: 1, 4: 2},
+    )(half, parts, *([] if first is None else first))
 
 
 def final_kernel(side, own, same, swp, diag, both):
@@ -468,15 +487,17 @@
     r_swap = lax.ppermute(d_swap, GRID, back(SWAP))
     r_same = lax.ppermute(d_same, GRID, BACK_SAME)
     r_diag = lax.ppermute(d_diag, GRID, BACK_DIAG)
-    def planes(x):
-        x = a2a(total_and_spread(group, x, 8), "z")
-        return a2a(total_and_spread(group, x, PARTS), PLANE)
-
-    part = lax.cond(counts[0] >= 0, planes, lambda x: x, part)
+    def z_stage(x):
+        return a2a(total_and_spread(group, x, 8), "z")
+
+    part = lax.cond(counts[0] >= 0, z_stage, lambda x: x[:8], part)
     part, r_swap, r_same, r_diag = lax.optimization_barrier((part, r_swap, r_same, r_diag))
+    part = a2a(total_and_spread(group, part, PARTS), PLANE)
+    grad_latent = final_latents(side, d_own, r_same, r_swap, r_diag)
+    part, grad_latent = lax.optimization_barrier((part, grad_latent))
     got = lax.ppermute(part, "c", [(0, 1), (1, 0)])
-    grad_latent = final_latents(side, d_own, r_same, r_swap, r_diag)
-    gw_in, gw_out_t, gb_in, gb_out, loss = unpack(core, part, got)
+    first = unpack(core, part)
+    gw_in, gw_out_t, gb_in, gb_out, loss = unpack(1 - core, got, first)
     return (
         grad_latent,
         gw_in,

time: 151 us -> 150 us (level)
  blocking collectives: 60.6 us -> 42.4 us
  waiting for transfers between devices: 30.7 us -> 41.8 us
  starting transfers between devices: 32.4 us -> 39.8 us
  Pallas kernels: 14.4 us -> 17.6 us
  local copies, waits for them, and re-layouts: 5.07 us -> 2.45 us
  other arithmetic: 5.31 us -> 3.51 us
    all_to_all x4 -> x3, blocking collectives: 60.6 us -> 42.4 us  [a2a(): return lax.all_to_all(x, axes, split_axis=0, concat_axis=0, tiled=True)]
    all_to_all x1 -> x2, waiting for transfers between devices: 1.37 us -> 14.5 us  [a2a(): return lax.all_to_all(x, axes, split_axis=0, concat_axis=0, tiled=True)]
    ppermute x1, waiting for transfers between devices: 6.04 us -> 1.71 us  [body(): same = lax.ppermute(own, GRID, SAME)]
    all_to_all x1 -> x2, starting transfers between devices: 3.7 us -> 7.66 us  [a2a(): return lax.all_to_all(x, axes, split_axis=0, concat_axis=0, tiled=True)]
    ppermute x1, starting transfers between devices: 3.66 us -> 0.01 us  [body(): swapped = lax.ppermute(oth, GRID, SWAP)]
    ppermute x1, starting transfers between devices: 7.97 us -> 11.4 us  [body(): diag = lax.ppermute(oth, GRID, DIAG)]
    ppermute x1, starting transfers between devices: 0.01 us -> 2.97 us  [body(): edges_there = lax.ppermute(edge_src, GRID, SWAP)]
    unnamed x26 -> x28, local copies, waits for them, and re-layouts: 2.92 us -> 0.33 us
  transfers between devices with their start and end apart: 11 -> 12, of which waited for: 5 -> 6; matrix products, arithmetic and copies ran while one was open for 4% -> 3% of each run, Pallas kernels for 3% -> 5%
where the time goes in v4:
time: 150 us; the launch traced here: 149 us
  blocking collectives  42.4 us (28%)
  waiting for transfers between devices  41.8 us (28%)
  starting transfers between devices  39.8 us (27%)
  Pallas kernels  17.6 us (12%)
  other arithmetic  3.51 us (2%)
  local copies, waits for them, and re-layouts  2.45 us (2%)
  between operations  1.64 us (1%)
    all_to_all x3, blocking collectives, a2a(): return lax.all_to_all(x, axes, split_axis=0, concat_axis=0, tiled=True)  42.4 us
    all_to_all x2, waiting for transfers between devices, a2a(): return lax.all_to_all(x, axes, split_axis=0, concat_axis=0, tiled=True)  14.5 us
    ppermute x1, waiting for transfers between devices, body(): edges_there = lax.ppermute(edge_src, GRID, SWAP)  13.3 us
    ppermute x1, starting transfers between devices, body(): diag = lax.ppermute(oth, GRID, DIAG)  11.4 us
    ppermute x1, waiting for transfers between devices, body(): crossed = lax.ppermute(jnp.where(same_crosses, d_same, d_diag), GRID, CARRY)  11.3 us
    all_to_all x2, starting transfers between devices, a2a(): return lax.all_to_all(x, axes, split_axis=0, concat_axis=0, tiled=True)  7.66 us
    ppermute x1, starting transfers between devices, body(): crossed = lax.ppermute(jnp.where(same_crosses, d_same, d_diag), GRID, CARRY)  6.94 us
    ppermute x1, starting transfers between devices, body(): got = lax.ppermute(part, 'c', [(0, 1), (1, 0)])  4.86 us
  transfers between devices with their start and end apart: 12, of which 6 were waited for; matrix products, arithmetic and copies ran while one was open for 3% of the time, Pallas kernels for 5%

profile of v4, /device:TPU:1, one launch (start us, length us, event | category | flops | bytes accessed | tf_op | source)
XLA Modules:
  0.0 149.3 jit_solution(8949706115272653480)
XLA Ops:
  0.7 1.4 dynamic-slice_bitcast_fusion
  2.1 11.4 %collective-permute-start.3 = (bf16[256,1024]{1,0:T(8,128)(2,1)S(1)}, bf16[256,1024]{1,0:T(8,128)(2,1)S(1)}, u32[]{:S(2)}, u32[]{:S(2)}) collective-permute-start(bf16[256,1024]{1,0:T(8,128)(2,1)S(1)} %get-tuple-element.92), channel_id=1, source_target_pairs={{0,63},{1,2},{2,1},{3,4},{4,3},{5,6},{6,5},{7,8},{8,7},{9,10},{10,... | collective-permute-start | bytes 1572872 | tf_op jit(solution)/shard_map/ppermute | solution.py:434
  13.5 3.0 %collective-permute-start = (s32[256,3]{0,1:T(4,128)S(1)}, s32[256,3]{0,1:T(4,128)S(1)}, u32[]{:S(2)}, u32[]{:S(2)}) collective-permute-start(s32[256,3]{0,1:T(4,128)S(1)} %copy-done.7), channel_id=1, source_target_pairs={{0,1},{1,0},{2,3},{3,2},{4,5},{5,4},{6,7},{7,6},{8,9},{9,8},{10,11... | collective-permute-start | bytes 9224 | tf_op jit(solution)/shard_map/ppermute | solution.py:432
  18.8 13.3 %collective-permute-done = s32[256,3]{0,1:T(4,128)S(1)} collective-permute-done((s32[256,3]{0,1:T(4,128)S(1)}, s32[256,3]{0,1:T(4,128)S(1)}, u32[]{:S(2)}, u32[]{:S(2)}) %collective-permute-start) | collective-permute-done | bytes 3104 | tf_op jit(solution)/shard_map/ppermute | solution.py:432
  33.7 1.7 %collective-permute-done.2.same = bf16[256,1024]{1,0:T(8,128)(2,1)S(1)} collective-permute-done((bf16[256,1024]{1,0:T(8,128)(2,1)S(1)}, bf16[256,1024]{1,0:T(8,128)(2,1)S(1)}, u32[]{:S(2)}, u32[]{:S(2)}) %collective-permute-start.2) | collective-permute-done | bytes 524320 | tf_op jit(solution)/shard_map/ppermute | solution.py:435
  35.4 3.5 %forward.1 = (bf16[1024,512]{1,0:T(8,128)(2,1)S(1)}, bf16[512,1024]{1,0:T(8,128)(2,1)S(1)}, bf16[512,1024]{1,0:T(8,128)(2,1)S(1)}, f32[8,64,128]{2,1,0:T(8,128)S(1)}) custom-call(bf16[512,1024]{1,0:T(8,128)(2,1)S(1)} %add_convert_fusion.1.pick, bf16[256,1024]{1,0:T(8,128)(2,1)S(1)} %get-tuple-element.93.own, ...), custom_call_target="tpu_custom_call" | custom-call | flops 2281701376 | bytes 12582912 | tf_op jit(solution)/shard_map/forward/pallas_call | solution.py:113
  38.9 10.5 %all_to_all.25.pred = f32[8,64,128]{2,1,0:T(8,128)S(1)} all-to-all(f32[8,64,128]{2,1,0:T(8,128)S(1)} %get-tuple-element.55), channel_id=1, replica_groups=mesh['xl'=2,'c'=2,'z'=8,'y'=4,'xh'=2] {'xh','xl','c'}, dimensions={0} | all-to-all | bytes 524288 | tf_op jit(solution)/shard_map/all_to_all | solution.py:87
  49.8 8.8 %all_to_all.26 = bf16[8,64,128]{2,1,0:T(8,128)(2,1)S(1)} all-to-all(bf16[8,64,128]{2,1,0:T(8,128)(2,1)S(1)} %get-tuple-element.58), channel_id=1, replica_groups=mesh['xl'=2,'c'=2,'z'=8,'y'=4,'xh'=2] {'xh','xl','c'}, dimensions={0} | all-to-all | bytes 262144 | tf_op jit(solution)/shard_map/all_to_all | solution.py:87
  58.7 1.2 backward.1
  61.0 3.3 %latent_grads.1 = (f32[256,1024]{1,0:T(8,128)}, bf16[256,1024]{1,0:T(8,128)(2,1)}, bf16[256,1024]{1,0:T(8,128)(2,1)}, bf16[256,1024]{1,0:T(8,128)(2,1)}) custom-call(bf16[512,1024]{1,0:T(8,128)(2,1)S(1)} %get-tuple-element.63.dpre, bf16[1024,1024]{1,0:T(8,128)(2,1)S(1)} %copy-done.2, bf16[1024,512]{1,0:T(8,128)(2,1)S(1)} %add_convert_fusion.pick_t), custom_call_target="tpu_custom_call" | custom-call | flops 2147483648 | bytes 8388608 | tf_op jit(solution)/shard_map/latent_grads/pallas_call | solution.py:234
  64.4 1.8 %pair_sum.1 = bf16[16,288,128]{2,1,0:T(8,128)(2,1)} custom-call(s32[1]{0:T(128)} %bitcast.2.core.half, bf16[512,128]{1,0:T(8,128)(2,1)S(1)} %bitcast.22, bf16[512,1024]{1,0:T(8,128)(2,1)S(1)} %get-tuple-element.63.dpre, bf16[512,1024]{1,0:T(8,128)(2,1)S(1)} %get-tuple-element.60.hid, bf16[1024,512]{1,0:T(8,128)(2,1)S(1)} %get-tuple-element.61.feats_t, ...), custom_call_target="tpu_custom_call" | custom-call | flops 671088640 | bytes 6291456 | tf_op jit(solution)/shard_map/pair_sum/pallas_call | solution.py:261
  66.2 3.8 %all-to-all-start.3 = ((bf16[16,288,128]{2,1,0:T(8,128)(2,1)}), bf16[16,288,128]{2,1,0:T(8,128)(2,1)S(1)}, u32[]{:S(2)}, u32[]{:S(2)}) async-start(bf16[16,288,128]{2,1,0:T(8,128)(2,1)} %pair_sum.1), calls=%async_computation.3 | async-start | bytes 2359296 | tf_op jit(solution)/shard_map/all_to_all | solution.py:87
  70.1 6.9 %collective-permute-start.5 = (bf16[256,1024]{1,0:T(8,128)(2,1)S(1)}, bf16[256,1024]{1,0:T(8,128)(2,1)S(1)}, u32[]{:S(2)}, u32[]{:S(2)}) collective-permute-start(bf16[256,1024]{1,0:T(8,128)(2,1)S(1)} %broadcast_select_fusion.2), channel_id=1, source_target_pairs={{0,56},{1,57},{6,14},{7,15},{8,0},{9,1},{14,22},{15,23},{16,8},{17... | collective-permute-start | bytes 1572872 | tf_op jit(solution)/shard_map/ppermute | solution.py:482
  77.1 11.3 %collective-permute-done.5 = bf16[256,1024]{1,0:T(8,128)(2,1)S(1)} collective-permute-done((bf16[256,1024]{1,0:T(8,128)(2,1)S(1)}, bf16[256,1024]{1,0:T(8,128)(2,1)S(1)}, u32[]{:S(2)}, u32[]{:S(2)}) %collective-permute-start.5) | collective-permute-done | bytes 524320 | tf_op jit(solution)/shard_map/ppermute | solution.py:482
  89.5 1.6 %all-to-all-done.3 = bf16[16,288,128]{2,1,0:T(8,128)(2,1)S(1)} async-done(((bf16[16,288,128]{2,1,0:T(8,128)(2,1)}), bf16[16,288,128]{2,1,0:T(8,128)(2,1)S(1)}, u32[]{:S(2)}, u32[]{:S(2)}) %all-to-all-start.3) | async-done | bytes 1179680 | tf_op jit(solution)/shard_map/all_to_all | solution.py:87
  92.0 3.5 %collective-permute-start.8 = (bf16[256,1024]{1,0:T(8,128)(2,1)}, bf16[256,1024]{1,0:T(8,128)(2,1)}, u32[]{:S(2)}, u32[]{:S(2)}) collective-permute-start(bf16[256,1024]{1,0:T(8,128)(2,1)} %get-tuple-element.74), channel_id=1, source_target_pairs={{0,7},{1,2},{2,1},{3,4},{4,3},{5,6},{6,5},{7,0},{8,15},{9,10},{10,... | collective-permute-start | bytes 1572872 | tf_op jit(solution)/shard_map/ppermute | solution.py:489
  96.2 23.4 %conditional.1 = (bf16[8,288,128]{2,1,0:T(8,128)(2,1)S(1)}) conditional(s32[]{:T(128)} %bitcast.1, bf16[16,288,128]{2,1,0:T(8,128)(2,1)S(1)} %all-to-all-done.3, (s32[1]{0:T(128)}, bf16[16,288,128]{2,1,0:T(8,128)(2,1)S(1)}) %tuple.22), branch_computations={%region_0.1_spmd, %region_1.2_spmd} | conditional | flops 589824 | bytes 2949128 | solution.py:493
  96.4 23.2 %all_to_all.24 = bf16[8,288,128]{2,1,0:T(8,128)(2,1)S(1)} all-to-all(bf16[8,288,128]{2,1,0:T(8,128)(2,1)S(1)} %total.2), channel_id=1, replica_groups=mesh['xl'=2,'c'=2,'z'=8,'y'=4,'xh'=2] {'z'}, dimensions={0} | all-to-all | bytes 1179648 | tf_op jit(solution)/shard_map/cond/branch_1_fun/all_to_all | solution.py:87
  120.7 3.8 %all-to-all-start.4 = ((bf16[16,288,128]{2,1,0:T(8,128)(2,1)}), bf16[16,288,128]{2,1,0:T(8,128)(2,1)S(1)}, u32[]{:S(2)}, u32[]{:S(2)}) async-start(bf16[16,288,128]{2,1,0:T(8,128)(2,1)} %total.3), calls=%async_computation.4 | async-start | bytes 2359296 | tf_op jit(solution)/shard_map/all_to_all | solution.py:87
  124.5 2.4 %final_latents.1 = bf16[2,256,1024]{2,1,0:T(8,128)(2,1)} custom-call(s32[1]{0:T(128)} %bitcast.13.side, f32[256,1024]{1,0:T(8,128)S(1)} %copy-done.1, bf16[256,1024]{1,0:T(8,128)(2,1)} %collective-permute-done.7.same, bf16[256,1024]{1,0:T(8,128)(2,1)S(1)} %collective-permute-done.6.swp, bf16[256,1024]{1,0:T(8,128)(2,1)} %collective-permute-done.8.diag), custom_call_target="tpu_custom_call" | custom-call | bytes 5242880 | tf_op jit(solution)/shard_map/final_latents/pallas_call | solution.py:399
  126.9 12.9 %all-to-all-done.4.parts = bf16[16,288,128]{2,1,0:T(8,128)(2,1)S(1)} async-done(((bf16[16,288,128]{2,1,0:T(8,128)(2,1)}), bf16[16,288,128]{2,1,0:T(8,128)(2,1)S(1)}, u32[]{:S(2)}, u32[]{:S(2)}) %all-to-all-start.4) | async-done | bytes 1179680 | tf_op jit(solution)/shard_map/all_to_all | solution.py:87
  139.8 4.9 %collective-permute-start.9 = (bf16[16,288,128]{2,1,0:T(8,128)(2,1)S(1)}, bf16[16,288,128]{2,1,0:T(8,128)(2,1)S(1)}, u32[]{:S(2)}, u32[]{:S(2)}) collective-permute-start(bf16[16,288,128]{2,1,0:T(8,128)(2,1)S(1)} %all-to-all-done.4.parts), channel_id=1, source_target_pairs={{0,64},{64,0},{1,65},{65,1},{2,66},{66,2},{3,67},{67,3},{4,68},{68... | collective-permute-start | bytes 3538952 | tf_op jit(solution)/shard_map/ppermute | solution.py:498
  144.6 1.5 unpack_first.1
  147.1 2.2 %unpack_second.1 = (f32[1024,1024]{1,0:T(8,128)}, f32[100,1024]{1,0:T(8,128)}, f32[1,1024]{1,0:T(1,128)}, f32[1,100]{1,0:T(1,128)}, f32[1,1]{1,0:T(1,128)}) custom-call(s32[1]{0:T(128)S(6)} %sub.27.half, bf16[16,288,128]{2,1,0:T(8,128)(2,1)S(1)} %collective-permute-done.9.parts, ...), custom_call_target="tpu_custom_call", output_to_operand_aliasing={{0}: (2, {}), {1}: (3, {}), {2}: (4, {})} | custom-call | bytes 4194304 | tf_op jit(solution)/shard_map/unpack_second/pallas_call | solution.py:354
  (57 shorter events, 9.8 us)
Async XLA Ops:
  0.6 16.9 %copy-start = (f32[100,256]{1,0:T(8,128)S(1)}, f32[100,256]{1,0:T(8,128)}, u32[]{:S(2)}) copy-start(f32[100,256]{1,0:T(8,128)} %param.15) | copy-start | bytes 307204
  0.6 12.9 %copy-start.7 = (s32[256,3]{0,1:T(4,128)S(1)}, s32[256,3]{0,1:T(4,128)}, u32[]{:S(2)}) copy-start(s32[256,3]{0,1:T(4,128)} %param.13) | copy-start | bytes 9220
  0.7 16.3 %copy-start.11 = (f32[100]{0:T(128)S(1)}, f32[100]{0:T(128)}, u32[]{:S(2)}) copy-start(f32[100]{0:T(128)} %param.17) | copy-start | bytes 1204
  0.7 16.3 %copy-start.8 = (s32[64]{0:T(128)S(1)}, s32[64]{0:T(128)}, u32[]{:S(2)}) copy-start(s32[64]{0:T(128)} %param.14) | copy-start | bytes 772
  0.7 17.0 %copy-start.9 = (f32[256]{0:T(256)S(1)}, f32[256]{0:T(256)}, u32[]{:S(2)}) copy-start(f32[256]{0:T(256)} %param.16) | copy-start | bytes 3076
  0.7 17.8 %copy-start.12 = (f32[100]{0:T(128)S(1)}, f32[100]{0:T(128)}, u32[]{:S(2)}) copy-start(f32[100]{0:T(128)} %param.21) | copy-start | bytes 1204
  0.7 17.9 %copy-start.6 = (bf16[1024,100]{0,1:T(8,128)(2,1)S(1)}, bf16[1024,100]{0,1:T(8,128)(2,1)}, u32[]{:S(2)}) copy-start(bf16[1024,100]{0,1:T(8,128)(2,1)} %param.20) | copy-start | bytes 614404
  2.1 33.3 %copy-start.3 = (f32[1024]{0:T(1024)S(1)}, f32[1024]{0:T(1024)}, u32[]{:S(2)}) copy-start(f32[1024]{0:T(1024)} %param.19) | copy-start | bytes 12292
  2.1 31.5 %collective-permute-start.3 = (bf16[256,1024]{1,0:T(8,128)(2,1)S(1)}, bf16[256,1024]{1,0:T(8,128)(2,1)S(1)}, u32[]{:S(2)}, u32[]{:S(2)}) collective-permute-start(bf16[256,1024]{1,0:T(8,128)(2,1)S(1)} %get-tuple-element.92), channel_id=1, source_target_pairs={{0,63},{1,2},{2,1},{3,4},{4,3},{5,6},{6,5},{7,8},{8,7},{9,10},{10,... | collective-permute-start | bytes 1572872 | tf_op jit(solution)/shard_map/ppermute | solution.py:434
  13.5 20.1 %collective-permute-start.1 = (bf16[256,1024]{1,0:T(8,128)(2,1)S(1)}, bf16[256,1024]{1,0:T(8,128)(2,1)S(1)}, u32[]{:S(2)}, u32[]{:S(2)}) collective-permute-start(bf16[256,1024]{1,0:T(8,128)(2,1)S(1)} %get-tuple-element.92), channel_id=1, source_target_pairs={{0,1},{1,0},{2,3},{3,2},{4,5},{5,4},{6,7},{7,6},{8,9},{9,8},{10,11... | collective-permute-start | bytes 1572872 | tf_op jit(solution)/shard_map/ppermute | solution.py:433
  13.5 18.6 %collective-permute-start = (s32[256,3]{0,1:T(4,128)S(1)}, s32[256,3]{0,1:T(4,128)S(1)}, u32[]{:S(2)}, u32[]{:S(2)}) collective-permute-start(s32[256,3]{0,1:T(4,128)S(1)} %copy-done.7), channel_id=1, source_target_pairs={{0,1},{1,0},{2,3},{3,2},{4,5},{5,4},{6,7},{7,6},{8,9},{9,8},{10,11... | collective-permute-start | bytes 9224 | tf_op jit(solution)/shard_map/ppermute | solution.py:432
  16.5 18.9 %collective-permute-start.2 = (bf16[256,1024]{1,0:T(8,128)(2,1)S(1)}, bf16[256,1024]{1,0:T(8,128)(2,1)S(1)}, u32[]{:S(2)}, u32[]{:S(2)}) collective-permute-start(bf16[256,1024]{1,0:T(8,128)(2,1)S(1)} %get-tuple-element.93.own), channel_id=1, source_target_pairs={{0,62},{1,3},{2,0},{3,5},{4,2},{5,7},{6,4},{7,9},{8,6},{9,11},{10,... | collective-permute-start | bytes 1572872 | tf_op jit(solution)/shard_map/ppermute | solution.py:435
  49.4 11.6 %copy-start.2 = (bf16[1024,1024]{1,0:T(8,128)(2,1)S(1)}, bf16[1024,1024]{1,0:T(8,128)(2,1)}, u32[]{:S(2)}) copy-start(bf16[1024,1024]{1,0:T(8,128)(2,1)} %w_in.3) | copy-start | bytes 6291460
  59.9 4.5 %collective-permute-start.4 = (bf16[16,288,128]{2,1,0:T(8,128)(2,1)S(1)}, bf16[16,288,128]{2,1,0:T(8,128)(2,1)S(1)}, u32[]{:S(2)}, u32[]{:S(2)}) collective-permute-start(bf16[16,288,128]{2,1,0:T(8,128)(2,1)S(1)} %get-tuple-element.64), channel_id=1, source_target_pairs={{0,64},{64,0},{1,65},{65,1},{2,66},{66,2},{3,67},{67,3},{4,68},{68... | collective-permute-start | bytes 3538952 | tf_op jit(solution)/shard_map/ppermute | solution.py:473
  66.2 3.9 %copy-start.4 = (bf16[256,1024]{1,0:T(8,128)(2,1)S(1)}, bf16[256,1024]{1,0:T(8,128)(2,1)}, u32[]{:S(2)}) copy-start(bf16[256,1024]{1,0:T(8,128)(2,1)} %get-tuple-element.69) | copy-start | bytes 1572868
  66.2 3.9 %copy-start.5 = (bf16[256,1024]{1,0:T(8,128)(2,1)S(1)}, bf16[256,1024]{1,0:T(8,128)(2,1)}, u32[]{:S(2)}) copy-start(bf16[256,1024]{1,0:T(8,128)(2,1)} %get-tuple-element.70) | copy-start | bytes 1572868
  66.2 24.9 %all-to-all-start.3 = ((bf16[16,288,128]{2,1,0:T(8,128)(2,1)}), bf16[16,288,128]{2,1,0:T(8,128)(2,1)S(1)}, u32[]{:S(2)}, u32[]{:S(2)}) async-start(bf16[16,288,128]{2,1,0:T(8,128)(2,1)} %pair_sum.1), calls=%async_computation.3 | async-start | bytes 2359296 | tf_op jit(solution)/shard_map/all_to_all | solution.py:87
  70.1 18.3 %collective-permute-start.5 = (bf16[256,1024]{1,0:T(8,128)(2,1)S(1)}, bf16[256,1024]{1,0:T(8,128)(2,1)S(1)}, u32[]{:S(2)}, u32[]{:S(2)}) collective-permute-start(bf16[256,1024]{1,0:T(8,128)(2,1)S(1)} %broadcast_select_fusion.2), channel_id=1, source_target_pairs={{0,56},{1,57},{6,14},{7,15},{8,0},{9,1},{14,22},{15,23},{16,8},{17... | collective-permute-start | bytes 1572872 | tf_op jit(solution)/shard_map/ppermute | solution.py:482
  91.2 28.4 %collective-permute-start.6 = (bf16[256,1024]{1,0:T(8,128)(2,1)S(1)}, bf16[256,1024]{1,0:T(8,128)(2,1)S(1)}, u32[]{:S(2)}, u32[]{:S(2)}) collective-permute-start(bf16[256,1024]{1,0:T(8,128)(2,1)S(1)} %copy-done.10), channel_id=1, source_target_pairs={{1,0},{0,1},{3,2},{2,3},{5,4},{4,5},{7,6},{6,7},{9,8},{8,9},{11,10... | collective-permute-start | bytes 1572872 | tf_op jit(solution)/shard_map/ppermute | solution.py:487
  92.0 27.6 %collective-permute-start.7 = (bf16[256,1024]{1,0:T(8,128)(2,1)}, bf16[256,1024]{1,0:T(8,128)(2,1)}, u32[]{:S(2)}, u32[]{:S(2)}) collective-permute-start(bf16[256,1024]{1,0:T(8,128)(2,1)} %get-tuple-element.73), channel_id=1, source_target_pairs={{0,2},{1,7},{2,4},{3,1},{4,6},{5,3},{6,0},{7,5},{8,10},{9,15},{10,... | collective-permute-start | bytes 1572872 | tf_op jit(solution)/shard_map/ppermute | solution.py:488
  92.0 27.5 %collective-permute-start.8 = (bf16[256,1024]{1,0:T(8,128)(2,1)}, bf16[256,1024]{1,0:T(8,128)(2,1)}, u32[]{:S(2)}, u32[]{:S(2)}) collective-permute-start(bf16[256,1024]{1,0:T(8,128)(2,1)} %get-tuple-element.74), channel_id=1, source_target_pairs={{0,7},{1,2},{2,1},{3,4},{4,3},{5,6},{6,5},{7,0},{8,15},{9,10},{10,... | collective-permute-start | bytes 1572872 | tf_op jit(solution)/shard_map/ppermute | solution.py:489
  119.5 5.0 %copy-start.1 = (f32[256,1024]{1,0:T(8,128)S(1)}, f32[256,1024]{1,0:T(8,128)}, u32[]{:S(2)}) copy-start(f32[256,1024]{1,0:T(8,128)} %get-tuple-element.76.own) | copy-start | bytes 3145732
  120.7 19.1 %all-to-all-start.4 = ((bf16[16,288,128]{2,1,0:T(8,128)(2,1)}), bf16[16,288,128]{2,1,0:T(8,128)(2,1)S(1)}, u32[]{:S(2)}, u32[]{:S(2)}) async-start(bf16[16,288,128]{2,1,0:T(8,128)(2,1)} %total.3), calls=%async_computation.4 | async-start | bytes 2359296 | tf_op jit(solution)/shard_map/all_to_all | solution.py:87
  139.8 7.3 %collective-permute-start.9 = (bf16[16,288,128]{2,1,0:T(8,128)(2,1)S(1)}, bf16[16,288,128]{2,1,0:T(8,128)(2,1)S(1)}, u32[]{:S(2)}, u32[]{:S(2)}) collective-permute-start(bf16[16,288,128]{2,1,0:T(8,128)(2,1)S(1)} %all-to-all-done.4.parts), channel_id=1, source_target_pairs={{0,64},{64,0},{1,65},{65,1},{2,66},{66,2},{3,67},{67,3},{4,68},{68... | collective-permute-start | bytes 3538952 | tf_op jit(solution)/shard_map/ppermute | solution.py:498
  (1 other events, 2.7 us)

commit v5 on v4

--- a/solution.py
+++ b/solution.py
@@ -87,13 +87,18 @@
     return lax.all_to_all(x, axes, split_axis=0, concat_axis=0, tiled=True)
 
 
-def forward_kernel(pick, own, swp, same, diag, w_in, b_in, w_out, b_out, feats_t, hid, slope, pred, w_here, sem):
-    n = own.shape[0]
+def forward_kernel(
+    pick, own, swp_a, swp_b, same, diag_a, diag_b, w_in, b_in, w_out, b_out,
+    feats_t, hid, slope, pred, w_here, sem
+):
     copy = pltpu.make_async_copy(w_in, w_here, sem)
     copy.start()
+    n = own.shape[0]
+    swp = jnp.concatenate([swp_a[...], swp_b[...]], axis=0)
+    diag = jnp.concatenate([diag_a[...], diag_b[...]], axis=0)
     total = dot(pick[:, :n], own[...])
-    for k, ref in enumerate((swp, same, diag)):
-        total = total + dot(pick[:, (k + 1) * n : (k + 2) * n], ref[...])
+    for k, block in enumerate((swp, same[...], diag)):
+        total = total + dot(pick[:, (k + 1) * n : (k + 2) * n], block)
     feats = (total / 3.0).astype(bf16)
     feats_t[...] = feats.T
     copy.wait()
@@ -108,7 +113,7 @@
         pred[i] = p[i * pts : (i + 1) * pts]
 
 
-def forward(pick, own, swp, same, diag, w_in, b_in, w_out, b_out):
+def forward(pick, nodes, w_in, b_in, w_out, b_out):
     m = pick.shape[0]
     return call(
         forward_kernel,
@@ -116,7 +121,7 @@
         flops=2 * m * H * (2 * H + LANES),
         nbytes=12 * 2**20,
         trans=2 * m * H,
-        in_specs=[pl.BlockSpec(memory_space=pltpu.VMEM)] * 5
+        in_specs=[pl.BlockSpec(memory_space=pltpu.VMEM)] * 7
         + [pl.BlockSpec(memory_space=pl.ANY)]
         + [pl.BlockSpec(memory_space=pltpu.VMEM)] * 3,
         scratch_shapes=[pltpu.VMEM((H, H), bf16), pltpu.SemaphoreType.DMA],
@@ -126,7 +131,7 @@
             out((m, H), bf16),
             jax.ShapeDtypeStruct((MEMBERS, m // MEMBERS, LANES), f32),
         ],
-    )(*near(pick, own, swp, same, diag), far(w_in), *near(b_in, w_out, b_out))
+    )(pick, *nodes, far(w_in), b_in, w_out, b_out)
 
 
 def crps_kernel(pred, aim, wgt, dpred, small):
@@ -413,7 +418,7 @@
 
 
 def body(latent, edge_src, counts, targets, area, var_weight, w_in, b_in, w_out, b_out):
-    l_tile = latent.shape[1]
+    l_tile, width = latent.shape[1:]
     g_tile, k_edges = edge_src.shape
     n_vars = w_out.shape[1]
     h = lax.axis_index("xh")
@@ -427,12 +432,19 @@
     group = lax.rem(lax.axis_index(PLANE), ROW_GROUPS)
     group = jnp.reshape(group, (1,)).astype(jnp.int32)
 
-    own = lax.dynamic_index_in_dim(latent, h, 0, keepdims=False)
-    oth = lax.dynamic_index_in_dim(latent, 1 - h, 0, keepdims=False)
+    half = l_tile // 2
+    oth_a = lax.dynamic_slice(latent, (1 - h, 0, 0), (1, half, width))[0]
     edges_there = lax.ppermute(edge_src, GRID, SWAP)
-    swapped = lax.ppermute(oth, GRID, SWAP)
-    diag = lax.ppermute(oth, GRID, DIAG)
+    swap_a = lax.ppermute(oth_a, GRID, SWAP)
+    later, edges_there, edge_src, targets, area, counts, w_out, b_out = lax.optimization_barrier(
+        (latent, edges_there, edge_src, targets, area, counts, w_out, b_out)
+    )
+    own = lax.dynamic_index_in_dim(later, h, 0, keepdims=False)
+    oth_b = lax.dynamic_slice(later, (1 - h, half, 0), (1, half, width))[0]
+    swap_b = lax.ppermute(oth_b, GRID, SWAP)
+    diag_b = lax.ppermute(oth_b, GRID, DIAG)
     same = lax.ppermute(own, GRID, SAME)
+    diag_a = lax.ppermute(swap_a, GRID, back(SAME))
 
     edges = jnp.where(
         h == 0,
@@ -464,7 +476,7 @@
 
     pick, pick_t, aim, wgt = lax.optimization_barrier((pick, pick_t, aim, wgt))
     feats_t, hidden, slope, pred = forward(
-        pick, own, swapped, same, diag, w_in, b_in[None], w_out_p, b_out_p
+        pick, (own, swap_a, swap_b, same, diag_a, diag_b), w_in, b_in[None], w_out_p, b_out_p
     )
     pred = a2a(pred, GROUP)
     dpred, small = crps(pred, aim, wgt)

time: 150 us -> 151 us (level)
  waiting for transfers between devices: 41.8 us -> 38.8 us
  starting transfers between devices: 39.8 us -> 36.9 us
  other arithmetic: 3.51 us -> 6.1 us
  local copies, waits for them, and re-layouts: 2.45 us -> 4.77 us
  blocking collectives: 42.4 us -> 44.5 us
    ppermute x1, waiting for transfers between devices: 13.3 us -> 0.01 us  [body(): edges_there = lax.ppermute(edge_src, GRID, SWAP)]
    ppermute x2 -> x4, waiting for transfers between devices: 0.01 us -> 7.37 us  [the longest x1 7.36 us: body(): diag_a = lax.ppermute(swap_a, GRID, back(SAME))]
    ppermute x1, starting transfers between devices: 6.94 us -> 2.92 us  [body(): crossed = lax.ppermute(jnp.where(same_crosses, d_same, d_diag), GRID, CARRY)]
    ppermute x1, waiting for transfers between devices: 0.01 us -> 2.23 us  [body(): r_diag = lax.ppermute(d_diag, GRID, BACK_DIAG)]
    optimization_barrier x0 -> x2, local copies, waits for them, and re-layouts: none -> 2.11 us  [body(): lax.optimization_barrier((latent, edges_there, edge_src, targets, area, c...]
    all_to_all x3, blocking collectives: 42.4 us -> 44.5 us  [a2a(): return lax.all_to_all(x, axes, split_axis=0, concat_axis=0, tiled=True)]
    ppermute x2 -> x4, starting transfers between devices: 11.4 us -> 12.4 us  [the longest x1 10.1 us: body(): diag_b = lax.ppermute(oth_b, GRID, DIAG)]
  transfers between devices with their start and end apart: 12 -> 14, of which waited for: 6 -> 7; matrix products, arithmetic and copies ran while one was open for 3% -> 6% of each run, Pallas kernels for 5% -> 5%
where the time goes in v5:
time: 151 us; the launch traced here: 150 us
  blocking collectives  44.5 us (29%)
  waiting for transfers between devices  38.8 us (26%)
  starting transfers between devices  36.9 us (24%)
  Pallas kernels  17.5 us (12%)
  other arithmetic  6.1 us (4%)
  local copies, waits for them, and re-layouts  4.77 us (3%)
  between operations  1.6 us (1%)
    all_to_all x3, blocking collectives, a2a(): return lax.all_to_all(x, axes, split_axis=0, concat_axis=0, tiled=True)  44.5 us
    all_to_all x2, waiting for transfers between devices, a2a(): return lax.all_to_all(x, axes, split_axis=0, concat_axis=0, tiled=True)  15.1 us
    ppermute x1, waiting for transfers between devices, body(): crossed = lax.ppermute(jnp.where(same_crosses, d_same, d_diag), GRID, CARRY)  12.8 us
    ppermute x1, starting transfers between devices, body(): diag_b = lax.ppermute(oth_b, GRID, DIAG)  10.1 us
    all_to_all x2, starting transfers between devices, a2a(): return lax.all_to_all(x, axes, split_axis=0, concat_axis=0, tiled=True)  8.54 us
    ppermute x1, waiting for transfers between devices, body(): diag_a = lax.ppermute(swap_a, GRID, back(SAME))  7.36 us
    ppermute x1, starting transfers between devices, body(): got = lax.ppermute(part, 'c', [(0, 1), (1, 0)])  3.85 us
    ppermute x1, starting transfers between devices, body(): edges_there = lax.ppermute(edge_src, GRID, SWAP)  3.66 us
  transfers between devices with their start and end apart: 14, of which 7 were waited for; matrix products, arithmetic and copies ran while one was open for 6% of the time, Pallas kernels for 5%

profile of v5, /device:TPU:1, one launch (start us, length us, event | category | flops | bytes accessed | tf_op | source)
XLA Modules:
  0.0 150.1 jit_solution(17215111825318465681)
XLA Ops:
  0.7 3.7 %collective-permute-start = (s32[256,3]{0,1:T(4,128)}, s32[256,3]{0,1:T(4,128)S(1)}, u32[]{:S(2)}, u32[]{:S(2)}) collective-permute-start(s32[256,3]{0,1:T(4,128)} %param.13), channel_id=1, source_target_pairs={{0,1},{1,0},{2,3},{3,2},{4,5},{5,4},{6,7},{7,6},{8,9},{9,8},{10,11... | collective-permute-start | bytes 9224 | tf_op jit(solution)/shard_map/ppermute | solution.py:437
  6.2 10.1 %collective-permute-start.5 = (bf16[128,1024]{1,0:T(8,128)(2,1)S(1)}, bf16[128,1024]{1,0:T(8,128)(2,1)S(1)}, u32[]{:S(2)}, u32[]{:S(2)}) collective-permute-start(bf16[128,1024]{1,0:T(8,128)(2,1)S(1)} %dynamic-slice_bitcast_fusion.1), channel_id=1, source_target_pairs={{0,63},{1,2},{2,1},{3,4},{4,3},{5,6},{6,5},{7,8},{8,7},{9,10},{10,... | collective-permute-start | bytes 786440 | tf_op jit(solution)/shard_map/ppermute | solution.py:445
  24.0 7.4 %collective-permute-done.4.diag_a = bf16[128,1024]{1,0:T(8,128)(2,1)S(1)} collective-permute-done((bf16[128,1024]{1,0:T(8,128)(2,1)S(1)}, bf16[128,1024]{1,0:T(8,128)(2,1)S(1)}, u32[]{:S(2)}, u32[]{:S(2)}) %collective-permute-start.4) | collective-permute-done | bytes 262176 | tf_op jit(solution)/shard_map/ppermute | solution.py:447
  31.7 3.5 %forward.1 = (bf16[1024,512]{1,0:T(8,128)(2,1)S(1)}, bf16[512,1024]{1,0:T(8,128)(2,1)S(1)}, bf16[512,1024]{1,0:T(8,128)(2,1)S(1)}, f32[8,64,128]{2,1,0:T(8,128)S(1)}) custom-call(bf16[512,1024]{1,0:T(8,128)(2,1)S(1)} %add_convert_fusion.1.pick, bf16[256,1024]{1,0:T(8,128)(2,1)S(1)} %dynamic-slice_bitcast_fusion.own, ...), custom_call_target="tpu_custom_call" | custom-call | flops 2281701376 | bytes 12582912 | tf_op jit(solution)/shard_map/forward/pallas_call | solution.py:118
  35.2 16.3 %all_to_all.25.pred = f32[8,64,128]{2,1,0:T(8,128)S(1)} all-to-all(f32[8,64,128]{2,1,0:T(8,128)S(1)} %get-tuple-element.71), channel_id=1, replica_groups=mesh['xl'=2,'c'=2,'z'=8,'y'=4,'xh'=2] {'xh','xl','c'}, dimensions={0} | all-to-all | bytes 524288 | tf_op jit(solution)/shard_map/all_to_all | solution.py:87
  51.9 8.8 %all_to_all.26 = bf16[8,64,128]{2,1,0:T(8,128)(2,1)S(1)} all-to-all(bf16[8,64,128]{2,1,0:T(8,128)(2,1)S(1)} %get-tuple-element.74), channel_id=1, replica_groups=mesh['xl'=2,'c'=2,'z'=8,'y'=4,'xh'=2] {'xh','xl','c'}, dimensions={0} | all-to-all | bytes 262144 | tf_op jit(solution)/shard_map/all_to_all | solution.py:87
  63.1 3.3 %latent_grads.1 = (f32[256,1024]{1,0:T(8,128)}, bf16[256,1024]{1,0:T(8,128)(2,1)}, bf16[256,1024]{1,0:T(8,128)(2,1)}, bf16[256,1024]{1,0:T(8,128)(2,1)}) custom-call(bf16[512,1024]{1,0:T(8,128)(2,1)S(1)} %get-tuple-element.79.dpre, bf16[1024,1024]{1,0:T(8,128)(2,1)S(1)} %copy-done.2, bf16[1024,512]{1,0:T(8,128)(2,1)S(1)} %add_convert_fusion.pick_t), custom_call_target="tpu_custom_call" | custom-call | flops 2147483648 | bytes 8388608 | tf_op jit(solution)/shard_map/latent_grads/pallas_call | solution.py:239
  66.4 1.8 %pair_sum.1 = bf16[16,288,128]{2,1,0:T(8,128)(2,1)} custom-call(s32[1]{0:T(128)} %bitcast.2.core.half, bf16[512,128]{1,0:T(8,128)(2,1)S(1)} %bitcast.25, bf16[512,1024]{1,0:T(8,128)(2,1)S(1)} %get-tuple-element.79.dpre, bf16[512,1024]{1,0:T(8,128)(2,1)S(1)} %get-tuple-element.76.hid, bf16[1024,512]{1,0:T(8,128)(2,1)S(1)} %get-tuple-element.77.feats_t, ...), custom_call_target="tpu_custom_call" | custom-call | flops 671088640 | bytes 6291456 | tf_op jit(solution)/shard_map/pair_sum/pallas_call | solution.py:266
  68.3 3.8 %all-to-all-start.3 = ((bf16[16,288,128]{2,1,0:T(8,128)(2,1)}), bf16[16,288,128]{2,1,0:T(8,128)(2,1)S(1)}, u32[]{:S(2)}, u32[]{:S(2)}) async-start(bf16[16,288,128]{2,1,0:T(8,128)(2,1)} %pair_sum.1), calls=%async_computation.3 | async-start | bytes 2359296 | tf_op jit(solution)/shard_map/all_to_all | solution.py:87
  73.0 2.9 %collective-permute-start.7 = (bf16[256,1024]{1,0:T(8,128)(2,1)}, bf16[256,1024]{1,0:T(8,128)(2,1)}, u32[]{:S(2)}, u32[]{:S(2)}) collective-permute-start(bf16[256,1024]{1,0:T(8,128)(2,1)} %broadcast_select_fusion.2), channel_id=1, source_target_pairs={{0,56},{1,57},{6,14},{7,15},{8,0},{9,1},{14,22},{15,23},{16,8},{17... | collective-permute-start | bytes 1572872 | tf_op jit(solution)/shard_map/ppermute | solution.py:494
  75.9 12.8 %collective-permute-done.7 = bf16[256,1024]{1,0:T(8,128)(2,1)} collective-permute-done((bf16[256,1024]{1,0:T(8,128)(2,1)}, bf16[256,1024]{1,0:T(8,128)(2,1)}, u32[]{:S(2)}, u32[]{:S(2)}) %collective-permute-start.7) | collective-permute-done | bytes 524320 | tf_op jit(solution)/shard_map/ppermute | solution.py:494
  88.7 2.1 %broadcast_select_fusion = (bf16[256,1024]{1,0:T(8,128)(2,1)}, bf16[256,1024]{1,0:T(8,128)(2,1)}) fusion(bf16[256,1024]{1,0:T(8,128)(2,1)} %collective-permute-done.7, bf16[256,1024]{1,0:T(8,128)(2,1)S(1)} %copy-done.5, pred[]{:T(512)S(6)} %or.7, bf16[256,1024]{1,0:T(8,128)(2,1)S(1)} %copy-done.4, pred[]{:T(512)S(6)} %or.6), kind=kLoop, calls=%fused_computation.9 | loop fusion | flops 524288 | bytes 2621442 | tf_op jit(solution)/shard_map/jit(_where)/select_n | solution.py:496
  90.9 2.4 %all-to-all-done.3 = bf16[16,288,128]{2,1,0:T(8,128)(2,1)S(1)} async-done(((bf16[16,288,128]{2,1,0:T(8,128)(2,1)}), bf16[16,288,128]{2,1,0:T(8,128)(2,1)S(1)}, u32[]{:S(2)}, u32[]{:S(2)}) %all-to-all-start.3) | async-done | bytes 1179680 | tf_op jit(solution)/shard_map/all_to_all | solution.py:87
  94.1 3.0 %collective-permute-start.10 = (bf16[256,1024]{1,0:T(8,128)(2,1)}, bf16[256,1024]{1,0:T(8,128)(2,1)}, u32[]{:S(2)}, u32[]{:S(2)}) collective-permute-start(bf16[256,1024]{1,0:T(8,128)(2,1)} %get-tuple-element.90), channel_id=1, source_target_pairs={{0,7},{1,2},{2,1},{3,4},{4,3},{5,6},{6,5},{7,0},{8,15},{9,10},{10,... | collective-permute-start | bytes 1572872 | tf_op jit(solution)/shard_map/ppermute | solution.py:501
  97.8 19.6 %conditional.1 = (bf16[8,288,128]{2,1,0:T(8,128)(2,1)S(1)}) conditional(s32[]{:T(128)} %bitcast.1, bf16[16,288,128]{2,1,0:T(8,128)(2,1)S(1)} %all-to-all-done.3, (s32[1]{0:T(128)}, bf16[16,288,128]{2,1,0:T(8,128)(2,1)S(1)}) %tuple.24), branch_computations={%region_0.1_spmd, %region_1.2_spmd} | conditional | flops 589824 | bytes 2949128 | solution.py:505
  97.9 19.4 %all_to_all.24 = bf16[8,288,128]{2,1,0:T(8,128)(2,1)S(1)} all-to-all(bf16[8,288,128]{2,1,0:T(8,128)(2,1)S(1)} %total.2), channel_id=1, replica_groups=mesh['xl'=2,'c'=2,'z'=8,'y'=4,'xh'=2] {'z'}, dimensions={0} | all-to-all | bytes 1179648 | tf_op jit(solution)/shard_map/cond/branch_1_fun/all_to_all | solution.py:87
  117.4 2.2 %collective-permute-done.10.diag = bf16[256,1024]{1,0:T(8,128)(2,1)} collective-permute-done((bf16[256,1024]{1,0:T(8,128)(2,1)}, bf16[256,1024]{1,0:T(8,128)(2,1)}, u32[]{:S(2)}, u32[]{:S(2)}) %collective-permute-start.10) | collective-permute-done | bytes 524320 | tf_op jit(solution)/shard_map/ppermute | solution.py:501
  120.7 4.7 %all-to-all-start.4 = ((bf16[16,288,128]{2,1,0:T(8,128)(2,1)}), bf16[16,288,128]{2,1,0:T(8,128)(2,1)S(1)}, u32[]{:S(2)}, u32[]{:S(2)}) async-start(bf16[16,288,128]{2,1,0:T(8,128)(2,1)} %total.3), calls=%async_computation.4 | async-start | bytes 2359296 | tf_op jit(solution)/shard_map/all_to_all | solution.py:87
  125.4 1.2 copy-done.1
  126.7 2.3 %final_latents.1 = bf16[2,256,1024]{2,1,0:T(8,128)(2,1)} custom-call(s32[1]{0:T(128)} %bitcast.14.side, f32[256,1024]{1,0:T(8,128)S(1)} %copy-done.1, bf16[256,1024]{1,0:T(8,128)(2,1)} %collective-permute-done.9.same, bf16[256,1024]{1,0:T(8,128)(2,1)S(1)} %collective-permute-done.8.swp, bf16[256,1024]{1,0:T(8,128)(2,1)} %collective-permute-done.10.diag), custom_call_target="tpu_custom_call" | custom-call | bytes 5242880 | tf_op jit(solution)/shard_map/final_latents/pallas_call | solution.py:404
  128.9 12.7 %all-to-all-done.4.parts = bf16[16,288,128]{2,1,0:T(8,128)(2,1)S(1)} async-done(((bf16[16,288,128]{2,1,0:T(8,128)(2,1)}), bf16[16,288,128]{2,1,0:T(8,128)(2,1)S(1)}, u32[]{:S(2)}, u32[]{:S(2)}) %all-to-all-start.4) | async-done | bytes 1179680 | tf_op jit(solution)/shard_map/all_to_all | solution.py:87
  141.6 3.8 %collective-permute-start.11 = (bf16[16,288,128]{2,1,0:T(8,128)(2,1)S(1)}, bf16[16,288,128]{2,1,0:T(8,128)(2,1)S(1)}, u32[]{:S(2)}, u32[]{:S(2)}) collective-permute-start(bf16[16,288,128]{2,1,0:T(8,128)(2,1)S(1)} %all-to-all-done.4.parts), channel_id=1, source_target_pairs={{0,64},{64,0},{1,65},{65,1},{2,66},{66,2},{3,67},{67,3},{4,68},{68... | collective-permute-start | bytes 3538952 | tf_op jit(solution)/shard_map/ppermute | solution.py:510
  145.4 1.5 unpack_first.1
  147.9 2.2 %unpack_second.1 = (f32[1024,1024]{1,0:T(8,128)}, f32[100,1024]{1,0:T(8,128)}, f32[1,1024]{1,0:T(1,128)}, f32[1,100]{1,0:T(1,128)}, f32[1,1]{1,0:T(1,128)}) custom-call(s32[1]{0:T(128)S(6)} %sub.28.half, bf16[16,288,128]{2,1,0:T(8,128)(2,1)S(1)} %collective-permute-done.11.parts, ...), custom_call_target="tpu_custom_call", output_to_operand_aliasing={{0}: (2, {}), {1}: (3, {}), {2}: (4, {})} | custom-call | bytes 4194304 | tf_op jit(solution)/shard_map/unpack_second/pallas_call | solution.py:359
  (55 shorter events, 16.5 us)
Async XLA Ops:
  0.6 3.7 %copy-start = (bf16[2,256,1024]{2,1,0:T(8,128)(2,1)S(1)}, bf16[2,256,1024]{2,1,0:T(8,128)(2,1)}, u32[]{:S(2)}) copy-start(bf16[2,256,1024]{2,1,0:T(8,128)(2,1)} %param.12) | copy-start | bytes 3145732
  0.6 20.7 %copy-start.7 = (f32[256]{0:T(256)S(1)}, f32[256]{0:T(256)}, u32[]{:S(2)}) copy-start(f32[256]{0:T(256)} %param.16) | copy-start | bytes 3076
  0.7 19.2 %copy-start.6 = (s32[64]{0:T(128)S(1)}, s32[64]{0:T(128)}, u32[]{:S(2)}) copy-start(s32[64]{0:T(128)} %param.14) | copy-start | bytes 772
  0.7 5.6 %collective-permute-start = (s32[256,3]{0,1:T(4,128)}, s32[256,3]{0,1:T(4,128)S(1)}, u32[]{:S(2)}, u32[]{:S(2)}) collective-permute-start(s32[256,3]{0,1:T(4,128)} %param.13), channel_id=1, source_target_pairs={{0,1},{1,0},{2,3},{3,2},{4,5},{5,4},{6,7},{7,6},{8,9},{9,8},{10,11... | collective-permute-start | bytes 9224 | tf_op jit(solution)/shard_map/ppermute | solution.py:437
  4.4 18.4 %collective-permute-start.1 = (bf16[128,1024]{1,0:T(8,128)(2,1)S(1)}, bf16[128,1024]{1,0:T(8,128)(2,1)S(1)}, u32[]{:S(2)}, u32[]{:S(2)}) collective-permute-start(bf16[128,1024]{1,0:T(8,128)(2,1)S(1)} %dynamic-slice_bitcast_fusion.2), channel_id=1, source_target_pairs={{0,1},{1,0},{2,3},{3,2},{4,5},{5,4},{6,7},{7,6},{8,9},{9,8},{10,11... | collective-permute-start | bytes 786440 | tf_op jit(solution)/shard_map/ppermute | solution.py:438
  6.2 17.7 %collective-permute-start.5 = (bf16[128,1024]{1,0:T(8,128)(2,1)S(1)}, bf16[128,1024]{1,0:T(8,128)(2,1)S(1)}, u32[]{:S(2)}, u32[]{:S(2)}) collective-permute-start(bf16[128,1024]{1,0:T(8,128)(2,1)S(1)} %dynamic-slice_bitcast_fusion.1), channel_id=1, source_target_pairs={{0,63},{1,2},{2,1},{3,4},{4,3},{5,6},{6,5},{7,8},{8,7},{9,10},{10,... | collective-permute-start | bytes 786440 | tf_op jit(solution)/shard_map/ppermute | solution.py:445
  16.4 7.7 %collective-permute-start.2 = (bf16[128,1024]{1,0:T(8,128)(2,1)S(1)}, bf16[128,1024]{1,0:T(8,128)(2,1)S(1)}, u32[]{:S(2)}, u32[]{:S(2)}) collective-permute-start(bf16[128,1024]{1,0:T(8,128)(2,1)S(1)} %dynamic-slice_bitcast_fusion.1), channel_id=1, source_target_pairs={{0,1},{1,0},{2,3},{3,2},{4,5},{5,4},{6,7},{7,6},{8,9},{9,8},{10,11... | collective-permute-start | bytes 786440 | tf_op jit(solution)/shard_map/ppermute | solution.py:444
  18.2 5.8 %copy-start.8 = (f32[100]{0:T(128)S(1)}, f32[100]{0:T(128)}, u32[]{:S(2)}) copy-start(f32[100]{0:T(128)} %param.21) | copy-start | bytes 1204
  18.2 13.5 %copy-start.3 = (f32[1024]{0:T(1024)S(1)}, f32[1024]{0:T(1024)}, u32[]{:S(2)}) copy-start(f32[1024]{0:T(1024)} %param.19) | copy-start | bytes 12292
  19.4 12.3 %collective-permute-start.3 = (bf16[256,1024]{1,0:T(8,128)(2,1)S(1)}, bf16[256,1024]{1,0:T(8,128)(2,1)S(1)}, u32[]{:S(2)}, u32[]{:S(2)}) collective-permute-start(bf16[256,1024]{1,0:T(8,128)(2,1)S(1)} %dynamic-slice_bitcast_fusion.own), channel_id=1, source_target_pairs={{0,62},{1,3},{2,0},{3,5},{4,2},{5,7},{6,4},{7,9},{8,6},{9,11},{10,... | collective-permute-start | bytes 1572872 | tf_op jit(solution)/shard_map/ppermute | solution.py:446
  22.8 8.6 %collective-permute-start.4 = (bf16[128,1024]{1,0:T(8,128)(2,1)S(1)}, bf16[128,1024]{1,0:T(8,128)(2,1)S(1)}, u32[]{:S(2)}, u32[]{:S(2)}) collective-permute-start(bf16[128,1024]{1,0:T(8,128)(2,1)S(1)} %collective-permute-done.1.swp_a), channel_id=1, source_target_pairs={{62,0},{3,1},{0,2},{5,3},{2,4},{7,5},{4,6},{9,7},{6,8},{11,9},{8,1... | collective-permute-start | bytes 786440 | tf_op jit(solution)/shard_map/ppermute | solution.py:447
  51.5 11.6 %copy-start.2 = (bf16[1024,1024]{1,0:T(8,128)(2,1)S(1)}, bf16[1024,1024]{1,0:T(8,128)(2,1)}, u32[]{:S(2)}) copy-start(bf16[1024,1024]{1,0:T(8,128)(2,1)} %w_in.3) | copy-start | bytes 6291460
  61.9 4.5 %collective-permute-start.6 = (bf16[16,288,128]{2,1,0:T(8,128)(2,1)S(1)}, bf16[16,288,128]{2,1,0:T(8,128)(2,1)S(1)}, u32[]{:S(2)}, u32[]{:S(2)}) collective-permute-start(bf16[16,288,128]{2,1,0:T(8,128)(2,1)S(1)} %get-tuple-element.80), channel_id=1, source_target_pairs={{0,64},{64,0},{1,65},{65,1},{2,66},{66,2},{3,67},{67,3},{4,68},{68... | collective-permute-start | bytes 3538952 | tf_op jit(solution)/shard_map/ppermute | solution.py:485
  68.3 3.9 %copy-start.4 = (bf16[256,1024]{1,0:T(8,128)(2,1)S(1)}, bf16[256,1024]{1,0:T(8,128)(2,1)}, u32[]{:S(2)}) copy-start(bf16[256,1024]{1,0:T(8,128)(2,1)} %get-tuple-element.85) | copy-start | bytes 1572868
  68.3 3.9 %copy-start.5 = (bf16[256,1024]{1,0:T(8,128)(2,1)S(1)}, bf16[256,1024]{1,0:T(8,128)(2,1)}, u32[]{:S(2)}) copy-start(bf16[256,1024]{1,0:T(8,128)(2,1)} %get-tuple-element.86) | copy-start | bytes 1572868
  68.3 25.0 %all-to-all-start.3 = ((bf16[16,288,128]{2,1,0:T(8,128)(2,1)}), bf16[16,288,128]{2,1,0:T(8,128)(2,1)S(1)}, u32[]{:S(2)}, u32[]{:S(2)}) async-start(bf16[16,288,128]{2,1,0:T(8,128)(2,1)} %pair_sum.1), calls=%async_computation.3 | async-start | bytes 2359296 | tf_op jit(solution)/shard_map/all_to_all | solution.py:87
  73.0 15.7 %collective-permute-start.7 = (bf16[256,1024]{1,0:T(8,128)(2,1)}, bf16[256,1024]{1,0:T(8,128)(2,1)}, u32[]{:S(2)}, u32[]{:S(2)}) collective-permute-start(bf16[256,1024]{1,0:T(8,128)(2,1)} %broadcast_select_fusion.2), channel_id=1, source_target_pairs={{0,56},{1,57},{6,14},{7,15},{8,0},{9,1},{14,22},{15,23},{16,8},{17... | collective-permute-start | bytes 1572872 | tf_op jit(solution)/shard_map/ppermute | solution.py:494
  93.3 24.1 %collective-permute-start.8 = (bf16[256,1024]{1,0:T(8,128)(2,1)}, bf16[256,1024]{1,0:T(8,128)(2,1)S(1)}, u32[]{:S(2)}, u32[]{:S(2)}) collective-permute-start(bf16[256,1024]{1,0:T(8,128)(2,1)} %get-tuple-element.88), channel_id=1, source_target_pairs={{1,0},{0,1},{3,2},{2,3},{5,4},{4,5},{7,6},{6,7},{9,8},{8,9},{11,10... | collective-permute-start | bytes 1572872 | tf_op jit(solution)/shard_map/ppermute | solution.py:499
  93.3 24.1 %collective-permute-start.9 = (bf16[256,1024]{1,0:T(8,128)(2,1)}, bf16[256,1024]{1,0:T(8,128)(2,1)}, u32[]{:S(2)}, u32[]{:S(2)}) collective-permute-start(bf16[256,1024]{1,0:T(8,128)(2,1)} %get-tuple-element.89), channel_id=1, source_target_pairs={{0,2},{1,7},{2,4},{3,1},{4,6},{5,3},{6,0},{7,5},{8,10},{9,15},{10,... | collective-permute-start | bytes 1572872 | tf_op jit(solution)/shard_map/ppermute | solution.py:500
  94.1 25.5 %collective-permute-start.10 = (bf16[256,1024]{1,0:T(8,128)(2,1)}, bf16[256,1024]{1,0:T(8,128)(2,1)}, u32[]{:S(2)}, u32[]{:S(2)}) collective-permute-start(bf16[256,1024]{1,0:T(8,128)(2,1)} %get-tuple-element.90), channel_id=1, source_target_pairs={{0,7},{1,2},{2,1},{3,4},{4,3},{5,6},{6,5},{7,0},{8,15},{9,10},{10,... | collective-permute-start | bytes 1572872 | tf_op jit(solution)/shard_map/ppermute | solution.py:501
  120.7 20.9 %all-to-all-start.4 = ((bf16[16,288,128]{2,1,0:T(8,128)(2,1)}), bf16[16,288,128]{2,1,0:T(8,128)(2,1)S(1)}, u32[]{:S(2)}, u32[]{:S(2)}) async-start(bf16[16,288,128]{2,1,0:T(8,128)(2,1)} %total.3), calls=%async_computation.4 | async-start | bytes 2359296 | tf_op jit(solution)/shard_map/all_to_all | solution.py:87
  125.4 1.2 copy-start.1
  141.6 6.3 %collective-permute-start.11 = (bf16[16,288,128]{2,1,0:T(8,128)(2,1)S(1)}, bf16[16,288,128]{2,1,0:T(8,128)(2,1)S(1)}, u32[]{:S(2)}, u32[]{:S(2)}) collective-permute-start(bf16[16,288,128]{2,1,0:T(8,128)(2,1)S(1)} %all-to-all-done.4.parts), channel_id=1, source_target_pairs={{0,64},{64,0},{1,65},{65,1},{2,66},{66,2},{3,67},{67,3},{4,68},{68... | collective-permute-start | bytes 3538952 | tf_op jit(solution)/shard_map/ppermute | solution.py:510

commit v6 on v4

--- a/solution.py
+++ b/solution.py
@@ -487,15 +487,14 @@
     r_swap = lax.ppermute(d_swap, GRID, back(SWAP))
     r_same = lax.ppermute(d_same, GRID, BACK_SAME)
     r_diag = lax.ppermute(d_diag, GRID, BACK_DIAG)
-    def z_stage(x):
-        return a2a(total_and_spread(group, x, 8), "z")
-
-    part = lax.cond(counts[0] >= 0, z_stage, lambda x: x[:8], part)
+    def planes(x):
+        x = a2a(total_and_spread(group, x, 8), "z")
+        return a2a(total_and_spread(group, x, PARTS), PLANE)
+
+    part = lax.cond(counts[0] >= 0, planes, lambda x: x, part)
     part, r_swap, r_same, r_diag = lax.optimization_barrier((part, r_swap, r_same, r_diag))
-    part = a2a(total_and_spread(group, part, PARTS), PLANE)
+    got = lax.ppermute(part, "c", [(0, 1), (1, 0)])
     grad_latent = final_latents(side, d_own, r_same, r_swap, r_diag)
-    part, grad_latent = lax.optimization_barrier((part, grad_latent))
-    got = lax.ppermute(part, "c", [(0, 1), (1, 0)])
     first = unpack(core, part)
     gw_in, gw_out_t, gb_in, gb_out, loss = unpack(1 - core, got, first)
     return (

time: 150 us -> 149 us (level)
  blocking collectives: 42.4 us -> 61.4 us
  waiting for transfers between devices: 41.8 us -> 28.1 us
  starting transfers between devices: 39.8 us -> 35.5 us
    all_to_all x3 -> x4, blocking collectives: 42.4 us -> 61.4 us  [a2a(): return lax.all_to_all(x, axes, split_axis=0, concat_axis=0, tiled=True)]
    all_to_all x2 -> x1, waiting for transfers between devices: 14.5 us -> 1.82 us  [a2a(): return lax.all_to_all(x, axes, split_axis=0, concat_axis=0, tiled=True)]
    all_to_all x2 -> x1, starting transfers between devices: 7.66 us -> 3.83 us  [a2a(): return lax.all_to_all(x, axes, split_axis=0, concat_axis=0, tiled=True)]
  transfers between devices with their start and end apart: 12 -> 11, of which waited for: 6 -> 4; matrix products, arithmetic and copies ran while one was open for 3% -> 3% of each run, Pallas kernels for 5% -> 5%
where the time goes in v6:
time: 149 us
  blocking collectives  61.4 us (41%)
  starting transfers between devices  35.5 us (24%)
  waiting for transfers between devices  28.1 us (19%)
  Pallas kernels  16.4 us (11%)
  other arithmetic  3.44 us (2%)
  local copies, waits for them, and re-layouts  2.44 us (2%)
  between operations  1.67 us (1%)
    all_to_all x4, blocking collectives, a2a(): return lax.all_to_all(x, axes, split_axis=0, concat_axis=0, tiled=True)  61.4 us
    ppermute x1, waiting for transfers between devices, body(): edges_there = lax.ppermute(edge_src, GRID, SWAP)  13.3 us
    ppermute x1, starting transfers between devices, body(): diag = lax.ppermute(oth, GRID, DIAG)  11.4 us
    ppermute x1, waiting for transfers between devices, body(): crossed = lax.ppermute(jnp.where(same_crosses, d_same, d_diag), GRID, CARRY)  11.3 us
    ppermute x1, starting transfers between devices, body(): crossed = lax.ppermute(jnp.where(same_crosses, d_same, d_diag), GRID, CARRY)  6.94 us
    ppermute x1, starting transfers between devices, body(): got = lax.ppermute(part, 'c', [(0, 1), (1, 0)])  4.59 us
    all_to_all x1, starting transfers between devices, a2a(): return lax.all_to_all(x, axes, split_axis=0, concat_axis=0, tiled=True)  3.83 us
    pallas_call x2, Pallas kernels, unpack(): call(first_kernel if first is None else second_kernel, 'unpack_first' if...  3.64 us
  transfers between devices with their start and end apart: 11, of which 4 were waited for; matrix products, arithmetic and copies ran while one was open for 3% of the time, Pallas kernels for 5%

profile of v6, /device:TPU:1, one launch (start us, length us, event | category | flops | bytes accessed | tf_op | source)
XLA Modules:
  0.0 149.0 jit_solution(11969200300287748689)
XLA Ops:
  0.7 1.4 dynamic-slice_bitcast_fusion
  2.1 11.4 %collective-permute-start.3 = (bf16[256,1024]{1,0:T(8,128)(2,1)S(1)}, bf16[256,1024]{1,0:T(8,128)(2,1)S(1)}, u32[]{:S(2)}, u32[]{:S(2)}) collective-permute-start(bf16[256,1024]{1,0:T(8,128)(2,1)S(1)} %get-tuple-element.113), channel_id=1, source_target_pairs={{0,63},{1,2},{2,1},{3,4},{4,3},{5,6},{6,5},{7,8},{8,7},{9,10},{10,... | collective-permute-start | bytes 1572872 | tf_op jit(solution)/shard_map/ppermute | solution.py:434
  13.5 3.0 %collective-permute-start = (s32[256,3]{0,1:T(4,128)S(1)}, s32[256,3]{0,1:T(4,128)S(1)}, u32[]{:S(2)}, u32[]{:S(2)}) collective-permute-start(s32[256,3]{0,1:T(4,128)S(1)} %copy-done.7), channel_id=1, source_target_pairs={{0,1},{1,0},{2,3},{3,2},{4,5},{5,4},{6,7},{7,6},{8,9},{9,8},{10,11... | collective-permute-start | bytes 9224 | tf_op jit(solution)/shard_map/ppermute | solution.py:432
  18.8 13.3 %collective-permute-done = s32[256,3]{0,1:T(4,128)S(1)} collective-permute-done((s32[256,3]{0,1:T(4,128)S(1)}, s32[256,3]{0,1:T(4,128)S(1)}, u32[]{:S(2)}, u32[]{:S(2)}) %collective-permute-start) | collective-permute-done | bytes 3104 | tf_op jit(solution)/shard_map/ppermute | solution.py:432
  33.7 1.7 %collective-permute-done.2.same = bf16[256,1024]{1,0:T(8,128)(2,1)S(1)} collective-permute-done((bf16[256,1024]{1,0:T(8,128)(2,1)S(1)}, bf16[256,1024]{1,0:T(8,128)(2,1)S(1)}, u32[]{:S(2)}, u32[]{:S(2)}) %collective-permute-start.2) | collective-permute-done | bytes 524320 | tf_op jit(solution)/shard_map/ppermute | solution.py:435
  35.4 3.6 %forward.1 = (bf16[1024,512]{1,0:T(8,128)(2,1)S(1)}, bf16[512,1024]{1,0:T(8,128)(2,1)S(1)}, bf16[512,1024]{1,0:T(8,128)(2,1)S(1)}, f32[8,64,128]{2,1,0:T(8,128)S(1)}) custom-call(bf16[512,1024]{1,0:T(8,128)(2,1)S(1)} %add_convert_fusion.1.pick, bf16[256,1024]{1,0:T(8,128)(2,1)S(1)} %get-tuple-element.114.own, ...), custom_call_target="tpu_custom_call" | custom-call | flops 2281701376 | bytes 12582912 | tf_op jit(solution)/shard_map/forward/pallas_call | solution.py:113
  38.9 10.5 %all_to_all.25.pred = f32[8,64,128]{2,1,0:T(8,128)S(1)} all-to-all(f32[8,64,128]{2,1,0:T(8,128)S(1)} %get-tuple-element.78), channel_id=1, replica_groups=mesh['xl'=2,'c'=2,'z'=8,'y'=4,'xh'=2] {'xh','xl','c'}, dimensions={0} | all-to-all | bytes 524288 | tf_op jit(solution)/shard_map/all_to_all | solution.py:87
  49.9 8.8 %all_to_all.26 = bf16[8,64,128]{2,1,0:T(8,128)(2,1)S(1)} all-to-all(bf16[8,64,128]{2,1,0:T(8,128)(2,1)S(1)} %get-tuple-element.81), channel_id=1, replica_groups=mesh['xl'=2,'c'=2,'z'=8,'y'=4,'xh'=2] {'xh','xl','c'}, dimensions={0} | all-to-all | bytes 262144 | tf_op jit(solution)/shard_map/all_to_all | solution.py:87
  58.7 1.2 backward.1
  59.9 1.1 collective-permute-start.4
  61.0 3.3 %latent_grads.1 = (f32[256,1024]{1,0:T(8,128)}, bf16[256,1024]{1,0:T(8,128)(2,1)}, bf16[256,1024]{1,0:T(8,128)(2,1)}, bf16[256,1024]{1,0:T(8,128)(2,1)}) custom-call(bf16[512,1024]{1,0:T(8,128)(2,1)S(1)} %get-tuple-element.87.dpre, bf16[1024,1024]{1,0:T(8,128)(2,1)S(1)} %copy-done.2, bf16[1024,512]{1,0:T(8,128)(2,1)S(1)} %add_convert_fusion.pick_t), custom_call_target="tpu_custom_call" | custom-call | flops 2147483648 | bytes 8388608 | tf_op jit(solution)/shard_map/latent_grads/pallas_call | solution.py:234
  64.3 1.8 %pair_sum.1 = bf16[16,288,128]{2,1,0:T(8,128)(2,1)} custom-call(s32[1]{0:T(128)} %bitcast.2.core.half, bf16[512,128]{1,0:T(8,128)(2,1)S(1)} %bitcast.22, bf16[512,1024]{1,0:T(8,128)(2,1)S(1)} %get-tuple-element.87.dpre, bf16[512,1024]{1,0:T(8,128)(2,1)S(1)} %get-tuple-element.83.hid, bf16[1024,512]{1,0:T(8,128)(2,1)S(1)} %get-tuple-element.84.feats_t, ...), custom_call_target="tpu_custom_call" | custom-call | flops 671088640 | bytes 6291456 | tf_op jit(solution)/shard_map/pair_sum/pallas_call | solution.py:261
  66.2 3.8 %all-to-all-start.4 = ((bf16[16,288,128]{2,1,0:T(8,128)(2,1)}), bf16[16,288,128]{2,1,0:T(8,128)(2,1)S(1)}, u32[]{:S(2)}, u32[]{:S(2)}) async-start(bf16[16,288,128]{2,1,0:T(8,128)(2,1)} %pair_sum.1), calls=%async_computation.4 | async-start | bytes 2359296 | tf_op jit(solution)/shard_map/all_to_all | solution.py:87
  70.1 6.9 %collective-permute-start.5 = (bf16[256,1024]{1,0:T(8,128)(2,1)S(1)}, bf16[256,1024]{1,0:T(8,128)(2,1)S(1)}, u32[]{:S(2)}, u32[]{:S(2)}) collective-permute-start(bf16[256,1024]{1,0:T(8,128)(2,1)S(1)} %broadcast_select_fusion.2), channel_id=1, source_target_pairs={{0,56},{1,57},{6,14},{7,15},{8,0},{9,1},{14,22},{15,23},{16,8},{17... | collective-permute-start | bytes 1572872 | tf_op jit(solution)/shard_map/ppermute | solution.py:482
  77.1 11.3 %collective-permute-done.5 = bf16[256,1024]{1,0:T(8,128)(2,1)S(1)} collective-permute-done((bf16[256,1024]{1,0:T(8,128)(2,1)S(1)}, bf16[256,1024]{1,0:T(8,128)(2,1)S(1)}, u32[]{:S(2)}, u32[]{:S(2)}) %collective-permute-start.5) | collective-permute-done | bytes 524320 | tf_op jit(solution)/shard_map/ppermute | solution.py:482
  89.4 1.8 %all-to-all-done.4 = bf16[16,288,128]{2,1,0:T(8,128)(2,1)S(1)} async-done(((bf16[16,288,128]{2,1,0:T(8,128)(2,1)}), bf16[16,288,128]{2,1,0:T(8,128)(2,1)S(1)}, u32[]{:S(2)}, u32[]{:S(2)}) %all-to-all-start.4) | async-done | bytes 1179680 | tf_op jit(solution)/shard_map/all_to_all | solution.py:87
  92.0 3.4 %collective-permute-start.8 = (bf16[256,1024]{1,0:T(8,128)(2,1)}, bf16[256,1024]{1,0:T(8,128)(2,1)}, u32[]{:S(2)}, u32[]{:S(2)}) collective-permute-start(bf16[256,1024]{1,0:T(8,128)(2,1)} %get-tuple-element.98), channel_id=1, source_target_pairs={{0,7},{1,2},{2,1},{3,4},{4,3},{5,6},{6,5},{7,0},{8,15},{9,10},{10,... | collective-permute-start | bytes 1572872 | tf_op jit(solution)/shard_map/ppermute | solution.py:489
  96.1 42.4 %conditional.1 = (bf16[16,288,128]{2,1,0:T(8,128)(2,1)S(1)}) conditional(s32[]{:T(128)} %bitcast.13, bf16[16,288,128]{2,1,0:T(8,128)(2,1)S(1)} %all-to-all-done.4, (s32[]{:T(128)}, s32[]{:T(128)}, s32[]{:T(128)}, bf16[16,288,128]{2,1,0:T(8,128)(2,1)S(1)}) %tuple.22), branch_computations={%region_0.1_spmd, %region_1.2_spmd} | conditional | flops 884746 | bytes 7078007 | solution.py:494
  96.3 23.4 %all_to_all.23.parts = bf16[8,288,128]{2,1,0:T(8,128)(2,1)S(1)} all-to-all(bf16[8,288,128]{2,1,0:T(8,128)(2,1)S(1)} %total.2), channel_id=1, replica_groups=mesh['xl'=2,'c'=2,'z'=8,'y'=4,'xh'=2] {'z'}, dimensions={0} | all-to-all | bytes 1179648 | tf_op jit(solution)/shard_map/cond/branch_1_fun/all_to_all | solution.py:87
  119.8 18.7 %all_to_all.24 = bf16[16,288,128]{2,1,0:T(8,128)(2,1)S(1)} all-to-all(bf16[16,288,128]{2,1,0:T(8,128)(2,1)S(1)} %total.3), channel_id=1, replica_groups=mesh['xl'=2,'c'=2,'z'=8,'y'=4,'xh'=2] {'y','xh','xl'}, dimensions={0} | all-to-all | bytes 2359296 | tf_op jit(solution)/shard_map/cond/branch_1_fun/all_to_all | solution.py:87
  138.5 4.6 %collective-permute-start.9 = (bf16[16,288,128]{2,1,0:T(8,128)(2,1)S(1)}, bf16[16,288,128]{2,1,0:T(8,128)(2,1)S(1)}, u32[]{:S(2)}, u32[]{:S(2)}) collective-permute-start(bf16[16,288,128]{2,1,0:T(8,128)(2,1)S(1)} %get-tuple-element.122.parts), channel_id=1, source_target_pairs={{0,64},{64,0},{1,65},{65,1},{2,66},{66,2},{3,67},{67,3},{4,68},{68... | collective-permute-start | bytes 3538952 | tf_op jit(solution)/shard_map/ppermute | solution.py:496
  143.1 1.5 unpack_first.1
  144.6 2.1 %final_latents.1 = bf16[2,256,1024]{2,1,0:T(8,128)(2,1)} custom-call(s32[1]{0:T(128)} %bitcast.1.side, f32[256,1024]{1,0:T(8,128)S(1)} %copy-done.1, bf16[256,1024]{1,0:T(8,128)(2,1)S(1)} %collective-permute-done.7.same, bf16[256,1024]{1,0:T(8,128)(2,1)S(1)} %collective-permute-done.6.swp, bf16[256,1024]{1,0:T(8,128)(2,1)} %collective-permute-done.8.diag), custom_call_target="tpu_custom_call" | custom-call | bytes 5242880 | tf_op jit(solution)/shard_map/final_latents/pallas_call | solution.py:399
  146.7 2.2 %unpack_second.1 = (f32[1024,1024]{1,0:T(8,128)}, f32[100,1024]{1,0:T(8,128)}, f32[1,1024]{1,0:T(1,128)}, f32[1,100]{1,0:T(1,128)}, f32[1,1]{1,0:T(1,128)}) custom-call(s32[1]{0:T(128)S(6)} %sub.27.half, bf16[16,288,128]{2,1,0:T(8,128)(2,1)S(1)} %collective-permute-done.9.parts, ...), custom_call_target="tpu_custom_call", output_to_operand_aliasing={{0}: (2, {}), {1}: (3, {}), {2}: (4, {})} | custom-call | bytes 4194304 | tf_op jit(solution)/shard_map/unpack_second/pallas_call | solution.py:354
  (54 shorter events, 6.4 us)
Async XLA Ops:
  0.6 16.9 %copy-start = (f32[100,256]{1,0:T(8,128)S(1)}, f32[100,256]{1,0:T(8,128)}, u32[]{:S(2)}) copy-start(f32[100,256]{1,0:T(8,128)} %param.15) | copy-start | bytes 307204
  0.6 12.9 %copy-start.7 = (s32[256,3]{0,1:T(4,128)S(1)}, s32[256,3]{0,1:T(4,128)}, u32[]{:S(2)}) copy-start(s32[256,3]{0,1:T(4,128)} %param.13) | copy-start | bytes 9220
  0.7 16.3 %copy-start.10 = (f32[100]{0:T(128)S(1)}, f32[100]{0:T(128)}, u32[]{:S(2)}) copy-start(f32[100]{0:T(128)} %param.17) | copy-start | bytes 1204
  0.7 16.3 %copy-start.8 = (s32[64]{0:T(128)S(1)}, s32[64]{0:T(128)}, u32[]{:S(2)}) copy-start(s32[64]{0:T(128)} %param.14) | copy-start | bytes 772
  0.7 17.0 %copy-start.9 = (f32[256]{0:T(256)S(1)}, f32[256]{0:T(256)}, u32[]{:S(2)}) copy-start(f32[256]{0:T(256)} %param.16) | copy-start | bytes 3076
  0.7 17.8 %copy-start.11 = (f32[100]{0:T(128)S(1)}, f32[100]{0:T(128)}, u32[]{:S(2)}) copy-start(f32[100]{0:T(128)} %param.21) | copy-start | bytes 1204
  0.7 17.9 %copy-start.6 = (bf16[1024,100]{0,1:T(8,128)(2,1)S(1)}, bf16[1024,100]{0,1:T(8,128)(2,1)}, u32[]{:S(2)}) copy-start(bf16[1024,100]{0,1:T(8,128)(2,1)} %param.20) | copy-start | bytes 614404
  2.1 33.3 %copy-start.3 = (f32[1024]{0:T(1024)S(1)}, f32[1024]{0:T(1024)}, u32[]{:S(2)}) copy-start(f32[1024]{0:T(1024)} %param.19) | copy-start | bytes 12292
  2.1 31.5 %collective-permute-start.3 = (bf16[256,1024]{1,0:T(8,128)(2,1)S(1)}, bf16[256,1024]{1,0:T(8,128)(2,1)S(1)}, u32[]{:S(2)}, u32[]{:S(2)}) collective-permute-start(bf16[256,1024]{1,0:T(8,128)(2,1)S(1)} %get-tuple-element.113), channel_id=1, source_target_pairs={{0,63},{1,2},{2,1},{3,4},{4,3},{5,6},{6,5},{7,8},{8,7},{9,10},{10,... | collective-permute-start | bytes 1572872 | tf_op jit(solution)/shard_map/ppermute | solution.py:434
  13.5 20.1 %collective-permute-start.1 = (bf16[256,1024]{1,0:T(8,128)(2,1)S(1)}, bf16[256,1024]{1,0:T(8,128)(2,1)S(1)}, u32[]{:S(2)}, u32[]{:S(2)}) collective-permute-start(bf16[256,1024]{1,0:T(8,128)(2,1)S(1)} %get-tuple-element.113), channel_id=1, source_target_pairs={{0,1},{1,0},{2,3},{3,2},{4,5},{5,4},{6,7},{7,6},{8,9},{9,8},{10,11... | collective-permute-start | bytes 1572872 | tf_op jit(solution)/shard_map/ppermute | solution.py:433
  13.5 18.6 %collective-permute-start = (s32[256,3]{0,1:T(4,128)S(1)}, s32[256,3]{0,1:T(4,128)S(1)}, u32[]{:S(2)}, u32[]{:S(2)}) collective-permute-start(s32[256,3]{0,1:T(4,128)S(1)} %copy-done.7), channel_id=1, source_target_pairs={{0,1},{1,0},{2,3},{3,2},{4,5},{5,4},{6,7},{7,6},{8,9},{9,8},{10,11... | collective-permute-start | bytes 9224 | tf_op jit(solution)/shard_map/ppermute | solution.py:432
  16.5 18.9 %collective-permute-start.2 = (bf16[256,1024]{1,0:T(8,128)(2,1)S(1)}, bf16[256,1024]{1,0:T(8,128)(2,1)S(1)}, u32[]{:S(2)}, u32[]{:S(2)}) collective-permute-start(bf16[256,1024]{1,0:T(8,128)(2,1)S(1)} %get-tuple-element.114.own), channel_id=1, source_target_pairs={{0,62},{1,3},{2,0},{3,5},{4,2},{5,7},{6,4},{7,9},{8,6},{9,11},{10,... | collective-permute-start | bytes 1572872 | tf_op jit(solution)/shard_map/ppermute | solution.py:435
  49.4 11.6 %copy-start.2 = (bf16[1024,1024]{1,0:T(8,128)(2,1)S(1)}, bf16[1024,1024]{1,0:T(8,128)(2,1)}, u32[]{:S(2)}) copy-start(bf16[1024,1024]{1,0:T(8,128)(2,1)} %w_in.3) | copy-start | bytes 6291460
  59.9 4.5 %collective-permute-start.4 = (bf16[16,288,128]{2,1,0:T(8,128)(2,1)S(1)}, bf16[16,288,128]{2,1,0:T(8,128)(2,1)S(1)}, u32[]{:S(2)}, u32[]{:S(2)}) collective-permute-start(bf16[16,288,128]{2,1,0:T(8,128)(2,1)S(1)} %get-tuple-element.86), channel_id=1, source_target_pairs={{0,64},{64,0},{1,65},{65,1},{2,66},{66,2},{3,67},{67,3},{4,68},{68... | collective-permute-start | bytes 3538952 | tf_op jit(solution)/shard_map/ppermute | solution.py:473
  66.2 3.9 %copy-start.4 = (bf16[256,1024]{1,0:T(8,128)(2,1)S(1)}, bf16[256,1024]{1,0:T(8,128)(2,1)}, u32[]{:S(2)}) copy-start(bf16[256,1024]{1,0:T(8,128)(2,1)} %get-tuple-element.93) | copy-start | bytes 1572868
  66.2 3.9 %copy-start.5 = (bf16[256,1024]{1,0:T(8,128)(2,1)S(1)}, bf16[256,1024]{1,0:T(8,128)(2,1)}, u32[]{:S(2)}) copy-start(bf16[256,1024]{1,0:T(8,128)(2,1)} %get-tuple-element.94) | copy-start | bytes 1572868
  66.2 25.1 %all-to-all-start.4 = ((bf16[16,288,128]{2,1,0:T(8,128)(2,1)}), bf16[16,288,128]{2,1,0:T(8,128)(2,1)S(1)}, u32[]{:S(2)}, u32[]{:S(2)}) async-start(bf16[16,288,128]{2,1,0:T(8,128)(2,1)} %pair_sum.1), calls=%async_computation.4 | async-start | bytes 2359296 | tf_op jit(solution)/shard_map/all_to_all | solution.py:87
  70.1 18.3 %collective-permute-start.5 = (bf16[256,1024]{1,0:T(8,128)(2,1)S(1)}, bf16[256,1024]{1,0:T(8,128)(2,1)S(1)}, u32[]{:S(2)}, u32[]{:S(2)}) collective-permute-start(bf16[256,1024]{1,0:T(8,128)(2,1)S(1)} %broadcast_select_fusion.2), channel_id=1, source_target_pairs={{0,56},{1,57},{6,14},{7,15},{8,0},{9,1},{14,22},{15,23},{16,8},{17... | collective-permute-start | bytes 1572872 | tf_op jit(solution)/shard_map/ppermute | solution.py:482
  91.3 47.3 %collective-permute-start.6 = (bf16[256,1024]{1,0:T(8,128)(2,1)}, bf16[256,1024]{1,0:T(8,128)(2,1)S(1)}, u32[]{:S(2)}, u32[]{:S(2)}) collective-permute-start(bf16[256,1024]{1,0:T(8,128)(2,1)} %get-tuple-element.96), channel_id=1, source_target_pairs={{1,0},{0,1},{3,2},{2,3},{5,4},{4,5},{7,6},{6,7},{9,8},{8,9},{11,10... | collective-permute-start | bytes 1572872 | tf_op jit(solution)/shard_map/ppermute | solution.py:487
  91.9 46.7 %collective-permute-start.7 = (bf16[256,1024]{1,0:T(8,128)(2,1)}, bf16[256,1024]{1,0:T(8,128)(2,1)S(1)}, u32[]{:S(2)}, u32[]{:S(2)}) collective-permute-start(bf16[256,1024]{1,0:T(8,128)(2,1)} %get-tuple-element.97), channel_id=1, source_target_pairs={{0,2},{1,7},{2,4},{3,1},{4,6},{5,3},{6,0},{7,5},{8,10},{9,15},{10,... | collective-permute-start | bytes 1572872 | tf_op jit(solution)/shard_map/ppermute | solution.py:488
  92.0 46.5 %collective-permute-start.8 = (bf16[256,1024]{1,0:T(8,128)(2,1)}, bf16[256,1024]{1,0:T(8,128)(2,1)}, u32[]{:S(2)}, u32[]{:S(2)}) collective-permute-start(bf16[256,1024]{1,0:T(8,128)(2,1)} %get-tuple-element.98), channel_id=1, source_target_pairs={{0,7},{1,2},{2,1},{3,4},{4,3},{5,6},{6,5},{7,0},{8,15},{9,10},{10,... | collective-permute-start | bytes 1572872 | tf_op jit(solution)/shard_map/ppermute | solution.py:489
  96.1 48.5 %copy-start.1 = (f32[256,1024]{1,0:T(8,128)S(1)}, f32[256,1024]{1,0:T(8,128)}, u32[]{:S(2)}) copy-start(f32[256,1024]{1,0:T(8,128)} %get-tuple-element.90.own) | copy-start | bytes 3145732
  138.5 8.2 %collective-permute-start.9 = (bf16[16,288,128]{2,1,0:T(8,128)(2,1)S(1)}, bf16[16,288,128]{2,1,0:T(8,128)(2,1)S(1)}, u32[]{:S(2)}, u32[]{:S(2)}) collective-permute-start(bf16[16,288,128]{2,1,0:T(8,128)(2,1)S(1)} %get-tuple-element.122.parts), channel_id=1, source_target_pairs={{0,64},{64,0},{1,65},{65,1},{2,66},{66,2},{3,67},{67,3},{4,68},{68... | collective-permute-start | bytes 3538952 | tf_op jit(solution)/shard_map/ppermute | solution.py:496
